TPU v7x, 32 devices: a whole 2x2x4 slice. The times are simulated.
32 devices in a mesh: group: 2 (over x), expert: 16 (over z, y, core), dp: 1.
Axes of the slice: x: 2, y: 2, z: 4, core: 2. Of those that a mesh axis runs over, the one named last changes fastest.
Arguments:
- gate_update: bfloat16 [16, 4096, 768], P(None, ('expert', 'dp')), may hold values from -0.09375 to 0.09375
- up_update: bfloat16 [16, 4096, 768], P(None, ('expert', 'dp')), may hold values from -0.09375 to 0.09375
- down_weight: bfloat16 [16, 768, 4096], P('expert', 'dp'), may hold values from -0.21875 to 0.21875
- out_proj: bfloat16 [8192, 4096], P('expert'), may hold values from -0.0625 to 0.0625
- norm_gain: float32 [4096], replicated, may hold values from 0.1 to 1.9
- residual: bfloat16 [2, 2, 64, 4096], P(None, ('group', 'dp'), 'expert'), parts along dimension 1, may hold values from -4 to 4
- queries: bfloat16 [2, 2, 64, 8192], P(None, ('group', 'dp'), 'expert'), parts along dimension 1, may hold values from -150 to 150
- token_keys: bfloat16 [2, 2, 64, 512], P(None, ('group', 'dp'), 'expert'), parts along dimension 1, may hold values from -6 to 6
- token_values: bfloat16 [2, 2, 64, 512], P(None, ('group', 'dp'), 'expert'), parts along dimension 1, may hold values from -6 to 6
- cached_key_rows: bfloat16 [2, 64, 192, 512], P(('group', 'dp'), 'expert'), parts along dimension 0, may hold values from -6 to 6
- cached_value_rows: bfloat16 [2, 64, 192, 512], P(('group', 'dp'), 'expert'), parts along dimension 0, may hold values from -6 to 6
- lengths: int32 [2, 64], P(('group', 'dp'), 'expert'), parts along dimension 0, may hold values from 2 to 192, as said below
- expert_ids: int32 [2, 2, 64, 8], P(None, ('group', 'dp'), 'expert'), parts along dimension 1, may hold values from 0 to 15, all different within a row; in each aligned block of 4 rows (0 to 3, 4 to 7, ..., all dimensions but the last counted through in order) at most 3 rows name the same one
- gate_probs: float32 [2, 2, 64, 8], P(None, ('group', 'dp'), 'expert'), parts along dimension 1, may hold values from 0.02 to 0.5
Outputs:
- stream: bfloat16 [2, 2, 64, 4096], P(None, ('group', 'dp'), 'expert'), parts along dimension 1
- mixed: bfloat16 [2, 2, 64, 4096], P(None, ('group', 'dp'), 'expert'), parts along dimension 1
There are 2 independent parts, one for each index of `group`. A program takes and returns all parts, laid end to end along the dimension named above; an argument that names none is the same for every part. Nothing has to cross between parts.
Inputs may be any that keep to these rules, and one draw needn't show every extreme that they name: `lengths`: cache slots at and beyond a row's length are not used. `expert_ids`: each row names 8 different experts; within the rows of one device in one step no expert is named by more than 3 rows.
All inputs are finite; a program needn't handle non-finite values.
Results may differ from a plain program's by a relative error of at most 0.04.
Values may be sent and summed in bfloat16 or wider, within the bound.
A program may use at most 128 MiB of HBM per device.

v0:
```python
import math

import jax
import jax.numpy as jnp
from jax import lax
from jax.sharding import PartitionSpec as P

QUERY_HEADS = 64
KEY_VALUE_HEADS = 4
HEAD_SIZE = 128
CACHE_SLOTS = 192


def run_experts(slots, gate_local, up_local, down_local):
    gate_part = jnp.dot(slots, gate_local, preferred_element_type=jnp.float32)
    up_part = jnp.dot(slots, up_local, preferred_element_type=jnp.float32)
    hidden = (jax.nn.silu(gate_part) * up_part).astype(jnp.bfloat16)
    return jnp.dot(hidden, down_local, preferred_element_type=jnp.float32)


def shards(
    gate_update,
    up_update,
    down_weight,
    out_proj,
    norm_gain,
    residual,
    queries,
    token_keys,
    token_values,
    cached_key_rows,
    cached_value_rows,
    lengths,
    expert_ids,
    gate_probs,
):
    expert_count = gate_update.shape[0]
    pair_count = lax.axis_size("dp")
    step_count = residual.shape[0]
    count_of_rows = residual.shape[2]
    model_width = residual.shape[3]
    top_count = expert_ids.shape[3]
    capacity = min(count_of_rows, max(2, 3 * count_of_rows * top_count // (2 * expert_count)))
    head_groups = QUERY_HEADS // KEY_VALUE_HEADS
    score_scale = 1.0 / math.sqrt(HEAD_SIZE)
    gate_moved, up_moved = (
        lax.all_to_all(
            lax.all_to_all(gate_update, "dp", split_axis=2, concat_axis=1, tiled=True),
            "expert",
            split_axis=0,
            concat_axis=1,
            tiled=True,
        ),
        lax.all_to_all(
            lax.all_to_all(up_update, "dp", split_axis=2, concat_axis=1, tiled=True),
            "expert",
            split_axis=0,
            concat_axis=1,
            tiled=True,
        ),
    )
    gate_local = gate_moved[0]
    up_local = up_moved[0]
    down_local = down_weight[0]
    key_cache_table = cached_key_rows[0].reshape(
        count_of_rows, CACHE_SLOTS, KEY_VALUE_HEADS, HEAD_SIZE
    )
    value_cache_table = cached_value_rows[0].reshape(
        count_of_rows, CACHE_SLOTS, KEY_VALUE_HEADS, HEAD_SIZE
    )
    cache_valid = jnp.arange(CACHE_SLOTS, dtype=jnp.int32)[None, :] < lengths[0][:, None]
    expert_range = jnp.arange(expert_count, dtype=jnp.int32)
    slot_range = jnp.arange(capacity, dtype=jnp.int32)
    gain_row = norm_gain[None, :]
    streams = []
    mixes = []
    for decode_step_index in range(step_count):
        query_matrix = queries[decode_step_index, 0].reshape(
            count_of_rows, KEY_VALUE_HEADS, head_groups, HEAD_SIZE
        )
        incoming_keys = token_keys[: decode_step_index + 1, 0].reshape(
            decode_step_index + 1, count_of_rows, KEY_VALUE_HEADS, HEAD_SIZE
        )
        incoming_values = token_values[: decode_step_index + 1, 0].reshape(
            decode_step_index + 1, count_of_rows, KEY_VALUE_HEADS, HEAD_SIZE
        )
        cache_scores = (
            jnp.einsum(
                "rhgd,rlhd->rhgl", query_matrix, key_cache_table, preferred_element_type=jnp.float32
            )
            * score_scale
        )
        fresh_scores = (
            jnp.einsum(
                "rhgd,lrhd->rhgl", query_matrix, incoming_keys, preferred_element_type=jnp.float32
            )
            * score_scale
        )
        cache_scores = jnp.where(cache_valid[:, None, None, :], cache_scores, -1e30)
        peak_score = jnp.maximum(
            jnp.max(cache_scores, axis=-1, keepdims=True),
            jnp.max(fresh_scores, axis=-1, keepdims=True),
        )
        cache_exp = jnp.exp(cache_scores - peak_score)
        fresh_exp = jnp.exp(fresh_scores - peak_score)
        weight_total = jnp.sum(cache_exp, axis=-1, keepdims=True) + jnp.sum(
            fresh_exp, axis=-1, keepdims=True
        )
        cache_weights = (cache_exp / weight_total).astype(jnp.bfloat16)
        fresh_weights = (fresh_exp / weight_total).astype(jnp.bfloat16)
        attended = jnp.einsum(
            "rhgl,rlhd->rhgd", cache_weights, value_cache_table, preferred_element_type=jnp.float32
        )
        attended = attended + jnp.einsum(
            "rhgl,lrhd->rhgd", fresh_weights, incoming_values, preferred_element_type=jnp.float32
        )
        attended = attended.astype(jnp.bfloat16).reshape(count_of_rows, QUERY_HEADS * HEAD_SIZE)
        spread = lax.all_to_all(attended, "expert", split_axis=1, concat_axis=0, tiled=True)
        projected = lax.psum_scatter(
            jnp.dot(spread, out_proj, preferred_element_type=jnp.float32).astype(jnp.bfloat16),
            "expert",
            scatter_dimension=0,
            tiled=True,
        ).astype(jnp.float32)
        stream_now = (residual[decode_step_index, 0].astype(jnp.float32) + projected).astype(
            jnp.bfloat16
        )
        wide = stream_now.astype(jnp.float32)
        mean_square = jnp.mean(wide * wide, axis=-1, keepdims=True)
        normed = (wide * lax.rsqrt(mean_square + 1e-06) * gain_row).astype(jnp.bfloat16)
        chosen_ids = expert_ids[decode_step_index, 0]
        matches = chosen_ids[:, :, None] == expert_range[None, None, :]
        present = jnp.sum(matches.astype(jnp.int32), axis=1)
        slot_rank = jnp.cumsum(present, axis=0) - present
        slot_select = (
            present[:, :, None]
            * (slot_rank[:, :, None] == slot_range[None, None, :]).astype(jnp.int32)
        ).astype(jnp.float32)
        outgoing = jnp.einsum(
            "rec,rd->ecd",
            slot_select.astype(jnp.bfloat16),
            normed,
            preferred_element_type=jnp.float32,
        ).astype(jnp.bfloat16)
        pick_weight = jnp.sum(
            matches.astype(jnp.float32) * gate_probs[decode_step_index, 0][:, :, None], axis=1
        )
        coefficient = slot_select * pick_weight[:, :, None]
        copies = jnp.broadcast_to(
            outgoing[:, None], (expert_count, pair_count, capacity, model_width)
        )
        copies = copies.reshape(expert_count * pair_count, capacity, model_width)
        incoming = lax.all_to_all(copies, ("expert", "dp"), split_axis=0, concat_axis=0, tiled=True)
        partial_out = run_experts(
            incoming.reshape(-1, model_width), gate_local, up_local, down_local
        )
        partial_out = partial_out.reshape(expert_count * pair_count, capacity, model_width)
        returned = lax.all_to_all(
            partial_out.astype(jnp.bfloat16),
            ("expert", "dp"),
            split_axis=0,
            concat_axis=0,
            tiled=True,
        ).astype(partial_out.dtype)
        results = jnp.sum(
            returned.reshape(expert_count, pair_count, capacity, model_width), axis=1
        ).astype(jnp.bfloat16)
        mixed_now = jnp.einsum(
            "rec,ecd->rd", coefficient, results.astype(jnp.float32), precision=lax.Precision.HIGHEST
        ).astype(jnp.bfloat16)
        streams.append(stream_now)
        mixes.append(mixed_now)
    stream = jnp.stack(streams)[:, None]
    mixed = jnp.stack(mixes)[:, None]
    return (stream, mixed)


def solution(mesh):
    in_specs = (
        P(None, ("expert", "dp"), None),
        P(None, ("expert", "dp"), None),
        P("expert", "dp", None),
        P("expert", None),
        P(),
        P(None, ("group", "dp"), "expert", None),
        P(None, ("group", "dp"), "expert", None),
        P(None, ("group", "dp"), "expert", None),
        P(None, ("group", "dp"), "expert", None),
        P(("group", "dp"), "expert", None, None),
        P(("group", "dp"), "expert", None, None),
        P(("group", "dp"), "expert"),
        P(None, ("group", "dp"), "expert", None),
        P(None, ("group", "dp"), "expert", None),
    )
    out_specs = (P(None, ("group", "dp"), "expert", None), P(None, ("group", "dp"), "expert", None))
    return jax.shard_map(shards, mesh=mesh, in_specs=in_specs, out_specs=out_specs, check_vma=False)
```

profile of v0, /device:TPU:0, one launch (start us, length us, event | category | flops | bytes accessed | tf_op | source)
XLA Modules:
  0.0 518.7 jit_solution(13006092484491438347)
XLA Ops:
  7.2 0.0 slice-start
  7.2 0.9 slice_bitcast_fusion.1
  8.1 1.8 reshape_squeeze.21
  9.9 0.7 iota_compare_fusion.6
  10.6 0.7 reshape_squeeze.24
  11.3 0.2 fusion.85
  11.5 0.6 fusion.84
  12.1 0.2 fusion.27
  12.4 0.7 reshape_squeeze.25
  13.1 1.7 reshape_squeeze.22
  14.9 0.2 fusion.51
  15.1 0.4 fusion.19
  15.5 0.1 all_to_all.58
  15.5 0.7 copy.61
  16.2 7.4 %all-to-all-start.1 = ((bf16[4,16,512]{2,0,1:T(4,128)(2,1)}), bf16[4,16,512]{2,0,1:T(4,128)(2,1)S(1)}, u32[]{:S(2)}, u32[]{:S(2)}) async-start(bf16[4,16,512]{2,0,1:T(4,128)(2,1)} %copy.61), calls=%async_computation.1 | async-start | bytes 131072 | tf_op jit(solution)/shard_map/all_to_all | solution.py:118
  23.7 0.6 fusion.86
  24.3 0.1 fusion.87
  24.4 0.2 fusion.26
  24.7 0.0 copy-start.5
  24.7 0.4 fusion.18
  25.1 0.1 all_to_all.54
  25.2 0.7 copy.56
  25.9 4.6 all-to-all-done.1
  30.5 3.5 all-to-all-start
  34.0 0.0 all-reduce.5.cloned.1.call-start
  34.1 6.8 %all-to-all-done = bf16[4,16,512]{2,0,1:T(4,128)(2,1)S(1)} async-done(((bf16[4,16,512]{2,0,1:T(4,128)(2,1)}), bf16[4,16,512]{2,0,1:T(4,128)(2,1)S(1)}, u32[]{:S(2)}, u32[]{:S(2)}) %all-to-all-start) | async-done | bytes 65568 | tf_op jit(solution)/shard_map/all_to_all | solution.py:118
  40.9 3.9 convolution_convert_fusion
  44.8 3.8 convolution_convert_fusion.1
  48.6 0.0 all-reduce.5.cloned.1.call-update
  48.6 0.1 convert_reduce_fusion.1
  48.8 0.6 dynamic-slice
  50.0 89.3 %all-reduce.5.cloned.1.call-done = (bf16[64,4096]{1,0:T(8,128)(2,1)}, bf16[64,4096]{1,0:T(8,128)(2,1)}) async-done(((bf16[64,4096]{1,0:T(8,128)(2,1)}, bf16[64,4096]{1,0:T(8,128)(2,1)}), (bf16[64,4096]{1,0:T(8,128)(2,1)}, bf16[64,4096]{1,0:T(8,128)(2,1)})) %all-reduce.5.cloned.1.call-update) | async-done | bytes 1048592
  139.3 1.1 fusion.34
  140.4 0.3 convolution_convert_fusion.3
  140.7 1.1 copy.62
  141.9 4.0 all-to-all-start.2
  145.9 0.1 convert_reduce_fusion
  146.0 0.3 convolution_convert_fusion.2
  146.4 0.3 copy.66
  146.7 13.6 %all-to-all-done.2 = bf16[16,3,4096]{2,1,0:T(4,128)(2,1)S(1)} async-done(((bf16[16,3,4096]{2,1,0:T(4,128)(2,1)}), bf16[16,3,4096]{2,1,0:T(4,128)(2,1)S(1)}, u32[]{:S(2)}, u32[]{:S(2)}) %all-to-all-start.2) | async-done | bytes 393248 | tf_op jit(solution)/shard_map/all_to_all | solution.py:153
  160.4 18.4 %all_to_all.76 = bf16[16,3,4096]{2,1,0:T(4,128)(2,1)S(1)} all-to-all(bf16[16,3,4096]{2,1,0:T(4,128)(2,1)S(1)} %copy.66), channel_id=1, replica_groups=mesh['group'=2,'expert'=16,'dp'=1] {'expert','dp'}, dimensions={0} | all-to-all | bytes 786432 | tf_op jit(solution)/shard_map/all_to_all | solution.py:153
  178.7 141.8 %all_to_all.77 = bf16[16,256,768]{2,1,0:T(8,128)(2,1)} all-to-all(bf16[16,256,768]{2,1,0:T(8,128)(2,1)} %param.14), channel_id=1, replica_groups=mesh['group'=2,'expert'=16,'dp'=1] {'expert'}, dimensions={0} | all-to-all | bytes 12582912 | tf_op jit(solution)/shard_map/all_to_all | solution.py:47
  320.5 5.1 all-to-all-start.4
  325.6 0.3 reshape.153
  326.0 0.3 reshape.154
  326.3 3.9 fusion.88
  330.2 109.6 %all-to-all-done.4 = bf16[16,256,768]{2,1,0:T(8,128)(2,1)} async-done(((bf16[16,256,768]{2,1,0:T(8,128)(2,1)}), bf16[16,256,768]{2,1,0:T(8,128)(2,1)}, u32[]{:S(2)}, u32[]{:S(2)}) %all-to-all-start.4) | async-done | bytes 6291488 | tf_op jit(solution)/shard_map/all_to_all | solution.py:54
  439.8 3.9 fusion.16
  443.8 4.0 fusion.4
  447.8 1.2 copy.64
  449.0 28.1 %all-to-all-start.5 = ((bf16[16,3,4096]{2,1,0:T(4,128)(2,1)}), bf16[16,3,4096]{2,1,0:T(4,128)(2,1)S(1)}, u32[]{:S(2)}, u32[]{:S(2)}) async-start(bf16[16,3,4096]{2,1,0:T(4,128)(2,1)} %copy.64), calls=%async_computation.5 | async-start | bytes 1048576 | tf_op jit(solution)/shard_map/all_to_all | solution.py:158
  477.1 3.9 fusion.89
  481.0 0.0 copy-start.4
  481.0 4.0 fusion.17
  485.0 4.0 fusion.7
  489.0 1.1 copy.68
  490.1 1.4 all-to-all-done.5
  491.5 4.6 all-to-all-start.7
  496.2 0.1 select_reduce_fusion
  496.3 0.7 maximum_bitcast_fusion
  497.0 0.5 fusion.13
  497.5 13.1 %all-to-all-done.7 = bf16[16,3,4096]{2,1,0:T(4,128)(2,1)S(1)} async-done(((bf16[16,3,4096]{2,1,0:T(4,128)(2,1)}), bf16[16,3,4096]{2,1,0:T(4,128)(2,1)S(1)}, u32[]{:S(2)}, u32[]{:S(2)}) %all-to-all-start.7) | async-done | bytes 393248 | tf_op jit(solution)/shard_map/all_to_all | solution.py:158
  510.6 0.5 fusion.12
  511.2 0.7 maximum_bitcast_fusion.1
  (33 shorter events, 0.4 us)
Async XLA Ops:
  7.2 17.1 %slice-start = ((bf16[2,1,4,512]{3,2,1,0:T(4,128)(2,1)}), bf16[1,1,4,512]{3,2,1,0:T(4,128)(2,1)S(1)}, s32[]{:S(2)}) async-start(bf16[2,1,4,512]{3,2,1,0:T(4,128)(2,1)} %param.21), calls=%async_computation.9 | async-start | bytes 8192 | tf_op jit(solution)/shard_map/slice | solution.py:81
  7.2 16.4 %copy-start.2 = (bf16[2,1,4,512]{3,2,1,0:T(4,128)(2,1)S(1)}, bf16[2,1,4,512]{3,2,1,0:T(4,128)(2,1)}, u32[]{:S(2)}) copy-start(bf16[2,1,4,512]{3,2,1,0:T(4,128)(2,1)} %param.22) | copy-start | bytes 24580
  16.2 14.3 %all-to-all-start.1 = ((bf16[4,16,512]{2,0,1:T(4,128)(2,1)}), bf16[4,16,512]{2,0,1:T(4,128)(2,1)S(1)}, u32[]{:S(2)}, u32[]{:S(2)}) async-start(bf16[4,16,512]{2,0,1:T(4,128)(2,1)} %copy.61), calls=%async_computation.1 | async-start | bytes 131072 | tf_op jit(solution)/shard_map/all_to_all | solution.py:118
  24.7 23.9 %copy-start.3 = (s32[2,1,4,8]{3,2,1,0:T(4,128)S(1)}, s32[2,1,4,8]{3,2,1,0:T(4,128)}, u32[]{:S(2)}) copy-start(s32[2,1,4,8]{3,2,1,0:T(4,128)} %param.26) | copy-start | bytes 772
  24.7 24.1 %copy-start.5 = (u32[32]{0:T(128)S(1)}, u32[32]{0:T(128)}, u32[]{:S(2)}) copy-start(u32[32]{0:T(128)} %constant.42) | copy-start | bytes 388
  24.7 114.6 %copy-start = (bf16[2,1,4,4096]{3,2,1,0:T(4,128)(2,1)S(1)}, bf16[2,1,4,4096]{3,2,1,0:T(4,128)(2,1)}, u32[]{:S(2)}) copy-start(bf16[2,1,4,4096]{3,2,1,0:T(4,128)(2,1)} %param.19) | copy-start | bytes 196612
  25.1 115.3 %copy-start.1 = (f32[4096]{0:T(1024)S(1)}, f32[4096]{0:T(1024)}, u32[]{:S(2)}) copy-start(f32[4096]{0:T(1024)} %param.18) | copy-start | bytes 49156
  30.5 10.4 %all-to-all-start = ((bf16[4,16,512]{2,0,1:T(4,128)(2,1)}), bf16[4,16,512]{2,0,1:T(4,128)(2,1)S(1)}, u32[]{:S(2)}, u32[]{:S(2)}) async-start(bf16[4,16,512]{2,0,1:T(4,128)(2,1)} %copy.56), calls=%async_computation | async-start | bytes 131072 | tf_op jit(solution)/shard_map/all_to_all | solution.py:118
  34.0 105.3 %all-reduce.5.cloned.1.call-start = ((), (), s32[]{:S(2)}) async-start(), calls=%async_computation.8 | async-start | bytes 2097152
  141.9 18.5 %all-to-all-start.2 = ((bf16[16,3,4096]{2,1,0:T(4,128)(2,1)}), bf16[16,3,4096]{2,1,0:T(4,128)(2,1)S(1)}, u32[]{:S(2)}, u32[]{:S(2)}) async-start(bf16[16,3,4096]{2,1,0:T(4,128)(2,1)} %copy.62), calls=%async_computation.2 | async-start | bytes 1048576 | tf_op jit(solution)/shard_map/all_to_all | solution.py:153
  320.5 119.3 %all-to-all-start.4 = ((bf16[16,256,768]{2,1,0:T(8,128)(2,1)}), bf16[16,256,768]{2,1,0:T(8,128)(2,1)}, u32[]{:S(2)}, u32[]{:S(2)}) async-start(bf16[16,256,768]{2,1,0:T(8,128)(2,1)} %param.15), calls=%async_computation.4 | async-start | bytes 12582912 | tf_op jit(solution)/shard_map/all_to_all | solution.py:54
  449.0 42.5 %all-to-all-start.5 = ((bf16[16,3,4096]{2,1,0:T(4,128)(2,1)}), bf16[16,3,4096]{2,1,0:T(4,128)(2,1)S(1)}, u32[]{:S(2)}, u32[]{:S(2)}) async-start(bf16[16,3,4096]{2,1,0:T(4,128)(2,1)} %copy.64), calls=%async_computation.5 | async-start | bytes 1048576 | tf_op jit(solution)/shard_map/all_to_all | solution.py:158
  481.0 15.2 %copy-start.4 = (f32[2,1,4,8]{3,2,1,0:T(4,128)S(1)}, f32[2,1,4,8]{3,2,1,0:T(4,128)}, u32[]{:S(2)}) copy-start(f32[2,1,4,8]{3,2,1,0:T(4,128)} %param.27) | copy-start | bytes 772
  491.5 19.1 %all-to-all-start.7 = ((bf16[16,3,4096]{2,1,0:T(4,128)(2,1)}), bf16[16,3,4096]{2,1,0:T(4,128)(2,1)S(1)}, u32[]{:S(2)}, u32[]{:S(2)}) async-start(bf16[16,3,4096]{2,1,0:T(4,128)(2,1)} %copy.68), calls=%async_computation.7 | async-start | bytes 1048576 | tf_op jit(solution)/shard_map/all_to_all | solution.py:158
Sparse Core Ops, SparseCore 0:
  48.7 90.5 all-reduce.4
where the time goes:
time: 520 us; the launch traced here: 519 us
  waiting for transfers between devices  239 us (46%)
  blocking collectives  160 us (31%)
  starting transfers between devices  52.7 us (10%)
  matrix products  35.6 us (7%)
  between operations  15 us (3%)
  local copies, waits for them, and re-layouts  12.6 us (2%)
    all_to_all x1, blocking collectives, shards(): lax.all_to_all(lax.all_to_all(gate_update, 'dp', split_axis=2, concat_axi...  142 us
    all_to_all x1, waiting for transfers between devices, shards(): lax.all_to_all(lax.all_to_all(up_update, 'dp', split_axis=2, concat_axis=...  110 us
    unnamed x2, waiting for transfers between devices  89.3 us
    all_to_all x2, starting transfers between devices, shards(): lax.all_to_all(partial_out.astype(jnp.bfloat16), ('expert', 'dp'), split_...  32.7 us
    all_to_all x1, blocking collectives, shards(): lax.all_to_all(copies, ('expert', 'dp'), split_axis=0, concat_axis=0, til...  18.4 us
    all_to_all x2, waiting for transfers between devices, shards(): lax.all_to_all(partial_out.astype(jnp.bfloat16), ('expert', 'dp'), split_...  14.5 us
    all_to_all x1, waiting for transfers between devices, shards(): lax.all_to_all(copies, ('expert', 'dp'), split_axis=0, concat_axis=0, til...  13.6 us
    all_to_all x2, waiting for transfers between devices, shards(): lax.all_to_all(attended, 'expert', split_axis=1, concat_axis=0, tiled=True)  11.4 us
  transfers between devices with their start and end apart: 7, of which 7 were waited for; matrix products, arithmetic and copies ran while one was open for 4% of the time, Pallas kernels for 0%

commit v1 on v0

v1 whole, which is shorter than its diff:
```python
import math

import jax
import jax.numpy as jnp
from jax import lax
from jax.sharding import PartitionSpec as P

QUERY_HEADS = 64
KEY_VALUE_HEADS = 4
HEAD_SIZE = 128
F32 = jnp.float32
BF16 = jnp.bfloat16


def scatter_sum(x, axis_name, order):
    count = x.shape[0]
    bits = count.bit_length() - 1
    if bits == 0:
        return x[0]
    me = lax.axis_index(axis_name)
    x = x.reshape((2,) * bits + x.shape[1:])
    left = list(range(bits - 1, -1, -1))
    for bit in order(bits):
        at = left.index(bit)
        left.pop(at)
        mine = (me >> bit) & 1
        keep = lax.dynamic_index_in_dim(x, mine, at, keepdims=False)
        send = lax.dynamic_index_in_dim(x, 1 - mine, at, keepdims=False)
        got = lax.ppermute(send, axis_name, [(i, i ^ (1 << bit)) for i in range(count)])
        x = (keep.astype(F32) + got.astype(F32)).astype(BF16)
    return x


def near_first(bits):
    return list(range(bits))


def far_first(bits):
    return [0] + list(range(2, bits)) + [1] if bits > 2 else list(range(bits))


def scatter_both(x, order):
    if x.shape[1] > 1:
        x = scatter_sum(jnp.moveaxis(x, 1, 0), "dp", near_first)
    else:
        x = x[:, 0]
    return scatter_sum(x, "expert", order)


def attend(queries, token_keys, token_values, key_rows, value_rows, lengths):
    steps, rows = queries.shape[0], queries.shape[2]
    slots = key_rows.shape[2]
    per = QUERY_HEADS // KEY_VALUE_HEADS
    q = queries[:, 0].reshape(steps, rows, KEY_VALUE_HEADS, per, HEAD_SIZE)
    kc = key_rows[0].reshape(rows, slots, KEY_VALUE_HEADS, HEAD_SIZE)
    vc = value_rows[0].reshape(rows, slots, KEY_VALUE_HEADS, HEAD_SIZE)
    kt = token_keys[:, 0].reshape(steps, rows, KEY_VALUE_HEADS, HEAD_SIZE)
    vt = token_values[:, 0].reshape(steps, rows, KEY_VALUE_HEADS, HEAD_SIZE)
    scale = 1.0 / math.sqrt(HEAD_SIZE)
    sc = jnp.einsum("srhgd,rlhd->rhsgl", q, kc, preferred_element_type=F32) * scale
    sf = jnp.einsum("srhgd,lrhd->rhsgl", q, kt, preferred_element_type=F32) * scale
    valid = jnp.arange(slots, dtype=jnp.int32)[None, :] < lengths[0][:, None]
    causal = jnp.arange(steps)[None, :] <= jnp.arange(steps)[:, None]
    sc = jnp.where(valid[:, None, None, None, :], sc, -1e30)
    sf = jnp.where(causal[None, None, :, None, :], sf, -1e30)
    peak = jnp.maximum(jnp.max(sc, -1, keepdims=True), jnp.max(sf, -1, keepdims=True))
    ec, ef = jnp.exp(sc - peak), jnp.exp(sf - peak)
    total = jnp.sum(ec, -1, keepdims=True) + jnp.sum(ef, -1, keepdims=True)
    wc, wf = (ec / total).astype(BF16), (ef / total).astype(BF16)
    out = jnp.einsum("rhsgl,rlhd->srhgd", wc, vc, preferred_element_type=F32)
    out = out + jnp.einsum("rhsgl,lrhd->srhgd", wf, vt, preferred_element_type=F32)
    return out.astype(BF16).reshape(steps * rows, QUERY_HEADS * HEAD_SIZE)


def shards(
    gate_update,
    up_update,
    down_weight,
    out_proj,
    norm_gain,
    residual,
    queries,
    token_keys,
    token_values,
    cached_key_rows,
    cached_value_rows,
    lengths,
    expert_ids,
    gate_probs,
):
    experts, depth, units = gate_update.shape
    ring = lax.axis_size("expert")
    pair = lax.axis_size("dp")
    steps, _, rows, width = residual.shape
    top = expert_ids.shape[3]
    own = steps * rows
    me, half = lax.axis_index("expert"), lax.axis_index("dp")

    ids = expert_ids.reshape(own, top)
    probs = gate_probs.reshape(own, top)
    match = ids[:, :, None] == jnp.arange(experts, dtype=jnp.int32)[None, None, :]
    coefs = jnp.sum(jnp.where(match, probs[:, :, None], 0.0), axis=1)
    coefs = lax.all_gather(coefs.T, ("expert", "dp"), axis=0)
    coefs = lax.dynamic_index_in_dim(coefs, me, 1, keepdims=False)
    coefs = coefs.reshape(ring, pair, own).swapaxes(0, 1).reshape(-1)

    attended = attend(queries, token_keys, token_values, cached_key_rows, cached_value_rows, lengths)
    spread = lax.all_to_all(attended, "expert", split_axis=1, concat_axis=0, tiled=True)
    partial = jnp.dot(spread, out_proj, preferred_element_type=F32)
    place = (jnp.arange(ring) == me).astype(F32)
    partial = partial.reshape(ring, own, width) + place[:, None, None] * residual.reshape(1, own, width).astype(F32)
    partial = partial.astype(BF16).reshape(ring * own, ring, width // ring).swapaxes(0, 1)
    columns = scatter_sum(partial, "expert", near_first)
    back = lax.all_to_all(columns, "expert", split_axis=0, concat_axis=1, tiled=True)
    stream = back.reshape(residual.shape)
    if pair > 1:
        columns = lax.all_to_all(columns, "dp", split_axis=1, concat_axis=0, tiled=True)

    wide = columns.astype(F32)
    square = lax.psum(jnp.sum(wide * wide, axis=1), ("expert", "dp"))
    scale = lax.rsqrt(square / width + 1e-6)[:, None]
    gain = lax.dynamic_slice_in_dim(norm_gain, (me * pair + half) * depth, depth)
    scaled = (wide * gain[None, :]).astype(BF16)
    all_rows = scaled.shape[0]

    def project(chosen, weight, order):
        sums = jnp.einsum("rd,edf->erf", chosen, weight, preferred_element_type=F32).astype(BF16)
        sums = sums.reshape(experts, chosen.shape[0], pair, units // pair).swapaxes(1, 2)
        return scatter_both(sums, order)

    def both(chosen):
        return project(chosen, gate_update, near_first), project(chosen, up_update, far_first)

    if all_rows <= 128:
        gate, up = both(scaled)
    else:
        gate, up = lax.map(both, scaled.reshape(-1, 128, depth))
    gate = gate.reshape(all_rows, -1).astype(F32) * scale
    up = up.reshape(all_rows, -1).astype(F32) * scale
    hidden = (jax.nn.silu(gate) * up * coefs[:, None]).astype(BF16)
    out = jnp.dot(hidden, down_weight[0], preferred_element_type=F32).astype(BF16)
    out = out.reshape(pair, ring, own, width).swapaxes(0, 1)
    mixed = scatter_both(out, near_first).reshape(residual.shape)
    return (stream, mixed)


def solution(mesh):
    in_specs = (
        P(None, ("expert", "dp"), None),
        P(None, ("expert", "dp"), None),
        P("expert", "dp", None),
        P("expert", None),
        P(),
        P(None, ("group", "dp"), "expert", None),
        P(None, ("group", "dp"), "expert", None),
        P(None, ("group", "dp"), "expert", None),
        P(None, ("group", "dp"), "expert", None),
        P(("group", "dp"), "expert", None, None),
        P(("group", "dp"), "expert", None, None),
        P(("group", "dp"), "expert"),
        P(None, ("group", "dp"), "expert", None),
        P(None, ("group", "dp"), "expert", None),
    )
    out_specs = (P(None, ("group", "dp"), "expert", None), P(None, ("group", "dp"), "expert", None))
    return jax.shard_map(shards, mesh=mesh, in_specs=in_specs, out_specs=out_specs, check_vma=False)
```

time: 520 us -> 174 us (0.33)
  waiting for transfers between devices: 239 us -> 69.8 us
  blocking collectives: 160 us -> 58.9 us
  starting transfers between devices: 52.7 us -> 18.7 us
  matrix products: 35.6 us -> 14.5 us
  between operations: 15 us -> 1.26 us
    all_to_all x2 -> x0, blocking collectives: 160 us -> none  [the longest x1 142 us: shards(): lax.all_to_all(lax.all_to_all(gate_update, 'dp', split_axis=2, concat_axi...]
    all_to_all x4 -> x1, waiting for transfers between devices: 138 us -> 4.39 us  [shards(): lax.all_to_all(columns, 'expert', split_axis=0, concat_axis=1, tiled=True)]
    unnamed x2 -> x0, waiting for transfers between devices: 89.3 us -> none
    ppermute x0 -> x16, waiting for transfers between devices: none -> 57.5 us  [scatter_sum(): lax.ppermute(send, axis_name, [(i, i ^ 1 << bit) for i in range(count)])]
    all_to_all x4 -> x1, starting transfers between devices: 41.8 us -> 4.78 us  [shards(): lax.all_to_all(columns, 'expert', split_axis=0, concat_axis=1, tiled=True)]
    psum x0 -> x1, blocking collectives: none -> 29.9 us  [shards(): square = lax.psum(jnp.sum(wide * wide, axis=1), ('expert', 'dp'))]
    all_gather x0 -> x1, blocking collectives: none -> 29 us  [shards(): coefs = lax.all_gather(coefs.T, ('expert', 'dp'), axis=0)]
    dot_general x19 -> x8, matrix products: 35.6 us -> 14.5 us  [the longest x2 5.81 us: project(): jnp.einsum('rd,edf->erf', chosen, weight, preferred_element_type=F32)]
  transfers between devices with their start and end apart: 7 -> 18, of which waited for: 7 -> 15; matrix products, arithmetic and copies ran while one was open for 4% -> 3% of each run, Pallas kernels for 0% -> 0%
where the time goes in v1:
time: 174 us
  waiting for transfers between devices  69.8 us (40%)
  blocking collectives  58.9 us (34%)
  starting transfers between devices  18.7 us (11%)
  matrix products  14.5 us (8%)
  local copies, waits for them, and re-layouts  7.45 us (4%)
  other arithmetic  3.13 us (2%)
    ppermute x16, waiting for transfers between devices, scatter_sum(): lax.ppermute(send, axis_name, [(i, i ^ 1 << bit) for i in range(count)])  57.5 us
    psum x1, blocking collectives, shards(): square = lax.psum(jnp.sum(wide * wide, axis=1), ('expert', 'dp'))  29.9 us
    all_gather x1, blocking collectives, shards(): coefs = lax.all_gather(coefs.T, ('expert', 'dp'), axis=0)  29 us
    all_to_all x1, waiting for transfers between devices, shards(): lax.all_to_all(attended, 'expert', split_axis=1, concat_axis=0, tiled=True)  7.88 us
    all_to_all x1, starting transfers between devices, shards(): lax.all_to_all(attended, 'expert', split_axis=1, concat_axis=0, tiled=True)  7.39 us
    ppermute x16, starting transfers between devices, scatter_sum(): lax.ppermute(send, axis_name, [(i, i ^ 1 << bit) for i in range(count)])  6.51 us
    dot_general x2, matrix products, project(): jnp.einsum('rd,edf->erf', chosen, weight, preferred_element_type=F32)  5.81 us
    all_to_all x1, starting transfers between devices, shards(): lax.all_to_all(columns, 'expert', split_axis=0, concat_axis=1, tiled=True)  4.78 us
  transfers between devices with their start and end apart: 18, of which 15 were waited for; matrix products, arithmetic and copies ran while one was open for 3% of the time, Pallas kernels for 0%

profile of v1, /device:TPU:0, one launch (start us, length us, event | category | flops | bytes accessed | tf_op | source)
XLA Modules:
  0.0 173.7 jit_solution(151921464409499149)
XLA Ops:
  0.7 1.8 %reshape_squeeze.18 = bf16[4,192,4,128]{3,2,1,0:T(4,128)(2,1)S(1)} reshape(bf16[1,4,192,512]{3,2,1,0:T(8,128)(2,1)} %param.24) | data formatting | bytes 1572864 | tf_op jit(solution)/shard_map/reshape;squeeze | solution.py:56
  2.5 0.2 reshape_squeeze.16
  2.7 0.2 reshape_squeeze.15
  2.9 0.1 iota_compare_fusion.1
  3.0 0.7 fusion.58
  3.7 0.4 fusion.59
  4.2 0.3 fusion.24
  4.4 0.1 fusion.50
  4.6 0.4 fusion.19
  5.0 0.3 fusion.13
  5.3 0.1 all_to_all.24
  5.4 0.7 copy.56
  6.1 7.4 %all-to-all-start = ((bf16[8,16,512]{2,0,1:T(8,128)(2,1)}), bf16[8,16,512]{2,0,1:T(8,128)(2,1)S(1)}, u32[]{:S(2)}, u32[]{:S(2)}) async-start(bf16[8,16,512]{2,0,1:T(8,128)(2,1)} %copy.56), calls=%async_computation | async-start | bytes 262144 | tf_op jit(solution)/shard_map/all_to_all | solution.py:108
  13.6 7.9 %all-to-all-done = bf16[8,16,512]{2,0,1:T(8,128)(2,1)S(1)} async-done(((bf16[8,16,512]{2,0,1:T(8,128)(2,1)}), bf16[8,16,512]{2,0,1:T(8,128)(2,1)S(1)}, u32[]{:S(2)}, u32[]{:S(2)}) %all-to-all-start) | async-done | bytes 131104 | tf_op jit(solution)/shard_map/all_to_all | solution.py:108
  21.5 2.9 %fusion.2 = bf16[16,8,4096]{2,1,0:T(8,128)(2,1)S(1)} fusion(bf16[512,4096]{1,0:T(8,128)(2,1)} %param.17, f32[8,4096]{1,0:T(8,128)S(1)} %reshape.129, f32[16]{0:T(128)S(1)} %compare_convert_fusion, bf16[8,16,512]{2,0,1:T(8,128)(2,1)S(1)} %all-to-all-done), kind=kOutput, calls=%fused_computation.3 | convolution fusion | flops 538443776 | bytes 5505088 | tf_op jit(solution)/shard_map/dot_general | solution.py:109
  24.4 0.2 copy.74
  24.7 0.3 copy.57
  25.1 1.9 %collective-permute-done = bf16[2,2,2,128,256]{4,3,2,1,0:T(8,128)(2,1)S(1)} collective-permute-done((bf16[2,2,2,128,256]{4,3,2,1,0:T(8,128)(2,1)S(1)}, bf16[2,2,2,128,256]{4,3,2,1,0:T(8,128)(2,1)S(1)}, u32[]{:S(2)}, u32[]{:S(2)}) %collective-permute-start) | collective-permute-done | bytes 524320 | tf_op jit(solution)/shard_map/ppermute | solution.py:29
  27.0 0.1 fusion.16
  27.2 0.1 collective-permute-start.1
  27.3 8.3 %collective-permute-done.1 = bf16[2,2,128,256]{3,2,1,0:T(8,128)(2,1)S(1)} collective-permute-done((bf16[2,2,128,256]{3,2,1,0:T(8,128)(2,1)S(1)}, bf16[2,2,128,256]{3,2,1,0:T(8,128)(2,1)S(1)}, u32[]{:S(2)}, u32[]{:S(2)}) %collective-permute-start.1) | collective-permute-done | bytes 262176 | tf_op jit(solution)/shard_map/ppermute | solution.py:29
  35.7 0.1 collective-permute-start.2
  35.8 4.9 %collective-permute-done.2 = bf16[2,128,256]{2,1,0:T(8,128)(2,1)S(1)} collective-permute-done((bf16[2,128,256]{2,1,0:T(8,128)(2,1)S(1)}, bf16[2,128,256]{2,1,0:T(8,128)(2,1)S(1)}, u32[]{:S(2)}, u32[]{:S(2)}) %collective-permute-start.2) | collective-permute-done | bytes 131104 | tf_op jit(solution)/shard_map/ppermute | solution.py:29
  40.8 0.5 collective-permute-start.3
  41.3 0.8 dynamic_slice.125
  42.1 4.1 %collective-permute-done.3 = bf16[128,256]{1,0:T(8,128)(2,1)S(1)} collective-permute-done((bf16[128,256]{1,0:T(8,128)(2,1)S(1)}, bf16[128,256]{1,0:T(8,128)(2,1)S(1)}, u32[]{:S(2)}, u32[]{:S(2)}) %collective-permute-start.3) | collective-permute-done | bytes 65568 | tf_op jit(solution)/shard_map/ppermute | solution.py:29
  46.2 0.7 fusion.41
  46.9 4.0 %convolution_convert_fusion.1 = bf16[128,16,768]{2,0,1:T(8,128)(2,1)S(1)} fusion(bf16[16,256,768]{2,1,0:T(8,128)(2,1)} %param.14, bf16[128,256]{1,0:T(8,128)(2,1)} %get-tuple-element.3, f32[256]{0:T(256)S(1)} %dynamic_slice.125), kind=kOutput, calls=%fused_computation.11 | convolution fusion | flops 806977536 | bytes 9503744 | tf_op jit(solution)/shard_map/rd,edf->erf/dot_general | solution.py:127
  50.8 0.1 dynamic-slice_bitcast_fusion
  51.0 0.1 collective-permute-start.4
  51.1 0.5 slice-done.1
  51.6 1.8 %convolution_convert_fusion = bf16[128,16,768]{2,0,1:T(8,128)(2,1)S(1)} fusion(bf16[16,256,768]{2,1,0:T(8,128)(2,1)S(1)} %bitcast.144, bf16[128,256]{1,0:T(8,128)(2,1)} %get-tuple-element.3, f32[256]{0:T(256)S(1)} %dynamic_slice.125), kind=kOutput, calls=%fused_computation.10 | convolution fusion | flops 806977536 | bytes 9503744 | tf_op jit(solution)/shard_map/rd,edf->erf/dot_general | solution.py:127
  53.4 0.3 constant_dynamic-slice_fusion.1
  53.7 0.1 copy.99
  53.9 0.5 collective-permute-done.4
  54.4 0.4 fusion.8
  54.9 0.7 collective-permute-start.5
  55.6 1.7 collective-permute-done.8
  57.3 0.4 fusion.7
  57.9 16.7 %collective-permute-done.5 = bf16[2,2,128,768]{3,2,1,0:T(8,128)(2,1)S(1)} collective-permute-done((bf16[2,2,128,768]{3,2,1,0:T(8,128)(2,1)S(1)}, bf16[2,2,128,768]{3,2,1,0:T(8,128)(2,1)S(1)}, u32[]{:S(2)}, u32[]{:S(2)}) %collective-permute-start.5) | collective-permute-done | bytes 786464 | tf_op jit(solution)/shard_map/ppermute | solution.py:29
  74.5 0.2 fusion.10
  74.9 3.1 %collective-permute-done.9 = bf16[2,2,128,768]{3,2,1,0:T(8,128)(2,1)S(1)} collective-permute-done((bf16[2,2,128,768]{3,2,1,0:T(8,128)(2,1)S(1)}, bf16[2,2,128,768]{3,2,1,0:T(8,128)(2,1)S(1)}, u32[]{:S(2)}, u32[]{:S(2)}) %collective-permute-start.9) | collective-permute-done | bytes 786464 | tf_op jit(solution)/shard_map/ppermute | solution.py:29
  78.0 0.2 fusion.9
  78.3 0.4 collective-permute-start.10
  78.7 0.1 select_reduce_fusion
  78.8 29.0 %all-gather.1 = f32[16,16,8]{1,2,0:T(8,128)S(1)} all-gather(f32[1,16,8]{1,2,0:T(8,128)S(1)} %bitcast.155), channel_id=2, replica_groups=mesh['group'=2,'expert'=16,'dp'=1] {'expert','dp'}, dimensions={0}, use_global_device_ids=true | all-gather | bytes 8704 | tf_op jit(solution)/shard_map/all_gather | solution.py:103
  107.8 0.2 dynamic-slice_reduce_fusion
  107.9 0.1 mul.86
  108.0 29.9 %psum.7 = f32[128]{0:T(128)S(1)} all-reduce(f32[128]{0:T(128)S(1)} %get-tuple-element.2), channel_id=1, replica_groups=mesh['group'=2,'expert'=16,'dp'=1] {'expert','dp'}, use_global_device_ids=true, to_apply=%region_5.6 | all-reduce | flops 128 | bytes 1024 | tf_op jit(solution)/shard_map/psum | solution.py:120
  138.0 0.1 fusion.18
  138.2 0.1 fusion.17
  138.4 6.9 %collective-permute-done.7 = bf16[128,768]{1,0:T(8,128)(2,1)S(1)} collective-permute-done((bf16[128,768]{1,0:T(8,128)(2,1)S(1)}, bf16[128,768]{1,0:T(8,128)(2,1)S(1)}, u32[]{:S(2)}, u32[]{:S(2)}) %collective-permute-start.7) | collective-permute-done | bytes 196640 | tf_op jit(solution)/shard_map/ppermute | solution.py:29
  145.3 4.0 %fusion.3 = bf16[128,4096]{1,0:T(8,128)(2,1)S(1)} fusion(bf16[1,768,4096]{2,1,0:T(8,128)(2,1)} %param.16, bf16[128,768]{1,0:T(8,128)(2,1)S(1)} %collective-permute-done.7, bf16[128,768]{1,0:T(8,128)(2,1)S(1)} %collective-permute-done.11, f32[128]{0:T(128)S(1)} %mul.86, bf16[2,128,768]{2,1,0:T(8,128)(2,1)S(1)} %fusion.17, s32[]{:T(128)S(6)} %select_n.85, ...), kind=kOutput, calls=%fused_computation.4 | convolution fusion | flops 807698432 | bytes 8127496 | tf_op jit(solution)/shard_map/dot_general | solution.py:141
  149.4 1.9 %collective-permute-done.12 = bf16[2,2,2,8,4096]{4,3,2,1,0:T(8,128)(2,1)S(1)} collective-permute-done((bf16[2,2,2,8,4096]{4,3,2,1,0:T(8,128)(2,1)S(1)}, bf16[2,2,2,8,4096]{4,3,2,1,0:T(8,128)(2,1)S(1)}, u32[]{:S(2)}, u32[]{:S(2)}) %collective-permute-start.12) | collective-permute-done | bytes 524320 | tf_op jit(solution)/shard_map/ppermute | solution.py:29
  151.3 0.1 fusion.15
  151.4 1.4 collective-permute-start.13
  152.8 7.0 %collective-permute-done.13 = bf16[2,2,8,4096]{3,2,1,0:T(8,128)(2,1)S(1)} collective-permute-done((bf16[2,2,8,4096]{3,2,1,0:T(8,128)(2,1)S(1)}, bf16[2,2,8,4096]{3,2,1,0:T(8,128)(2,1)S(1)}, u32[]{:S(2)}, u32[]{:S(2)}) %collective-permute-start.13) | collective-permute-done | bytes 262176 | tf_op jit(solution)/shard_map/ppermute | solution.py:29
  160.0 4.8 %all-to-all-start.1 = ((bf16[16,8,256]{2,1,0:T(8,128)(2,1)}), bf16[16,8,256]{2,1,0:T(8,128)(2,1)S(1)}, u32[]{:S(2)}, u32[]{:S(2)}) async-start(bf16[16,8,256]{2,1,0:T(8,128)(2,1)} %bitcast.19), calls=%async_computation.1 | async-start | bytes 131072 | tf_op jit(solution)/shard_map/all_to_all | solution.py:114
  164.8 0.2 collective-permute-done.14
  165.0 2.7 %collective-permute-start.15 = (bf16[8,4096]{1,0:T(8,128)(2,1)S(1)}, bf16[8,4096]{1,0:T(8,128)(2,1)S(1)}, u32[]{:S(2)}, u32[]{:S(2)}) collective-permute-start(bf16[8,4096]{1,0:T(8,128)(2,1)S(1)} %dynamic-slice_bitcast_fusion.13), channel_id=1, source_target_pairs={{0,8},{1,9},{2,10},{3,11},{4,12},{5,13},{6,14},{7,15},{8,0},{9,1},... | collective-permute-start | bytes 196616 | tf_op jit(solution)/shard_map/ppermute | solution.py:29
  167.8 4.4 %all-to-all-done.1 = bf16[16,8,256]{2,1,0:T(8,128)(2,1)S(1)} async-done(((bf16[16,8,256]{2,1,0:T(8,128)(2,1)}), bf16[16,8,256]{2,1,0:T(8,128)(2,1)S(1)}, u32[]{:S(2)}, u32[]{:S(2)}) %all-to-all-start.1) | async-done | bytes 65568 | tf_op jit(solution)/shard_map/all_to_all | solution.py:114
  172.2 0.7 reshape.127
  172.9 0.2 collective-permute-done.15
  173.1 0.7 reshape.128
  (60 shorter events, 1.4 us)
Async XLA Ops:
  0.6 1.9 %copy-start = (bf16[1,4,192,512]{3,2,1,0:T(8,128)(2,1)S(1)}, bf16[1,4,192,512]{3,2,1,0:T(8,128)(2,1)}, u32[]{:S(2)}) copy-start(bf16[1,4,192,512]{3,2,1,0:T(8,128)(2,1)} %param.23) | copy-start | bytes 2359300
  0.6 2.1 %copy-start.1 = (bf16[2,1,4,8192]{3,2,1,0:T(4,128)(2,1)S(1)}, bf16[2,1,4,8192]{3,2,1,0:T(4,128)(2,1)}, u32[]{:S(2)}) copy-start(bf16[2,1,4,8192]{3,2,1,0:T(4,128)(2,1)} %param.20) | copy-start | bytes 393220
  0.7 2.2 %copy-start.7 = (s32[1,4]{1,0:T(1,128)S(1)}, s32[1,4]{1,0:T(1,128)}, u32[]{:S(2)}) copy-start(s32[1,4]{1,0:T(1,128)} %param.25) | copy-start | bytes 52
  0.7 2.3 %copy-start.3 = (bf16[2,1,4,512]{3,2,1,0:T(4,128)(2,1)S(1)}, bf16[2,1,4,512]{3,2,1,0:T(4,128)(2,1)}, u32[]{:S(2)}) copy-start(bf16[2,1,4,512]{3,2,1,0:T(4,128)(2,1)} %param.21) | copy-start | bytes 24580
  2.5 2.0 %copy-start.4 = (bf16[2,1,4,512]{3,2,1,0:T(4,128)(2,1)S(1)}, bf16[2,1,4,512]{3,2,1,0:T(4,128)(2,1)}, u32[]{:S(2)}) copy-start(bf16[2,1,4,512]{3,2,1,0:T(4,128)(2,1)} %param.22) | copy-start | bytes 24580
  4.6 9.0 %copy-start.2 = (bf16[2,1,4,4096]{3,2,1,0:T(4,128)(2,1)S(1)}, bf16[2,1,4,4096]{3,2,1,0:T(4,128)(2,1)}, u32[]{:S(2)}) copy-start(bf16[2,1,4,4096]{3,2,1,0:T(4,128)(2,1)} %param.19) | copy-start | bytes 196612
  6.1 15.3 %all-to-all-start = ((bf16[8,16,512]{2,0,1:T(8,128)(2,1)}), bf16[8,16,512]{2,0,1:T(8,128)(2,1)S(1)}, u32[]{:S(2)}, u32[]{:S(2)}) async-start(bf16[8,16,512]{2,0,1:T(8,128)(2,1)} %copy.56), calls=%async_computation | async-start | bytes 262144 | tf_op jit(solution)/shard_map/all_to_all | solution.py:108
  25.1 2.0 %collective-permute-start = (bf16[2,2,2,128,256]{4,3,2,1,0:T(8,128)(2,1)S(1)}, bf16[2,2,2,128,256]{4,3,2,1,0:T(8,128)(2,1)S(1)}, u32[]{:S(2)}, u32[]{:S(2)}) collective-permute-start(bf16[2,2,2,128,256]{4,3,2,1,0:T(8,128)(2,1)S(1)} %dynamic-slice_bitcast_fusion.4), channel_id=1, source_target_pairs={{0,1},{1,0},{2,3},{3,2},{4,5},{5,4},{6,7},{7,6},{8,9},{9,8},{10,11... | collective-permute-start | bytes 1572872 | tf_op jit(solution)/shard_map/ppermute | solution.py:29
  27.2 8.4 %collective-permute-start.1 = (bf16[2,2,128,256]{3,2,1,0:T(8,128)(2,1)S(1)}, bf16[2,2,128,256]{3,2,1,0:T(8,128)(2,1)S(1)}, u32[]{:S(2)}, u32[]{:S(2)}) collective-permute-start(bf16[2,2,128,256]{3,2,1,0:T(8,128)(2,1)S(1)} %dynamic-slice_bitcast_fusion.8), channel_id=1, source_target_pairs={{0,2},{1,3},{2,0},{3,1},{4,6},{5,7},{6,4},{7,5},{8,10},{9,11},{10,... | collective-permute-start | bytes 786440 | tf_op jit(solution)/shard_map/ppermute | solution.py:29
  35.7 5.0 %collective-permute-start.2 = (bf16[2,128,256]{2,1,0:T(8,128)(2,1)S(1)}, bf16[2,128,256]{2,1,0:T(8,128)(2,1)S(1)}, u32[]{:S(2)}, u32[]{:S(2)}) collective-permute-start(bf16[2,128,256]{2,1,0:T(8,128)(2,1)S(1)} %dynamic-slice_bitcast_fusion.12), channel_id=1, source_target_pairs={{0,4},{1,5},{2,6},{3,7},{4,0},{5,1},{6,2},{7,3},{8,12},{9,13},{10,... | collective-permute-start | bytes 393224 | tf_op jit(solution)/shard_map/ppermute | solution.py:29
  40.8 5.4 %collective-permute-start.3 = (bf16[128,256]{1,0:T(8,128)(2,1)S(1)}, bf16[128,256]{1,0:T(8,128)(2,1)S(1)}, u32[]{:S(2)}, u32[]{:S(2)}) collective-permute-start(bf16[128,256]{1,0:T(8,128)(2,1)S(1)} %dynamic-slice_bitcast_fusion.14), channel_id=1, source_target_pairs={{0,8},{1,9},{2,10},{3,11},{4,12},{5,13},{6,14},{7,15},{8,0},{9,1},... | collective-permute-start | bytes 196616 | tf_op jit(solution)/shard_map/ppermute | solution.py:29
  46.9 4.2 %slice-start = ((s8[6291456]{0:T(1024)(128)(4,1)}), s8[4194304]{0:T(1024)(128)(4,1)S(1)}, s32[]{:S(2)}) async-start(s8[6291456]{0:T(1024)(128)(4,1)} %bitcast.143), calls=%async_computation.2 | async-start | bytes 8388608
  46.9 4.7 %slice-start.1 = ((s8[6291456]{0:T(1024)(128)(4,1)}), s8[2097152]{0:T(1024)(128)(4,1)S(1)}, s32[]{:S(2)}) async-start(s8[6291456]{0:T(1024)(128)(4,1)} %bitcast.143), calls=%async_computation.3 | async-start | bytes 4194304
  51.0 3.5 %collective-permute-start.4 = (bf16[2,2,2,128,768]{4,3,2,1,0:T(8,128)(2,1)S(1)}, bf16[2,2,2,128,768]{4,3,2,1,0:T(8,128)(2,1)S(1)}, u32[]{:S(2)}, u32[]{:S(2)}) collective-permute-start(bf16[2,2,2,128,768]{4,3,2,1,0:T(8,128)(2,1)S(1)} %dynamic-slice_bitcast_fusion), channel_id=1, source_target_pairs={{0,1},{1,0},{2,3},{3,2},{4,5},{5,4},{6,7},{7,6},{8,9},{9,8},{10,11... | collective-permute-start | bytes 4718600 | tf_op jit(solution)/shard_map/ppermute | solution.py:29
  53.8 3.5 %collective-permute-start.8 = (bf16[2,2,2,128,768]{4,3,2,0,1:T(8,128)(2,1)S(1)}, bf16[2,2,2,128,768]{4,3,2,0,1:T(8,128)(2,1)S(1)}, u32[]{:S(2)}, u32[]{:S(2)}) collective-permute-start(bf16[2,2,2,128,768]{4,3,2,0,1:T(8,128)(2,1)S(1)} %bitcast.150), channel_id=1, source_target_pairs={{0,1},{1,0},{2,3},{3,2},{4,5},{5,4},{6,7},{7,6},{8,9},{9,8},{10,11... | collective-permute-start | bytes 4718600 | tf_op jit(solution)/shard_map/ppermute | solution.py:29
  54.9 19.6 %collective-permute-start.5 = (bf16[2,2,128,768]{3,2,1,0:T(8,128)(2,1)S(1)}, bf16[2,2,128,768]{3,2,1,0:T(8,128)(2,1)S(1)}, u32[]{:S(2)}, u32[]{:S(2)}) collective-permute-start(bf16[2,2,128,768]{3,2,1,0:T(8,128)(2,1)S(1)} %dynamic-slice_bitcast_fusion.2), channel_id=1, source_target_pairs={{0,2},{1,3},{2,0},{3,1},{4,6},{5,7},{6,4},{7,5},{8,10},{9,11},{10,... | collective-permute-start | bytes 2359304 | tf_op jit(solution)/shard_map/ppermute | solution.py:29
  57.8 20.2 %collective-permute-start.9 = (bf16[2,2,128,768]{3,2,1,0:T(8,128)(2,1)S(1)}, bf16[2,2,128,768]{3,2,1,0:T(8,128)(2,1)S(1)}, u32[]{:S(2)}, u32[]{:S(2)}) collective-permute-start(bf16[2,2,128,768]{3,2,1,0:T(8,128)(2,1)S(1)} %dynamic-slice_bitcast_fusion.1), channel_id=1, source_target_pairs={{0,4},{1,5},{2,6},{3,7},{4,0},{5,1},{6,2},{7,3},{8,12},{9,13},{10,... | collective-permute-start | bytes 2359304 | tf_op jit(solution)/shard_map/ppermute | solution.py:29
  74.8 3.9 %copy-start.5 = (f32[2,1,4,8]{3,2,1,0:T(4,128)S(1)}, f32[2,1,4,8]{3,2,1,0:T(4,128)}, u32[]{:S(2)}) copy-start(f32[2,1,4,8]{3,2,1,0:T(4,128)} %param.27) | copy-start | bytes 772
  74.8 3.9 %copy-start.6 = (s32[2,1,4,8]{3,2,1,0:T(4,128)S(1)}, s32[2,1,4,8]{3,2,1,0:T(4,128)}, u32[]{:S(2)}) copy-start(s32[2,1,4,8]{3,2,1,0:T(4,128)} %param.26) | copy-start | bytes 772
  74.8 63.1 %collective-permute-start.6 = (bf16[2,128,768]{2,1,0:T(8,128)(2,1)S(1)}, bf16[2,128,768]{2,1,0:T(8,128)(2,1)S(1)}, u32[]{:S(2)}, u32[]{:S(2)}) collective-permute-start(bf16[2,128,768]{2,1,0:T(8,128)(2,1)S(1)} %dynamic-slice_bitcast_fusion.6), channel_id=1, source_target_pairs={{0,4},{1,5},{2,6},{3,7},{4,0},{5,1},{6,2},{7,3},{8,12},{9,13},{10,... | collective-permute-start | bytes 1179656 | tf_op jit(solution)/shard_map/ppermute | solution.py:29
  78.3 59.9 %collective-permute-start.10 = (bf16[2,128,768]{2,1,0:T(8,128)(2,1)S(1)}, bf16[2,128,768]{2,1,0:T(8,128)(2,1)S(1)}, u32[]{:S(2)}, u32[]{:S(2)}) collective-permute-start(bf16[2,128,768]{2,1,0:T(8,128)(2,1)S(1)} %dynamic-slice_bitcast_fusion.5), channel_id=1, source_target_pairs={{0,8},{1,9},{2,10},{3,11},{4,12},{5,13},{6,14},{7,15},{8,0},{9,1},... | collective-permute-start | bytes 1179656 | tf_op jit(solution)/shard_map/ppermute | solution.py:29
  138.1 7.2 %collective-permute-start.7 = (bf16[128,768]{1,0:T(8,128)(2,1)S(1)}, bf16[128,768]{1,0:T(8,128)(2,1)S(1)}, u32[]{:S(2)}, u32[]{:S(2)}) collective-permute-start(bf16[128,768]{1,0:T(8,128)(2,1)S(1)} %dynamic-slice_bitcast_fusion.10), channel_id=1, source_target_pairs={{0,8},{1,9},{2,10},{3,11},{4,12},{5,13},{6,14},{7,15},{8,0},{9,1},... | collective-permute-start | bytes 589832 | tf_op jit(solution)/shard_map/ppermute | solution.py:29
  138.3 7.0 %collective-permute-start.11 = (bf16[128,768]{1,0:T(8,128)(2,1)S(1)}, bf16[128,768]{1,0:T(8,128)(2,1)S(1)}, u32[]{:S(2)}, u32[]{:S(2)}) collective-permute-start(bf16[128,768]{1,0:T(8,128)(2,1)S(1)} %dynamic-slice_bitcast_fusion.9), channel_id=1, source_target_pairs={{0,2},{1,3},{2,0},{3,1},{4,6},{5,7},{6,4},{7,5},{8,10},{9,11},{10,... | collective-permute-start | bytes 589832 | tf_op jit(solution)/shard_map/ppermute | solution.py:29
  149.3 2.0 %collective-permute-start.12 = (bf16[2,2,2,8,4096]{4,3,2,1,0:T(8,128)(2,1)S(1)}, bf16[2,2,2,8,4096]{4,3,2,1,0:T(8,128)(2,1)S(1)}, u32[]{:S(2)}, u32[]{:S(2)}) collective-permute-start(bf16[2,2,2,8,4096]{4,3,2,1,0:T(8,128)(2,1)S(1)} %dynamic-slice_bitcast_fusion.3), channel_id=1, source_target_pairs={{0,1},{1,0},{2,3},{3,2},{4,5},{5,4},{6,7},{7,6},{8,9},{9,8},{10,11... | collective-permute-start | bytes 1572872 | tf_op jit(solution)/shard_map/ppermute | solution.py:29
  151.4 8.4 %collective-permute-start.13 = (bf16[2,2,8,4096]{3,2,1,0:T(8,128)(2,1)S(1)}, bf16[2,2,8,4096]{3,2,1,0:T(8,128)(2,1)S(1)}, u32[]{:S(2)}, u32[]{:S(2)}) collective-permute-start(bf16[2,2,8,4096]{3,2,1,0:T(8,128)(2,1)S(1)} %dynamic-slice_bitcast_fusion.7), channel_id=1, source_target_pairs={{0,2},{1,3},{2,0},{3,1},{4,6},{5,7},{6,4},{7,5},{8,10},{9,11},{10,... | collective-permute-start | bytes 786440 | tf_op jit(solution)/shard_map/ppermute | solution.py:29
  160.0 5.0 %collective-permute-start.14 = (bf16[2,8,4096]{2,1,0:T(8,128)(2,1)S(1)}, bf16[2,8,4096]{2,1,0:T(8,128)(2,1)S(1)}, u32[]{:S(2)}, u32[]{:S(2)}) collective-permute-start(bf16[2,8,4096]{2,1,0:T(8,128)(2,1)S(1)} %dynamic-slice_bitcast_fusion.11), channel_id=1, source_target_pairs={{0,4},{1,5},{2,6},{3,7},{4,0},{5,1},{6,2},{7,3},{8,12},{9,13},{10,... | collective-permute-start | bytes 393224 | tf_op jit(solution)/shard_map/ppermute | solution.py:29
  160.0 12.1 %all-to-all-start.1 = ((bf16[16,8,256]{2,1,0:T(8,128)(2,1)}), bf16[16,8,256]{2,1,0:T(8,128)(2,1)S(1)}, u32[]{:S(2)}, u32[]{:S(2)}) async-start(bf16[16,8,256]{2,1,0:T(8,128)(2,1)} %bitcast.19), calls=%async_computation.1 | async-start | bytes 131072 | tf_op jit(solution)/shard_map/all_to_all | solution.py:114
  165.0 8.0 %collective-permute-start.15 = (bf16[8,4096]{1,0:T(8,128)(2,1)S(1)}, bf16[8,4096]{1,0:T(8,128)(2,1)S(1)}, u32[]{:S(2)}, u32[]{:S(2)}) collective-permute-start(bf16[8,4096]{1,0:T(8,128)(2,1)S(1)} %dynamic-slice_bitcast_fusion.13), channel_id=1, source_target_pairs={{0,8},{1,9},{2,10},{3,11},{4,12},{5,13},{6,14},{7,15},{8,0},{9,1},... | collective-permute-start | bytes 196616 | tf_op jit(solution)/shard_map/ppermute | solution.py:29

commit v2 on v1

--- a/solution.py
+++ b/solution.py
@@ -28,6 +28,15 @@
         send = lax.dynamic_index_in_dim(x, 1 - mine, at, keepdims=False)
         got = lax.ppermute(send, axis_name, [(i, i ^ (1 << bit)) for i in range(count)])
         x = (keep.astype(F32) + got.astype(F32)).astype(BF16)
+    return x
+
+
+def add_up(x):
+    if lax.axis_size("dp") > 1:
+        x = lax.psum(x, "dp")
+    count = lax.axis_size("expert")
+    for bit in range(count.bit_length() - 1):
+        x = x + lax.ppermute(x, "expert", [(i, i ^ (1 << bit)) for i in range(count)])
     return x
 
 
@@ -100,24 +109,43 @@
     probs = gate_probs.reshape(own, top)
     match = ids[:, :, None] == jnp.arange(experts, dtype=jnp.int32)[None, None, :]
     coefs = jnp.sum(jnp.where(match, probs[:, :, None], 0.0), axis=1)
-    coefs = lax.all_gather(coefs.T, ("expert", "dp"), axis=0)
-    coefs = lax.dynamic_index_in_dim(coefs, me, 1, keepdims=False)
-    coefs = coefs.reshape(ring, pair, own).swapaxes(0, 1).reshape(-1)
+    coarse = coefs.astype(BF16)
+    fine = (coefs - coarse.astype(F32)).astype(BF16)
+    lanes = -(-2 * experts // 128) * 128
+    extra = jnp.pad(jnp.concatenate([coarse, fine], axis=1), ((0, 0), (0, lanes - 2 * experts)))
 
     attended = attend(queries, token_keys, token_values, cached_key_rows, cached_value_rows, lengths)
-    spread = lax.all_to_all(attended, "expert", split_axis=1, concat_axis=0, tiled=True)
+    packed = jnp.concatenate(
+        [attended.reshape(own, ring, -1), jnp.broadcast_to(extra[:, None], (own, ring, lanes))], axis=2
+    )
+    spread = lax.all_to_all(
+        packed.reshape(own, -1), "expert", split_axis=1, concat_axis=0, tiled=True
+    )
+    heads = out_proj.shape[0]
+    coefs = spread[:, heads:].astype(F32)
+    coefs = coefs[:, :experts] + coefs[:, experts : 2 * experts]
+    coefs = lax.dynamic_index_in_dim(coefs, me, 1, keepdims=False)
+    if pair > 1:
+        coefs = lax.all_gather(coefs, "dp", axis=0, tiled=True)
+    spread = spread[:, :heads]
     partial = jnp.dot(spread, out_proj, preferred_element_type=F32)
     place = (jnp.arange(ring) == me).astype(F32)
     partial = partial.reshape(ring, own, width) + place[:, None, None] * residual.reshape(1, own, width).astype(F32)
     partial = partial.astype(BF16).reshape(ring * own, ring, width // ring).swapaxes(0, 1)
-    columns = scatter_sum(partial, "expert", near_first)
+    middle = partial.shape[1] // 2
+    columns = jnp.concatenate(
+        [
+            scatter_sum(partial[:, :middle], "expert", near_first),
+            scatter_sum(partial[:, middle:], "expert", far_first),
+        ],
+        axis=0,
+    )
     back = lax.all_to_all(columns, "expert", split_axis=0, concat_axis=1, tiled=True)
-    stream = back.reshape(residual.shape)
     if pair > 1:
         columns = lax.all_to_all(columns, "dp", split_axis=1, concat_axis=0, tiled=True)
 
     wide = columns.astype(F32)
-    square = lax.psum(jnp.sum(wide * wide, axis=1), ("expert", "dp"))
+    square = add_up(jnp.sum(wide * wide, axis=1))
     scale = lax.rsqrt(square / width + 1e-6)[:, None]
     gain = lax.dynamic_slice_in_dim(norm_gain, (me * pair + half) * depth, depth)
     scaled = (wide * gain[None, :]).astype(BF16)
@@ -135,12 +163,18 @@
         gate, up = both(scaled)
     else:
         gate, up = lax.map(both, scaled.reshape(-1, 128, depth))
+    gate, up, back = lax.optimization_barrier((gate, up, back))
+    stream = back.reshape(residual.shape)
     gate = gate.reshape(all_rows, -1).astype(F32) * scale
     up = up.reshape(all_rows, -1).astype(F32) * scale
     hidden = (jax.nn.silu(gate) * up * coefs[:, None]).astype(BF16)
     out = jnp.dot(hidden, down_weight[0], preferred_element_type=F32).astype(BF16)
     out = out.reshape(pair, ring, own, width).swapaxes(0, 1)
-    mixed = scatter_both(out, near_first).reshape(residual.shape)
+    middle = width // 2
+    mixed = jnp.concatenate(
+        [scatter_both(out[..., :middle], near_first), scatter_both(out[..., middle:], far_first)],
+        axis=1,
+    ).reshape(residual.shape)
     return (stream, mixed)
 
 

time: 174 us -> 154 us (0.89)
  blocking collectives: 58.9 us -> 0 us
  waiting for transfers between devices: 69.8 us -> 82.2 us
  local copies, waits for them, and re-layouts: 7.45 us -> 17.6 us
  starting transfers between devices: 18.7 us -> 28.1 us
  other arithmetic: 3.13 us -> 10.7 us
    psum x1 -> x0, blocking collectives: 29.9 us -> none  [shards(): square = lax.psum(jnp.sum(wide * wide, axis=1), ('expert', 'dp'))]
    all_gather x1 -> x0, blocking collectives: 29 us -> none  [shards(): coefs = lax.all_gather(coefs.T, ('expert', 'dp'), axis=0)]
    ppermute x0 -> x4, waiting for transfers between devices: none -> 17.4 us  [add_up(): x = x + lax.ppermute(x, 'expert', [(i, i ^ 1 << bit) for i in range(count)])]
    convert_element_type x13 -> x24, other arithmetic: 1.9 us -> 7.52 us  [scatter_sum(): x = (keep.astype(F32) + got.astype(F32)).astype(BF16)]
    ppermute x0 -> x4, starting transfers between devices: none -> 5.62 us  [add_up(): x = x + lax.ppermute(x, 'expert', [(i, i ^ 1 << bit) for i in range(count)])]
    ppermute x16 -> x24, starting transfers between devices: 6.51 us -> 11.4 us  [scatter_sum(): lax.ppermute(send, axis_name, [(i, i ^ 1 << bit) for i in range(count)])]
    all_to_all x1, waiting for transfers between devices: 4.39 us -> 0.01 us  [shards(): lax.all_to_all(columns, 'expert', split_axis=0, concat_axis=1, tiled=True)]
    squeeze x15 -> x20, local copies, waits for them, and re-layouts: 0.55 us -> 3.58 us  [scatter_sum(): send = lax.dynamic_index_in_dim(x, 1 - mine, at, keepdims=False)]
  transfers between devices with their start and end apart: 18 -> 30, of which waited for: 15 -> 21; matrix products, arithmetic and copies ran while one was open for 3% -> 10% of each run, Pallas kernels for 0% -> 0%
where the time goes in v2:
time: 154 us
  waiting for transfers between devices  82.2 us (53%)
  starting transfers between devices  28.1 us (18%)
  local copies, waits for them, and re-layouts  17.6 us (11%)
  matrix products  13.6 us (9%)
  other arithmetic  10.7 us (7%)
    ppermute x24, waiting for transfers between devices, scatter_sum(): lax.ppermute(send, axis_name, [(i, i ^ 1 << bit) for i in range(count)])  57.4 us
    ppermute x4, waiting for transfers between devices, add_up(): x = x + lax.ppermute(x, 'expert', [(i, i ^ 1 << bit) for i in range(count)])  17.4 us
    ppermute x24, starting transfers between devices, scatter_sum(): lax.ppermute(send, axis_name, [(i, i ^ 1 << bit) for i in range(count)])  11.4 us
    convert_element_type x24, other arithmetic, scatter_sum(): x = (keep.astype(F32) + got.astype(F32)).astype(BF16)  7.52 us
    all_to_all x1, starting transfers between devices, shards(): lax.all_to_all(packed.reshape(own, -1), 'expert', split_axis=1, concat_ax...  7.39 us
    all_to_all x1, waiting for transfers between devices, shards(): lax.all_to_all(packed.reshape(own, -1), 'expert', split_axis=1, concat_ax...  7.38 us
    ppermute x4, starting transfers between devices, add_up(): x = x + lax.ppermute(x, 'expert', [(i, i ^ 1 << bit) for i in range(count)])  5.62 us
    dot_general x2, matrix products, project(): jnp.einsum('rd,edf->erf', chosen, weight, preferred_element_type=F32)  4.94 us
  transfers between devices with their start and end apart: 30, of which 21 were waited for; matrix products, arithmetic and copies ran while one was open for 10% of the time, Pallas kernels for 0%

profile of v2, /device:TPU:0, one launch (start us, length us, event | category | flops | bytes accessed | tf_op | source)
XLA Modules:
  0.0 153.6 jit_solution(12153979350910172885)
XLA Ops:
  0.6 0.7 iota_compare_fusion.2
  1.4 0.8 select_reduce_fusion
  2.2 0.7 reshape_squeeze.23
  2.9 0.7 reshape_squeeze.25
  3.6 1.1 reshape_squeeze.21
  4.7 1.8 %reshape_squeeze.22 = bf16[4,192,4,128]{3,2,1,0:T(4,128)(2,1)S(1)} reshape(bf16[1,4,192,512]{3,2,1,0:T(8,128)(2,1)} %param.23) | data formatting | bytes 1572864 | tf_op jit(solution)/shard_map/reshape;squeeze | solution.py:64
  7.0 0.7 fusion.70
  9.2 0.7 copy.88
  9.9 7.4 %all-to-all-start = ((bf16[8,16,640]{2,0,1:T(8,128)(2,1)}), bf16[8,16,640]{2,0,1:T(8,128)(2,1)S(1)}, u32[]{:S(2)}, u32[]{:S(2)}) async-start(bf16[8,16,640]{2,0,1:T(8,128)(2,1)} %copy.88), calls=%async_computation | async-start | bytes 327680 | tf_op jit(solution)/shard_map/all_to_all | solution.py:121
  17.7 0.7 copy.116
  18.4 7.4 %all-to-all-done = bf16[8,16,640]{2,0,1:T(8,128)(2,1)S(1)} async-done(((bf16[8,16,640]{2,0,1:T(8,128)(2,1)}), bf16[8,16,640]{2,0,1:T(8,128)(2,1)S(1)}, u32[]{:S(2)}, u32[]{:S(2)}) %all-to-all-start) | async-done | bytes 163872 | tf_op jit(solution)/shard_map/all_to_all | solution.py:121
  25.7 2.9 %fusion.41 = f32[128,4096]{1,0:T(8,128)S(1)} fusion(bf16[512,4096]{1,0:T(8,128)(2,1)} %param.17, bf16[128,640]{1,0:T(8,128)(2,1)S(1)} %bitcast.208), kind=kOutput, calls=%fused_computation.81 | convolution fusion | flops 536870912 | bytes 6422528 | tf_op jit(solution)/shard_map/dot_general | solution.py:131
  28.7 0.7 copy.115
  30.0 0.8 dynamic_slice.185
  31.0 0.5 collective-permute-start.4
  31.7 1.0 collective-permute-done.4
  32.8 4.3 %collective-permute-done.1 = bf16[2,2,64,256]{3,2,1,0:T(8,128)(2,1)S(1)} collective-permute-done((bf16[2,2,64,256]{3,2,1,0:T(8,128)(2,1)S(1)}, bf16[2,2,64,256]{3,2,1,0:T(8,128)(2,1)S(1)}, u32[]{:S(2)}, u32[]{:S(2)}) %collective-permute-start.1) | collective-permute-done | bytes 131104 | tf_op jit(solution)/shard_map/ppermute | solution.py:29
  37.4 1.2 collective-permute-done.5
  38.7 0.6 collective-permute-start.6
  39.3 2.3 %collective-permute-done.2 = bf16[2,64,256]{2,1,0:T(8,128)(2,1)S(1)} collective-permute-done((bf16[2,64,256]{2,1,0:T(8,128)(2,1)S(1)}, bf16[2,64,256]{2,1,0:T(8,128)(2,1)S(1)}, u32[]{:S(2)}, u32[]{:S(2)}) %collective-permute-start.2) | collective-permute-done | bytes 65568 | tf_op jit(solution)/shard_map/ppermute | solution.py:29
  41.6 0.6 collective-permute-start.3
  42.2 3.1 %collective-permute-done.6 = bf16[2,64,256]{2,1,0:T(8,128)(2,1)S(1)} collective-permute-done((bf16[2,64,256]{2,1,0:T(8,128)(2,1)S(1)}, bf16[2,64,256]{2,1,0:T(8,128)(2,1)S(1)}, u32[]{:S(2)}, u32[]{:S(2)}) %collective-permute-start.6) | collective-permute-done | bytes 65568 | tf_op jit(solution)/shard_map/ppermute | solution.py:29
  45.3 0.6 collective-permute-start.7
  45.9 0.8 collective-permute-done.3
  46.6 2.7 %collective-permute-done.7 = bf16[64,256]{1,0:T(8,128)(2,1)S(1)} collective-permute-done((bf16[64,256]{1,0:T(8,128)(2,1)S(1)}, bf16[64,256]{1,0:T(8,128)(2,1)S(1)}, u32[]{:S(2)}, u32[]{:S(2)}) %collective-permute-start.7) | collective-permute-done | bytes 32800 | tf_op jit(solution)/shard_map/ppermute | solution.py:29
  49.3 3.9 %convolution_convert_fusion = bf16[128,16,768]{2,0,1:T(8,128)(2,1)S(1)} fusion(bf16[16,256,768]{2,1,0:T(8,128)(2,1)} %param.15, f32[256]{0:T(256)S(1)} %dynamic_slice.185, bf16[64,256]{1,0:T(8,128)(2,1)S(1)} %fusion.53, bf16[64,256]{1,0:T(8,128)(2,1)S(1)} %fusion.54), kind=kOutput, calls=%fused_computation.8 | convolution fusion | flops 807075840 | bytes 9503744 | tf_op jit(solution)/shard_map/rd,edf->erf/dot_general | solution.py:155
  53.3 1.4 constant_dynamic-slice_fusion.5
  54.7 1.3 copy.153
  56.0 1.0 convolution_convert_fusion.1
  57.0 1.3 dynamic-slice_bitcast_fusion
  58.2 0.5 collective-permute-start.8
  58.7 1.0 collective-permute-done.12
  59.7 2.3 %fusion.8 = bf16[2,2,2,128,768]{4,3,2,0,1:T(8,128)(2,1)S(1)} fusion(bf16[2,2,2,128,768]{4,3,2,0,1:T(8,128)(2,1)} %collective-permute-done.12, bf16[2,2,2,1,128,768]{5,4,3,2,1,0:T(8,128)(2,1)} %get-tuple-element.10), kind=kLoop, calls=%fused_computation.5 | loop fusion | flops 3145728 | bytes 4718592 | tf_op jit(solution)/shard_map/convert_element_type | solution.py:30
  62.0 1.1 dynamic-slice_bitcast_fusion.1
  63.4 1.8 %fusion.9 = bf16[2,2,2,128,768]{4,3,2,1,0:T(8,128)(2,1)S(1)} fusion(bf16[2,2,2,128,768]{4,3,2,1,0:T(8,128)(2,1)} %collective-permute-done.8, bf16[2,2,2,2,128,768]{5,4,3,2,1,0:T(8,128)(2,1)S(1)} %bitcast.194, s32[]{:T(128)S(6)} %select_n.104), kind=kLoop, calls=%fused_computation.7 | loop fusion | flops 3145728 | bytes 4718596 | tf_op jit(solution)/shard_map/convert_element_type | solution.py:30
  65.2 1.1 copy-done
  66.3 1.0 dynamic-slice_bitcast_fusion.2
  68.1 1.0 collective-permute-done.16
  69.1 1.5 %collective-permute-start.17 = (f32[128]{0:T(128)S(1)}, f32[128]{0:T(128)S(1)}, u32[]{:S(2)}, u32[]{:S(2)}) collective-permute-start(f32[128]{0:T(128)S(1)} %add.237), channel_id=1, source_target_pairs={{0,2},{1,3},{2,0},{3,1},{4,6},{5,7},{6,4},{7,5},{8,10},{9,11},{10,... | collective-permute-start | bytes 1544 | tf_op jit(solution)/shard_map/ppermute | solution.py:39
  70.8 16.4 %collective-permute-done.17 = f32[128]{0:T(128)S(1)} collective-permute-done((f32[128]{0:T(128)S(1)}, f32[128]{0:T(128)S(1)}, u32[]{:S(2)}, u32[]{:S(2)}) %collective-permute-start.17) | collective-permute-done | bytes 544 | tf_op jit(solution)/shard_map/ppermute | solution.py:39
  87.2 1.4 collective-permute-start.18
  88.6 0.6 fusion.66
  89.2 3.7 %all-to-all-start.1 = ((bf16[16,8,256]{2,1,0:T(8,128)(2,1)}), bf16[16,8,256]{2,1,0:T(8,128)(2,1)S(1)}, u32[]{:S(2)}, u32[]{:S(2)}) async-start(bf16[16,8,256]{2,1,0:T(8,128)(2,1)} %fusion.66), calls=%async_computation.1 | async-start | bytes 131072 | tf_op jit(solution)/shard_map/all_to_all | solution.py:143
  92.9 2.6 %collective-permute-start.19 = (f32[128]{0:T(128)S(1)}, f32[128]{0:T(128)S(1)}, u32[]{:S(2)}, u32[]{:S(2)}) collective-permute-start(f32[128]{0:T(128)S(1)} %add.239), channel_id=1, source_target_pairs={{0,8},{1,9},{2,10},{3,11},{4,12},{5,13},{6,14},{7,15},{8,0},{9,1},... | collective-permute-start | bytes 1544 | tf_op jit(solution)/shard_map/ppermute | solution.py:39
  95.6 1.3 fusion.12
  97.4 1.3 fusion.13
  98.7 1.7 %collective-permute-start.10 = (bf16[2,128,768]{2,1,0:T(8,128)(2,1)S(1)}, bf16[2,128,768]{2,1,0:T(8,128)(2,1)S(1)}, u32[]{:S(2)}, u32[]{:S(2)}) collective-permute-start(bf16[2,128,768]{2,1,0:T(8,128)(2,1)S(1)} %dynamic-slice_bitcast_fusion.4), channel_id=1, source_target_pairs={{0,4},{1,5},{2,6},{3,7},{4,0},{5,1},{6,2},{7,3},{8,12},{9,13},{10,... | collective-permute-start | bytes 1179656 | tf_op jit(solution)/shard_map/ppermute | solution.py:29
  100.4 16.8 %collective-permute-done.14 = bf16[2,128,768]{2,1,0:T(8,128)(2,1)S(1)} collective-permute-done((bf16[2,128,768]{2,1,0:T(8,128)(2,1)S(1)}, bf16[2,128,768]{2,1,0:T(8,128)(2,1)S(1)}, u32[]{:S(2)}, u32[]{:S(2)}) %collective-permute-start.14) | collective-permute-done | bytes 393248 | tf_op jit(solution)/shard_map/ppermute | solution.py:29
  117.4 1.5 %collective-permute-start.15 = (bf16[128,768]{1,0:T(8,128)(2,1)S(1)}, bf16[128,768]{1,0:T(8,128)(2,1)S(1)}, u32[]{:S(2)}, u32[]{:S(2)}) collective-permute-start(bf16[128,768]{1,0:T(8,128)(2,1)S(1)} %dynamic-slice_bitcast_fusion.6), channel_id=1, source_target_pairs={{0,2},{1,3},{2,0},{3,1},{4,6},{5,7},{6,4},{7,5},{8,10},{9,11},{10,... | collective-permute-start | bytes 589832 | tf_op jit(solution)/shard_map/ppermute | solution.py:29
  119.5 3.8 %collective-permute-done.15 = bf16[128,768]{1,0:T(8,128)(2,1)S(1)} collective-permute-done((bf16[128,768]{1,0:T(8,128)(2,1)S(1)}, bf16[128,768]{1,0:T(8,128)(2,1)S(1)}, u32[]{:S(2)}, u32[]{:S(2)}) %collective-permute-start.15) | collective-permute-done | bytes 196640 | tf_op jit(solution)/shard_map/ppermute | solution.py:29
  123.4 6.2 %collective-permute-done.11 = bf16[128,768]{1,0:T(8,128)(2,1)S(1)} collective-permute-done((bf16[128,768]{1,0:T(8,128)(2,1)S(1)}, bf16[128,768]{1,0:T(8,128)(2,1)S(1)}, u32[]{:S(2)}, u32[]{:S(2)}) %collective-permute-start.11) | collective-permute-done | bytes 196640 | tf_op jit(solution)/shard_map/ppermute | solution.py:29
  129.6 3.9 %fusion.5 = bf16[16,1,8,4096]{3,2,0,1:T(8,128)(2,1)S(1)} fusion(bf16[1,768,4096]{2,1,0:T(8,128)(2,1)} %param.16, bf16[128,768]{1,0:T(8,128)(2,1)S(1)} %fusion.28, bf16[128,768]{1,0:T(8,128)(2,1)S(1)} %fusion.29, f32[128]{0:T(128)S(1)} %fusion.50, f32[128]{0:T(128)S(1)} %add_rsqrt_fusion), kind=kOutput, calls=%fused_computation.3 | convolution fusion | flops 806912000 | bytes 7734272 | tf_op jit(solution)/shard_map/dot_general | solution.py:171
  133.9 0.7 reshape.146
  134.5 0.6 collective-permute-start.24
  135.5 0.9 collective-permute-start.21
  136.5 4.6 %collective-permute-done.21 = bf16[2,2,8,2048]{3,2,0,1:T(8,128)(2,1)S(1)} collective-permute-done((bf16[2,2,8,2048]{3,2,0,1:T(8,128)(2,1)S(1)}, bf16[2,2,8,2048]{3,2,0,1:T(8,128)(2,1)S(1)}, u32[]{:S(2)}, u32[]{:S(2)}) %collective-permute-start.21) | collective-permute-done | bytes 131104 | tf_op jit(solution)/shard_map/ppermute | solution.py:29
  141.2 1.0 collective-permute-done.25
  142.3 1.1 collective-permute-start.26
  143.3 2.3 %collective-permute-done.22 = bf16[2,8,2048]{2,1,0:T(8,128)(2,1)S(1)} collective-permute-done((bf16[2,8,2048]{2,1,0:T(8,128)(2,1)S(1)}, bf16[2,8,2048]{2,1,0:T(8,128)(2,1)S(1)}, u32[]{:S(2)}, u32[]{:S(2)}) %collective-permute-start.22) | collective-permute-done | bytes 65568 | tf_op jit(solution)/shard_map/ppermute | solution.py:29
  145.7 3.2 %collective-permute-done.26 = bf16[2,8,2048]{2,1,0:T(8,128)(2,1)S(1)} collective-permute-done((bf16[2,8,2048]{2,1,0:T(8,128)(2,1)S(1)}, bf16[2,8,2048]{2,1,0:T(8,128)(2,1)S(1)}, u32[]{:S(2)}, u32[]{:S(2)}) %collective-permute-start.26) | collective-permute-done | bytes 65568 | tf_op jit(solution)/shard_map/ppermute | solution.py:29
  148.9 0.9 collective-permute-start.27
  149.8 0.9 collective-permute-done.23
  150.7 2.2 %collective-permute-done.27 = bf16[8,2048]{1,0:T(8,128)(2,1)S(1)} collective-permute-done((bf16[8,2048]{1,0:T(8,128)(2,1)S(1)}, bf16[8,2048]{1,0:T(8,128)(2,1)S(1)}, u32[]{:S(2)}, u32[]{:S(2)}) %collective-permute-start.27) | collective-permute-done | bytes 32800 | tf_op jit(solution)/shard_map/ppermute | solution.py:29
  152.9 0.7 reshape.147
  (116 shorter events, 7.6 us)
Async XLA Ops:
  4.7 3.4 %copy-start.4 = (bf16[1,4,192,512]{3,2,1,0:T(8,128)(2,1)S(1)}, bf16[1,4,192,512]{3,2,1,0:T(8,128)(2,1)}, u32[]{:S(2)}) copy-start(bf16[1,4,192,512]{3,2,1,0:T(8,128)(2,1)} %param.24) | copy-start | bytes 2359300
  8.3 9.2 %copy-start.5 = (bf16[2,1,4,4096]{3,2,1,0:T(4,128)(2,1)S(1)}, bf16[2,1,4,4096]{3,2,1,0:T(4,128)(2,1)}, u32[]{:S(2)}) copy-start(bf16[2,1,4,4096]{3,2,1,0:T(4,128)(2,1)} %param.19) | copy-start | bytes 196612
  9.9 15.9 %all-to-all-start = ((bf16[8,16,640]{2,0,1:T(8,128)(2,1)}), bf16[8,16,640]{2,0,1:T(8,128)(2,1)S(1)}, u32[]{:S(2)}, u32[]{:S(2)}) async-start(bf16[8,16,640]{2,0,1:T(8,128)(2,1)} %copy.88), calls=%async_computation | async-start | bytes 327680 | tf_op jit(solution)/shard_map/all_to_all | solution.py:121
  29.9 1.6 %collective-permute-start = (bf16[2,2,2,64,256]{4,3,2,1,0:T(8,128)(2,1)S(1)}, bf16[2,2,2,64,256]{4,3,2,1,0:T(8,128)(2,1)S(1)}, u32[]{:S(2)}, u32[]{:S(2)}) collective-permute-start(bf16[2,2,2,64,256]{4,3,2,1,0:T(8,128)(2,1)S(1)} %dynamic-slice_bitcast_fusion.5), channel_id=1, source_target_pairs={{0,1},{1,0},{2,3},{3,2},{4,5},{5,4},{6,7},{7,6},{8,9},{9,8},{10,11... | collective-permute-start | bytes 786440 | tf_op jit(solution)/shard_map/ppermute | solution.py:29
  31.0 1.7 %collective-permute-start.4 = (bf16[2,2,2,64,256]{4,3,2,0,1:T(8,128)(2,1)S(1)}, bf16[2,2,2,64,256]{4,3,2,0,1:T(8,128)(2,1)S(1)}, u32[]{:S(2)}, u32[]{:S(2)}) collective-permute-start(bf16[2,2,2,64,256]{4,3,2,0,1:T(8,128)(2,1)S(1)} %bitcast.210), channel_id=1, source_target_pairs={{0,1},{1,0},{2,3},{3,2},{4,5},{5,4},{6,7},{7,6},{8,9},{9,8},{10,11... | collective-permute-start | bytes 786440 | tf_op jit(solution)/shard_map/ppermute | solution.py:29
  31.6 5.6 %collective-permute-start.1 = (bf16[2,2,64,256]{3,2,1,0:T(8,128)(2,1)S(1)}, bf16[2,2,64,256]{3,2,1,0:T(8,128)(2,1)S(1)}, u32[]{:S(2)}, u32[]{:S(2)}) collective-permute-start(bf16[2,2,64,256]{3,2,1,0:T(8,128)(2,1)S(1)} %dynamic-slice_bitcast_fusion.11), channel_id=1, source_target_pairs={{0,2},{1,3},{2,0},{3,1},{4,6},{5,7},{6,4},{7,5},{8,10},{9,11},{10,... | collective-permute-start | bytes 393224 | tf_op jit(solution)/shard_map/ppermute | solution.py:29
  32.8 5.8 %collective-permute-start.5 = (bf16[2,2,64,256]{3,2,1,0:T(8,128)(2,1)S(1)}, bf16[2,2,64,256]{3,2,1,0:T(8,128)(2,1)S(1)}, u32[]{:S(2)}, u32[]{:S(2)}) collective-permute-start(bf16[2,2,64,256]{3,2,1,0:T(8,128)(2,1)S(1)} %dynamic-slice_bitcast_fusion.10), channel_id=1, source_target_pairs={{0,4},{1,5},{2,6},{3,7},{4,0},{5,1},{6,2},{7,3},{8,12},{9,13},{10,... | collective-permute-start | bytes 393224 | tf_op jit(solution)/shard_map/ppermute | solution.py:29
  37.2 4.3 %collective-permute-start.2 = (bf16[2,64,256]{2,1,0:T(8,128)(2,1)S(1)}, bf16[2,64,256]{2,1,0:T(8,128)(2,1)S(1)}, u32[]{:S(2)}, u32[]{:S(2)}) collective-permute-start(bf16[2,64,256]{2,1,0:T(8,128)(2,1)S(1)} %dynamic-slice_bitcast_fusion.15), channel_id=1, source_target_pairs={{0,4},{1,5},{2,6},{3,7},{4,0},{5,1},{6,2},{7,3},{8,12},{9,13},{10,... | collective-permute-start | bytes 196616 | tf_op jit(solution)/shard_map/ppermute | solution.py:29
  38.7 6.6 %collective-permute-start.6 = (bf16[2,64,256]{2,1,0:T(8,128)(2,1)S(1)}, bf16[2,64,256]{2,1,0:T(8,128)(2,1)S(1)}, u32[]{:S(2)}, u32[]{:S(2)}) collective-permute-start(bf16[2,64,256]{2,1,0:T(8,128)(2,1)S(1)} %dynamic-slice_bitcast_fusion.14), channel_id=1, source_target_pairs={{0,8},{1,9},{2,10},{3,11},{4,12},{5,13},{6,14},{7,15},{8,0},{9,1},... | collective-permute-start | bytes 196616 | tf_op jit(solution)/shard_map/ppermute | solution.py:29
  41.6 5.0 %collective-permute-start.3 = (bf16[64,256]{1,0:T(8,128)(2,1)S(1)}, bf16[64,256]{1,0:T(8,128)(2,1)S(1)}, u32[]{:S(2)}, u32[]{:S(2)}) collective-permute-start(bf16[64,256]{1,0:T(8,128)(2,1)S(1)} %dynamic-slice_bitcast_fusion.19), channel_id=1, source_target_pairs={{0,8},{1,9},{2,10},{3,11},{4,12},{5,13},{6,14},{7,15},{8,0},{9,1},... | collective-permute-start | bytes 98312 | tf_op jit(solution)/shard_map/ppermute | solution.py:29
  45.3 4.0 %collective-permute-start.7 = (bf16[64,256]{1,0:T(8,128)(2,1)S(1)}, bf16[64,256]{1,0:T(8,128)(2,1)S(1)}, u32[]{:S(2)}, u32[]{:S(2)}) collective-permute-start(bf16[64,256]{1,0:T(8,128)(2,1)S(1)} %dynamic-slice_bitcast_fusion.18), channel_id=1, source_target_pairs={{0,2},{1,3},{2,0},{3,1},{4,6},{5,7},{6,4},{7,5},{8,10},{9,11},{10,... | collective-permute-start | bytes 98312 | tf_op jit(solution)/shard_map/ppermute | solution.py:29
  49.3 6.7 %slice-start = ((s8[6291456]{0:T(1024)(128)(4,1)}), s8[4194304]{0:T(1024)(128)(4,1)S(1)}, s32[]{:S(2)}) async-start(s8[6291456]{0:T(1024)(128)(4,1)} %bitcast.198), calls=%async_computation.2 | async-start | bytes 8388608
  49.3 6.7 %slice-start.1 = ((s8[6291456]{0:T(1024)(128)(4,1)}), s8[2097152]{0:T(1024)(128)(4,1)S(1)}, s32[]{:S(2)}) async-start(s8[6291456]{0:T(1024)(128)(4,1)} %bitcast.198), calls=%async_computation.3 | async-start | bytes 4194304
  56.0 3.8 %collective-permute-start.12 = (bf16[2,2,2,128,768]{4,3,2,0,1:T(8,128)(2,1)}, bf16[2,2,2,128,768]{4,3,2,0,1:T(8,128)(2,1)}, u32[]{:S(2)}, u32[]{:S(2)}) collective-permute-start(bf16[2,2,2,128,768]{4,3,2,0,1:T(8,128)(2,1)} %bitcast.189), channel_id=1, source_target_pairs={{0,1},{1,0},{2,3},{3,2},{4,5},{5,4},{6,7},{7,6},{8,9},{9,8},{10,11... | collective-permute-start | bytes 4718600 | tf_op jit(solution)/shard_map/ppermute | solution.py:29
  58.2 5.2 %collective-permute-start.8 = (bf16[2,2,2,128,768]{4,3,2,1,0:T(8,128)(2,1)}, bf16[2,2,2,128,768]{4,3,2,1,0:T(8,128)(2,1)}, u32[]{:S(2)}, u32[]{:S(2)}) collective-permute-start(bf16[2,2,2,128,768]{4,3,2,1,0:T(8,128)(2,1)} %dynamic-slice_bitcast_fusion), channel_id=1, source_target_pairs={{0,1},{1,0},{2,3},{3,2},{4,5},{5,4},{6,7},{7,6},{8,9},{9,8},{10,11... | collective-permute-start | bytes 4718600 | tf_op jit(solution)/shard_map/ppermute | solution.py:29
  62.0 1.4 copy-start.2
  63.0 32.5 %collective-permute-start.13 = (bf16[2,2,128,768]{3,2,1,0:T(8,128)(2,1)}, bf16[2,2,128,768]{3,2,1,0:T(8,128)(2,1)}, u32[]{:S(2)}, u32[]{:S(2)}) collective-permute-start(bf16[2,2,128,768]{3,2,1,0:T(8,128)(2,1)} %dynamic-slice_bitcast_fusion.1), channel_id=1, source_target_pairs={{0,4},{1,5},{2,6},{3,7},{4,0},{5,1},{6,2},{7,3},{8,12},{9,13},{10,... | collective-permute-start | bytes 2359304 | tf_op jit(solution)/shard_map/ppermute | solution.py:29
  65.2 1.1 copy-start
  66.3 29.2 %copy-start.3 = (bf16[2,2,2,128,768]{4,3,2,0,1:T(8,128)(2,1)S(1)}, bf16[2,2,2,128,768]{4,3,2,0,1:T(8,128)(2,1)}, u32[]{:S(2)}) copy-start(bf16[2,2,2,128,768]{4,3,2,0,1:T(8,128)(2,1)} %copy-done.2) | copy-start | bytes 4718596
  67.3 30.1 %copy-start.1 = (bf16[2,2,2,128,768]{4,3,2,1,0:T(8,128)(2,1)S(1)}, bf16[2,2,2,128,768]{4,3,2,1,0:T(8,128)(2,1)}, u32[]{:S(2)}) copy-start(bf16[2,2,2,128,768]{4,3,2,1,0:T(8,128)(2,1)} %copy-done) | copy-start | bytes 4718596
  67.3 30.1 %collective-permute-start.9 = (bf16[2,2,128,768]{3,2,1,0:T(8,128)(2,1)}, bf16[2,2,128,768]{3,2,1,0:T(8,128)(2,1)}, u32[]{:S(2)}, u32[]{:S(2)}) collective-permute-start(bf16[2,2,128,768]{3,2,1,0:T(8,128)(2,1)} %dynamic-slice_bitcast_fusion.2), channel_id=1, source_target_pairs={{0,2},{1,3},{2,0},{3,1},{4,6},{5,7},{6,4},{7,5},{8,10},{9,11},{10,... | collective-permute-start | bytes 2359304 | tf_op jit(solution)/shard_map/ppermute | solution.py:29
  67.9 1.2 collective-permute-start.16
  69.1 18.1 %collective-permute-start.17 = (f32[128]{0:T(128)S(1)}, f32[128]{0:T(128)S(1)}, u32[]{:S(2)}, u32[]{:S(2)}) collective-permute-start(f32[128]{0:T(128)S(1)} %add.237), channel_id=1, source_target_pairs={{0,2},{1,3},{2,0},{3,1},{4,6},{5,7},{6,4},{7,5},{8,10},{9,11},{10,... | collective-permute-start | bytes 1544 | tf_op jit(solution)/shard_map/ppermute | solution.py:39
  87.2 5.7 %collective-permute-start.18 = (f32[128]{0:T(128)S(1)}, f32[128]{0:T(128)S(1)}, u32[]{:S(2)}, u32[]{:S(2)}) collective-permute-start(f32[128]{0:T(128)S(1)} %add.238), channel_id=1, source_target_pairs={{0,4},{1,5},{2,6},{3,7},{4,0},{5,1},{6,2},{7,3},{8,12},{9,13},{10,... | collective-permute-start | bytes 1544 | tf_op jit(solution)/shard_map/ppermute | solution.py:39
  89.2 40.4 %all-to-all-start.1 = ((bf16[16,8,256]{2,1,0:T(8,128)(2,1)}), bf16[16,8,256]{2,1,0:T(8,128)(2,1)S(1)}, u32[]{:S(2)}, u32[]{:S(2)}) async-start(bf16[16,8,256]{2,1,0:T(8,128)(2,1)} %fusion.66), calls=%async_computation.1 | async-start | bytes 131072 | tf_op jit(solution)/shard_map/all_to_all | solution.py:143
  92.9 7.5 %collective-permute-start.19 = (f32[128]{0:T(128)S(1)}, f32[128]{0:T(128)S(1)}, u32[]{:S(2)}, u32[]{:S(2)}) collective-permute-start(f32[128]{0:T(128)S(1)} %add.239), channel_id=1, source_target_pairs={{0,8},{1,9},{2,10},{3,11},{4,12},{5,13},{6,14},{7,15},{8,0},{9,1},... | collective-permute-start | bytes 1544 | tf_op jit(solution)/shard_map/ppermute | solution.py:39
  96.9 20.3 %collective-permute-start.14 = (bf16[2,128,768]{2,1,0:T(8,128)(2,1)S(1)}, bf16[2,128,768]{2,1,0:T(8,128)(2,1)S(1)}, u32[]{:S(2)}, u32[]{:S(2)}) collective-permute-start(bf16[2,128,768]{2,1,0:T(8,128)(2,1)S(1)} %dynamic-slice_bitcast_fusion.3), channel_id=1, source_target_pairs={{0,8},{1,9},{2,10},{3,11},{4,12},{5,13},{6,14},{7,15},{8,0},{9,1},... | collective-permute-start | bytes 1179656 | tf_op jit(solution)/shard_map/ppermute | solution.py:29
  98.7 20.2 %collective-permute-start.10 = (bf16[2,128,768]{2,1,0:T(8,128)(2,1)S(1)}, bf16[2,128,768]{2,1,0:T(8,128)(2,1)S(1)}, u32[]{:S(2)}, u32[]{:S(2)}) collective-permute-start(bf16[2,128,768]{2,1,0:T(8,128)(2,1)S(1)} %dynamic-slice_bitcast_fusion.4), channel_id=1, source_target_pairs={{0,4},{1,5},{2,6},{3,7},{4,0},{5,1},{6,2},{7,3},{8,12},{9,13},{10,... | collective-permute-start | bytes 1179656 | tf_op jit(solution)/shard_map/ppermute | solution.py:29
  117.4 6.0 %collective-permute-start.15 = (bf16[128,768]{1,0:T(8,128)(2,1)S(1)}, bf16[128,768]{1,0:T(8,128)(2,1)S(1)}, u32[]{:S(2)}, u32[]{:S(2)}) collective-permute-start(bf16[128,768]{1,0:T(8,128)(2,1)S(1)} %dynamic-slice_bitcast_fusion.6), channel_id=1, source_target_pairs={{0,2},{1,3},{2,0},{3,1},{4,6},{5,7},{6,4},{7,5},{8,10},{9,11},{10,... | collective-permute-start | bytes 589832 | tf_op jit(solution)/shard_map/ppermute | solution.py:29
  119.0 10.5 %collective-permute-start.11 = (bf16[128,768]{1,0:T(8,128)(2,1)S(1)}, bf16[128,768]{1,0:T(8,128)(2,1)S(1)}, u32[]{:S(2)}, u32[]{:S(2)}) collective-permute-start(bf16[128,768]{1,0:T(8,128)(2,1)S(1)} %dynamic-slice_bitcast_fusion.7), channel_id=1, source_target_pairs={{0,8},{1,9},{2,10},{3,11},{4,12},{5,13},{6,14},{7,15},{8,0},{9,1},... | collective-permute-start | bytes 589832 | tf_op jit(solution)/shard_map/ppermute | solution.py:29
  133.8 1.6 %collective-permute-start.20 = (bf16[2,2,2,8,2048]{4,3,0,1,2:T(8,128)(2,1)S(1)}, bf16[2,2,2,8,2048]{4,3,0,1,2:T(8,128)(2,1)S(1)}, u32[]{:S(2)}, u32[]{:S(2)}) collective-permute-start(bf16[2,2,2,8,2048]{4,3,0,1,2:T(8,128)(2,1)S(1)} %bitcast.212), channel_id=1, source_target_pairs={{0,1},{1,0},{2,3},{3,2},{4,5},{5,4},{6,7},{7,6},{8,9},{9,8},{10,11... | collective-permute-start | bytes 786440 | tf_op jit(solution)/shard_map/ppermute | solution.py:29
  134.5 1.8 %collective-permute-start.24 = (bf16[2,2,2,8,2048]{4,3,2,0,1:T(8,128)(2,1)S(1)}, bf16[2,2,2,8,2048]{4,3,2,0,1:T(8,128)(2,1)S(1)}, u32[]{:S(2)}, u32[]{:S(2)}) collective-permute-start(bf16[2,2,2,8,2048]{4,3,2,0,1:T(8,128)(2,1)S(1)} %bitcast.211), channel_id=1, source_target_pairs={{0,1},{1,0},{2,3},{3,2},{4,5},{5,4},{6,7},{7,6},{8,9},{9,8},{10,11... | collective-permute-start | bytes 786440 | tf_op jit(solution)/shard_map/ppermute | solution.py:29
  135.5 5.6 %collective-permute-start.21 = (bf16[2,2,8,2048]{3,2,0,1:T(8,128)(2,1)S(1)}, bf16[2,2,8,2048]{3,2,0,1:T(8,128)(2,1)S(1)}, u32[]{:S(2)}, u32[]{:S(2)}) collective-permute-start(bf16[2,2,8,2048]{3,2,0,1:T(8,128)(2,1)S(1)} %dynamic-slice_bitcast_fusion.9), channel_id=1, source_target_pairs={{0,2},{1,3},{2,0},{3,1},{4,6},{5,7},{6,4},{7,5},{8,10},{9,11},{10,... | collective-permute-start | bytes 393224 | tf_op jit(solution)/shard_map/ppermute | solution.py:29
  136.4 5.8 %collective-permute-start.25 = (bf16[2,2,8,2048]{3,2,1,0:T(8,128)(2,1)S(1)}, bf16[2,2,8,2048]{3,2,1,0:T(8,128)(2,1)S(1)}, u32[]{:S(2)}, u32[]{:S(2)}) collective-permute-start(bf16[2,2,8,2048]{3,2,1,0:T(8,128)(2,1)S(1)} %dynamic-slice_bitcast_fusion.8), channel_id=1, source_target_pairs={{0,4},{1,5},{2,6},{3,7},{4,0},{5,1},{6,2},{7,3},{8,12},{9,13},{10,... | collective-permute-start | bytes 393224 | tf_op jit(solution)/shard_map/ppermute | solution.py:29
  141.1 4.5 %collective-permute-start.22 = (bf16[2,8,2048]{2,1,0:T(8,128)(2,1)S(1)}, bf16[2,8,2048]{2,1,0:T(8,128)(2,1)S(1)}, u32[]{:S(2)}, u32[]{:S(2)}) collective-permute-start(bf16[2,8,2048]{2,1,0:T(8,128)(2,1)S(1)} %dynamic-slice_bitcast_fusion.13), channel_id=1, source_target_pairs={{0,4},{1,5},{2,6},{3,7},{4,0},{5,1},{6,2},{7,3},{8,12},{9,13},{10,... | collective-permute-start | bytes 196616 | tf_op jit(solution)/shard_map/ppermute | solution.py:29
  142.3 6.6 %collective-permute-start.26 = (bf16[2,8,2048]{2,1,0:T(8,128)(2,1)S(1)}, bf16[2,8,2048]{2,1,0:T(8,128)(2,1)S(1)}, u32[]{:S(2)}, u32[]{:S(2)}) collective-permute-start(bf16[2,8,2048]{2,1,0:T(8,128)(2,1)S(1)} %dynamic-slice_bitcast_fusion.12), channel_id=1, source_target_pairs={{0,8},{1,9},{2,10},{3,11},{4,12},{5,13},{6,14},{7,15},{8,0},{9,1},... | collective-permute-start | bytes 196616 | tf_op jit(solution)/shard_map/ppermute | solution.py:29
  145.7 5.0 %collective-permute-start.23 = (bf16[8,2048]{1,0:T(8,128)(2,1)S(1)}, bf16[8,2048]{1,0:T(8,128)(2,1)S(1)}, u32[]{:S(2)}, u32[]{:S(2)}) collective-permute-start(bf16[8,2048]{1,0:T(8,128)(2,1)S(1)} %dynamic-slice_bitcast_fusion.17), channel_id=1, source_target_pairs={{0,8},{1,9},{2,10},{3,11},{4,12},{5,13},{6,14},{7,15},{8,0},{9,1},... | collective-permute-start | bytes 98312 | tf_op jit(solution)/shard_map/ppermute | solution.py:29
  148.9 4.0 %collective-permute-start.27 = (bf16[8,2048]{1,0:T(8,128)(2,1)S(1)}, bf16[8,2048]{1,0:T(8,128)(2,1)S(1)}, u32[]{:S(2)}, u32[]{:S(2)}) collective-permute-start(bf16[8,2048]{1,0:T(8,128)(2,1)S(1)} %dynamic-slice_bitcast_fusion.16), channel_id=1, source_target_pairs={{0,2},{1,3},{2,0},{3,1},{4,6},{5,7},{6,4},{7,5},{8,10},{9,11},{10,... | collective-permute-start | bytes 98312 | tf_op jit(solution)/shard_map/ppermute | solution.py:29

commit v3 on v2

--- a/solution.py
+++ b/solution.py
@@ -146,23 +146,24 @@
 
     wide = columns.astype(F32)
     square = add_up(jnp.sum(wide * wide, axis=1))
-    scale = lax.rsqrt(square / width + 1e-6)[:, None]
     gain = lax.dynamic_slice_in_dim(norm_gain, (me * pair + half) * depth, depth)
     scaled = (wide * gain[None, :]).astype(BF16)
     all_rows = scaled.shape[0]
 
-    def project(chosen, weight, order):
+    def project(chosen, weight):
         sums = jnp.einsum("rd,edf->erf", chosen, weight, preferred_element_type=F32).astype(BF16)
-        sums = sums.reshape(experts, chosen.shape[0], pair, units // pair).swapaxes(1, 2)
-        return scatter_both(sums, order)
-
-    def both(chosen):
-        return project(chosen, gate_update, near_first), project(chosen, up_update, far_first)
+        return sums.reshape(experts, chosen.shape[0], pair, units // pair).swapaxes(1, 2)
+
+    def both(chosen, total):
+        gate, up = project(chosen, gate_update), project(chosen, up_update)
+        gate, up, total = lax.optimization_barrier((gate, up, total))
+        return scatter_both(gate, near_first), scatter_both(up, far_first), total
 
     if all_rows <= 128:
-        gate, up = both(scaled)
+        gate, up, square = both(scaled, square)
     else:
-        gate, up = lax.map(both, scaled.reshape(-1, 128, depth))
+        gate, up = lax.map(lambda chosen: both(chosen, square)[:2], scaled.reshape(-1, 128, depth))
+    scale = lax.rsqrt(square / width + 1e-6)[:, None]
     gate, up, back = lax.optimization_barrier((gate, up, back))
     stream = back.reshape(residual.shape)
     gate = gate.reshape(all_rows, -1).astype(F32) * scale

time: 154 us -> 150 us (0.974)
  waiting for transfers between devices: 82.2 us -> 67.7 us
  starting transfers between devices: 28.1 us -> 39.2 us
  matrix products: 13.6 us -> 16.2 us
    ppermute x4, waiting for transfers between devices: 17.4 us -> 1.87 us  [add_up(): x = x + lax.ppermute(x, 'expert', [(i, i ^ 1 << bit) for i in range(count)])]
    ppermute x24, starting transfers between devices: 11.4 us -> 23.1 us  [scatter_sum(): lax.ppermute(send, axis_name, [(i, i ^ 1 << bit) for i in range(count)])]
    dot_general x2, matrix products: 4.94 us -> 7.57 us  [project(): jnp.einsum('rd,edf->erf', chosen, weight, preferred_element_type=F32)]
    convert_element_type x24, other arithmetic: 7.52 us -> 5.98 us  [scatter_sum(): x = (keep.astype(F32) + got.astype(F32)).astype(BF16)]
  transfers between devices with their start and end apart: 30 -> 30, of which waited for: 21 -> 23; matrix products, arithmetic and copies ran while one was open for 10% -> 15% of each run, Pallas kernels for 0% -> 0%
where the time goes in v3:
time: 150 us
  waiting for transfers between devices  67.7 us (45%)
  starting transfers between devices  39.2 us (26%)
  matrix products  16.2 us (11%)
  local copies, waits for them, and re-layouts  16.1 us (11%)
  other arithmetic  9.22 us (6%)
    ppermute x24, waiting for transfers between devices, scatter_sum(): lax.ppermute(send, axis_name, [(i, i ^ 1 << bit) for i in range(count)])  58.4 us
    ppermute x24, starting transfers between devices, scatter_sum(): lax.ppermute(send, axis_name, [(i, i ^ 1 << bit) for i in range(count)])  23.1 us
    dot_general x2, matrix products, project(): jnp.einsum('rd,edf->erf', chosen, weight, preferred_element_type=F32)  7.57 us
    all_to_all x1, starting transfers between devices, shards(): lax.all_to_all(packed.reshape(own, -1), 'expert', split_axis=1, concat_ax...  7.39 us
    all_to_all x1, waiting for transfers between devices, shards(): lax.all_to_all(packed.reshape(own, -1), 'expert', split_axis=1, concat_ax...  7.38 us
    convert_element_type x24, other arithmetic, scatter_sum(): x = (keep.astype(F32) + got.astype(F32)).astype(BF16)  5.98 us
    ppermute x4, starting transfers between devices, add_up(): x = x + lax.ppermute(x, 'expert', [(i, i ^ 1 << bit) for i in range(count)])  4.99 us
    dot_general x1, matrix products, shards(): jnp.dot(hidden, down_weight[0], preferred_element_type=F32).astype(BF16)  3.92 us
  transfers between devices with their start and end apart: 30, of which 23 were waited for; matrix products, arithmetic and copies ran while one was open for 15% of the time, Pallas kernels for 0%

profile of v3, /device:TPU:0, one launch (start us, length us, event | category | flops | bytes accessed | tf_op | source)
XLA Modules:
  0.0 149.7 jit_solution(9750073789788439704)
XLA Ops:
  0.6 0.7 iota_compare_fusion.2
  1.4 0.8 select_reduce_fusion
  2.2 0.7 reshape_squeeze.29
  2.9 0.7 reshape_squeeze.31
  3.6 1.1 reshape_squeeze.27
  4.7 1.8 %reshape_squeeze.28 = bf16[4,192,4,128]{3,2,1,0:T(4,128)(2,1)S(1)} reshape(bf16[1,4,192,512]{3,2,1,0:T(8,128)(2,1)} %param.23) | data formatting | bytes 1572864 | tf_op jit(solution)/shard_map/reshape;squeeze | solution.py:64
  7.0 0.7 fusion.70
  9.2 0.7 copy.88
  9.9 7.4 %all-to-all-start = ((bf16[8,16,640]{2,0,1:T(8,128)(2,1)}), bf16[8,16,640]{2,0,1:T(8,128)(2,1)S(1)}, u32[]{:S(2)}, u32[]{:S(2)}) async-start(bf16[8,16,640]{2,0,1:T(8,128)(2,1)} %copy.88), calls=%async_computation | async-start | bytes 327680 | tf_op jit(solution)/shard_map/all_to_all | solution.py:121
  17.7 0.7 copy.116
  18.4 7.4 %all-to-all-done = bf16[8,16,640]{2,0,1:T(8,128)(2,1)S(1)} async-done(((bf16[8,16,640]{2,0,1:T(8,128)(2,1)}), bf16[8,16,640]{2,0,1:T(8,128)(2,1)S(1)}, u32[]{:S(2)}, u32[]{:S(2)}) %all-to-all-start) | async-done | bytes 163872 | tf_op jit(solution)/shard_map/all_to_all | solution.py:121
  25.7 2.9 %fusion.41 = f32[128,4096]{1,0:T(8,128)S(1)} fusion(bf16[512,4096]{1,0:T(8,128)(2,1)} %param.17, bf16[128,640]{1,0:T(8,128)(2,1)S(1)} %bitcast.210), kind=kOutput, calls=%fused_computation.81 | convolution fusion | flops 536870912 | bytes 6422528 | tf_op jit(solution)/shard_map/dot_general | solution.py:131
  28.6 0.7 copy.115
  30.7 0.7 collective-permute-done
  32.3 4.8 %collective-permute-done.1 = bf16[2,2,64,256]{3,2,1,0:T(8,128)(2,1)S(1)} collective-permute-done((bf16[2,2,64,256]{3,2,1,0:T(8,128)(2,1)S(1)}, bf16[2,2,64,256]{3,2,1,0:T(8,128)(2,1)S(1)}, u32[]{:S(2)}, u32[]{:S(2)}) %collective-permute-start.1) | collective-permute-done | bytes 131104 | tf_op jit(solution)/shard_map/ppermute | solution.py:29
  37.9 1.0 collective-permute-start.6
  38.9 3.2 %collective-permute-done.2 = bf16[2,64,256]{2,1,0:T(8,128)(2,1)S(1)} collective-permute-done((bf16[2,64,256]{2,1,0:T(8,128)(2,1)S(1)}, bf16[2,64,256]{2,1,0:T(8,128)(2,1)S(1)}, u32[]{:S(2)}, u32[]{:S(2)}) %collective-permute-start.2) | collective-permute-done | bytes 65568 | tf_op jit(solution)/shard_map/ppermute | solution.py:29
  42.4 0.8 collective-permute-done.6
  43.2 2.7 %collective-permute-start.7 = (bf16[64,256]{1,0:T(8,128)(2,1)S(1)}, bf16[64,256]{1,0:T(8,128)(2,1)S(1)}, u32[]{:S(2)}, u32[]{:S(2)}) collective-permute-start(bf16[64,256]{1,0:T(8,128)(2,1)S(1)} %dynamic-slice_bitcast_fusion.18), channel_id=1, source_target_pairs={{0,2},{1,3},{2,0},{3,1},{4,6},{5,7},{6,4},{7,5},{8,10},{9,11},{10,... | collective-permute-start | bytes 98312 | tf_op jit(solution)/shard_map/ppermute | solution.py:29
  45.9 1.1 collective-permute-done.3
  47.0 0.7 collective-permute-done.7
  48.0 1.1 collective-permute-done.8
  49.1 2.0 %collective-permute-start.9 = (f32[128]{0:T(128)S(1)}, f32[128]{0:T(128)S(1)}, u32[]{:S(2)}, u32[]{:S(2)}) collective-permute-start(f32[128]{0:T(128)S(1)} %add.229), channel_id=1, source_target_pairs={{0,2},{1,3},{2,0},{3,1},{4,6},{5,7},{6,4},{7,5},{8,10},{9,11},{10,... | collective-permute-start | bytes 1544 | tf_op jit(solution)/shard_map/ppermute | solution.py:39
  51.1 0.8 dynamic_slice.185
  51.8 0.8 collective-permute-done.9
  52.6 1.0 collective-permute-start.10
  53.6 3.8 %convert_bitcast_fusion = bf16[16,1,128,768]{3,2,0,1:T(8,128)(2,1)S(1)} fusion(bf16[16,256,768]{2,1,0:T(8,128)(2,1)} %param.15, f32[256]{0:T(256)S(1)} %dynamic_slice.185, bf16[64,256]{1,0:T(8,128)(2,1)S(1)} %fusion.53, bf16[64,256]{1,0:T(8,128)(2,1)S(1)} %fusion.54), kind=kOutput, calls=%fused_computation.8 | convolution fusion | flops 807075840 | bytes 9503744 | tf_op jit(solution)/shard_map/rd,edf->erf/dot_general | solution.py:154
  57.5 1.9 %collective-permute-start.11 = (f32[128]{0:T(128)S(1)}, f32[128]{0:T(128)S(1)}, u32[]{:S(2)}, u32[]{:S(2)}) collective-permute-start(f32[128]{0:T(128)S(1)} %add.231), channel_id=1, source_target_pairs={{0,8},{1,9},{2,10},{3,11},{4,12},{5,13},{6,14},{7,15},{8,0},{9,1},... | collective-permute-start | bytes 1544 | tf_op jit(solution)/shard_map/ppermute | solution.py:39
  59.3 3.8 %convert_bitcast_fusion.1 = bf16[16,1,128,768]{3,2,0,1:T(8,128)(2,1)S(1)} fusion(bf16[16,256,768]{2,1,0:T(8,128)(2,1)} %param.14, f32[256]{0:T(256)S(1)} %dynamic_slice.185, bf16[64,256]{1,0:T(8,128)(2,1)S(1)} %fusion.53, bf16[64,256]{1,0:T(8,128)(2,1)S(1)} %fusion.54), kind=kOutput, calls=%fused_computation.9 | convolution fusion | flops 807075840 | bytes 9503744 | tf_op jit(solution)/shard_map/rd,edf->erf/dot_general | solution.py:154
  63.1 1.3 dynamic-slice_bitcast_fusion
  64.4 1.4 constant_dynamic-slice_fusion.5
  65.8 1.3 copy.153
  67.6 0.6 collective-permute-done.12
  68.2 1.8 %fusion.9 = bf16[2,2,2,128,768]{4,3,2,1,0:T(8,128)(2,1)S(1)} fusion(bf16[2,2,2,128,768]{4,3,2,1,0:T(8,128)(2,1)} %collective-permute-done.12, bf16[2,2,2,2,128,768]{5,4,3,2,1,0:T(8,128)(2,1)S(1)} %bitcast.198, s32[]{:T(128)S(6)} %select_n.104), kind=kLoop, calls=%fused_computation.7 | loop fusion | flops 3145728 | bytes 4718596 | tf_op jit(solution)/shard_map/convert_element_type | solution.py:30
  70.0 1.1 dynamic-slice_bitcast_fusion.2
  71.0 0.6 collective-permute-start.13
  71.7 1.8 %fusion.8 = bf16[2,2,2,128,768]{4,3,2,0,1:T(8,128)(2,1)S(1)} fusion(bf16[2,2,2,128,768]{4,3,2,0,1:T(8,128)(2,1)} %collective-permute-done.16, bf16[2,2,2,1,128,768]{5,4,3,2,1,0:T(8,128)(2,1)S(1)} %copy-done.1), kind=kLoop, calls=%fused_computation.5 | loop fusion | flops 3145728 | bytes 4718592 | tf_op jit(solution)/shard_map/convert_element_type | solution.py:30
  73.5 1.0 dynamic-slice_bitcast_fusion.1
  74.5 1.2 collective-permute-start.17
  76.0 0.6 fusion.66
  76.6 3.7 %all-to-all-start.1 = ((bf16[16,8,256]{2,1,0:T(8,128)(2,1)}), bf16[16,8,256]{2,1,0:T(8,128)(2,1)S(1)}, u32[]{:S(2)}, u32[]{:S(2)}) async-start(bf16[16,8,256]{2,1,0:T(8,128)(2,1)} %fusion.66), calls=%async_computation.1 | async-start | bytes 131072 | tf_op jit(solution)/shard_map/all_to_all | solution.py:143
  80.3 10.8 %collective-permute-done.13 = bf16[2,2,128,768]{3,2,1,0:T(8,128)(2,1)S(1)} collective-permute-done((bf16[2,2,128,768]{3,2,1,0:T(8,128)(2,1)}, bf16[2,2,128,768]{3,2,1,0:T(8,128)(2,1)S(1)}, u32[]{:S(2)}, u32[]{:S(2)}) %collective-permute-start.13) | collective-permute-done | bytes 786464 | tf_op jit(solution)/shard_map/ppermute | solution.py:29
  91.1 1.3 fusion.13
  92.5 0.6 collective-permute-start.14
  93.1 1.6 %collective-permute-done.17 = bf16[2,2,128,768]{3,2,1,0:T(8,128)(2,1)S(1)} collective-permute-done((bf16[2,2,128,768]{3,2,1,0:T(8,128)(2,1)}, bf16[2,2,128,768]{3,2,1,0:T(8,128)(2,1)S(1)}, u32[]{:S(2)}, u32[]{:S(2)}) %collective-permute-start.17) | collective-permute-done | bytes 786464 | tf_op jit(solution)/shard_map/ppermute | solution.py:29
  95.0 2.2 %collective-permute-start.18 = (bf16[2,128,768]{2,1,0:T(8,128)(2,1)S(1)}, bf16[2,128,768]{2,1,0:T(8,128)(2,1)S(1)}, u32[]{:S(2)}, u32[]{:S(2)}) collective-permute-start(bf16[2,128,768]{2,1,0:T(8,128)(2,1)S(1)} %dynamic-slice_bitcast_fusion.3), channel_id=1, source_target_pairs={{0,8},{1,9},{2,10},{3,11},{4,12},{5,13},{6,14},{7,15},{8,0},{9,1},... | collective-permute-start | bytes 1179656 | tf_op jit(solution)/shard_map/ppermute | solution.py:29
  97.2 13.9 %collective-permute-done.14 = bf16[2,128,768]{2,1,0:T(8,128)(2,1)S(1)} collective-permute-done((bf16[2,128,768]{2,1,0:T(8,128)(2,1)S(1)}, bf16[2,128,768]{2,1,0:T(8,128)(2,1)S(1)}, u32[]{:S(2)}, u32[]{:S(2)}) %collective-permute-start.14) | collective-permute-done | bytes 393248 | tf_op jit(solution)/shard_map/ppermute | solution.py:29
  111.3 7.7 %collective-permute-done.18 = bf16[2,128,768]{2,1,0:T(8,128)(2,1)S(1)} collective-permute-done((bf16[2,128,768]{2,1,0:T(8,128)(2,1)S(1)}, bf16[2,128,768]{2,1,0:T(8,128)(2,1)S(1)}, u32[]{:S(2)}, u32[]{:S(2)}) %collective-permute-start.18) | collective-permute-done | bytes 393248 | tf_op jit(solution)/shard_map/ppermute | solution.py:29
  119.1 2.1 %collective-permute-start.19 = (bf16[128,768]{1,0:T(8,128)(2,1)S(1)}, bf16[128,768]{1,0:T(8,128)(2,1)S(1)}, u32[]{:S(2)}, u32[]{:S(2)}) collective-permute-start(bf16[128,768]{1,0:T(8,128)(2,1)S(1)} %dynamic-slice_bitcast_fusion.6), channel_id=1, source_target_pairs={{0,2},{1,3},{2,0},{3,1},{4,6},{5,7},{6,4},{7,5},{8,10},{9,11},{10,... | collective-permute-start | bytes 589832 | tf_op jit(solution)/shard_map/ppermute | solution.py:29
  121.2 1.2 collective-permute-done.15
  122.5 2.4 %collective-permute-done.19 = bf16[128,768]{1,0:T(8,128)(2,1)S(1)} collective-permute-done((bf16[128,768]{1,0:T(8,128)(2,1)S(1)}, bf16[128,768]{1,0:T(8,128)(2,1)S(1)}, u32[]{:S(2)}, u32[]{:S(2)}) %collective-permute-start.19) | collective-permute-done | bytes 196640 | tf_op jit(solution)/shard_map/ppermute | solution.py:29
  125.0 3.9 %fusion.5 = bf16[16,1,8,4096]{3,2,0,1:T(8,128)(2,1)S(1)} fusion(bf16[1,768,4096]{2,1,0:T(8,128)(2,1)} %param.16, bf16[128,768]{1,0:T(8,128)(2,1)S(1)} %fusion.28, bf16[128,768]{1,0:T(8,128)(2,1)S(1)} %fusion.29, f32[128]{0:T(128)S(1)} %fusion.50, f32[128]{0:T(128)S(1)} %add_rsqrt_fusion), kind=kOutput, calls=%fused_computation.3 | convolution fusion | flops 806912000 | bytes 7734272 | tf_op jit(solution)/shard_map/dot_general | solution.py:172
  129.2 0.7 reshape.146
  129.9 0.6 collective-permute-start.24
  130.8 2.1 %collective-permute-start.21 = (bf16[2,2,8,2048]{3,2,0,1:T(8,128)(2,1)S(1)}, bf16[2,2,8,2048]{3,2,0,1:T(8,128)(2,1)S(1)}, u32[]{:S(2)}, u32[]{:S(2)}) collective-permute-start(bf16[2,2,8,2048]{3,2,0,1:T(8,128)(2,1)S(1)} %dynamic-slice_bitcast_fusion.9), channel_id=1, source_target_pairs={{0,2},{1,3},{2,0},{3,1},{4,6},{5,7},{6,4},{7,5},{8,10},{9,11},{10,... | collective-permute-start | bytes 393224 | tf_op jit(solution)/shard_map/ppermute | solution.py:29
  133.3 3.3 %collective-permute-done.21 = bf16[2,2,8,2048]{3,2,0,1:T(8,128)(2,1)S(1)} collective-permute-done((bf16[2,2,8,2048]{3,2,0,1:T(8,128)(2,1)S(1)}, bf16[2,2,8,2048]{3,2,0,1:T(8,128)(2,1)S(1)}, u32[]{:S(2)}, u32[]{:S(2)}) %collective-permute-start.21) | collective-permute-done | bytes 131104 | tf_op jit(solution)/shard_map/ppermute | solution.py:29
  136.7 1.0 collective-permute-start.22
  137.8 0.5 collective-permute-done.25
  138.4 2.9 %collective-permute-start.26 = (bf16[2,8,2048]{2,1,0:T(8,128)(2,1)S(1)}, bf16[2,8,2048]{2,1,0:T(8,128)(2,1)S(1)}, u32[]{:S(2)}, u32[]{:S(2)}) collective-permute-start(bf16[2,8,2048]{2,1,0:T(8,128)(2,1)S(1)} %dynamic-slice_bitcast_fusion.12), channel_id=1, source_target_pairs={{0,8},{1,9},{2,10},{3,11},{4,12},{5,13},{6,14},{7,15},{8,0},{9,1},... | collective-permute-start | bytes 196616 | tf_op jit(solution)/shard_map/ppermute | solution.py:29
  141.3 2.5 %collective-permute-start.23 = (bf16[8,2048]{1,0:T(8,128)(2,1)S(1)}, bf16[8,2048]{1,0:T(8,128)(2,1)S(1)}, u32[]{:S(2)}, u32[]{:S(2)}) collective-permute-start(bf16[8,2048]{1,0:T(8,128)(2,1)S(1)} %dynamic-slice_bitcast_fusion.17), channel_id=1, source_target_pairs={{0,8},{1,9},{2,10},{3,11},{4,12},{5,13},{6,14},{7,15},{8,0},{9,1},... | collective-permute-start | bytes 98312 | tf_op jit(solution)/shard_map/ppermute | solution.py:29
  143.8 1.2 collective-permute-done.26
  145.1 1.2 collective-permute-start.27
  146.2 2.8 %collective-permute-done.27 = bf16[8,2048]{1,0:T(8,128)(2,1)S(1)} collective-permute-done((bf16[8,2048]{1,0:T(8,128)(2,1)S(1)}, bf16[8,2048]{1,0:T(8,128)(2,1)S(1)}, u32[]{:S(2)}, u32[]{:S(2)}) %collective-permute-start.27) | collective-permute-done | bytes 32800 | tf_op jit(solution)/shard_map/ppermute | solution.py:29
  149.1 0.7 reshape.147
  (108 shorter events, 8.5 us)
Async XLA Ops:
  4.7 3.4 %copy-start.2 = (bf16[1,4,192,512]{3,2,1,0:T(8,128)(2,1)S(1)}, bf16[1,4,192,512]{3,2,1,0:T(8,128)(2,1)}, u32[]{:S(2)}) copy-start(bf16[1,4,192,512]{3,2,1,0:T(8,128)(2,1)} %param.24) | copy-start | bytes 2359300
  8.3 9.2 %copy-start.3 = (bf16[2,1,4,4096]{3,2,1,0:T(4,128)(2,1)S(1)}, bf16[2,1,4,4096]{3,2,1,0:T(4,128)(2,1)}, u32[]{:S(2)}) copy-start(bf16[2,1,4,4096]{3,2,1,0:T(4,128)(2,1)} %param.19) | copy-start | bytes 196612
  9.9 15.9 %all-to-all-start = ((bf16[8,16,640]{2,0,1:T(8,128)(2,1)}), bf16[8,16,640]{2,0,1:T(8,128)(2,1)S(1)}, u32[]{:S(2)}, u32[]{:S(2)}) async-start(bf16[8,16,640]{2,0,1:T(8,128)(2,1)} %copy.88), calls=%async_computation | async-start | bytes 327680 | tf_op jit(solution)/shard_map/all_to_all | solution.py:121
  29.9 1.6 %collective-permute-start = (bf16[2,2,2,64,256]{4,3,2,1,0:T(8,128)(2,1)S(1)}, bf16[2,2,2,64,256]{4,3,2,1,0:T(8,128)(2,1)S(1)}, u32[]{:S(2)}, u32[]{:S(2)}) collective-permute-start(bf16[2,2,2,64,256]{4,3,2,1,0:T(8,128)(2,1)S(1)} %dynamic-slice_bitcast_fusion.5), channel_id=1, source_target_pairs={{0,1},{1,0},{2,3},{3,2},{4,5},{5,4},{6,7},{7,6},{8,9},{9,8},{10,11... | collective-permute-start | bytes 786440 | tf_op jit(solution)/shard_map/ppermute | solution.py:29
  30.2 1.7 %collective-permute-start.4 = (bf16[2,2,2,64,256]{4,3,2,0,1:T(8,128)(2,1)S(1)}, bf16[2,2,2,64,256]{4,3,2,0,1:T(8,128)(2,1)S(1)}, u32[]{:S(2)}, u32[]{:S(2)}) collective-permute-start(bf16[2,2,2,64,256]{4,3,2,0,1:T(8,128)(2,1)S(1)} %bitcast.212), channel_id=1, source_target_pairs={{0,1},{1,0},{2,3},{3,2},{4,5},{5,4},{6,7},{7,6},{8,9},{9,8},{10,11... | collective-permute-start | bytes 786440 | tf_op jit(solution)/shard_map/ppermute | solution.py:29
  31.6 5.6 %collective-permute-start.1 = (bf16[2,2,64,256]{3,2,1,0:T(8,128)(2,1)S(1)}, bf16[2,2,64,256]{3,2,1,0:T(8,128)(2,1)S(1)}, u32[]{:S(2)}, u32[]{:S(2)}) collective-permute-start(bf16[2,2,64,256]{3,2,1,0:T(8,128)(2,1)S(1)} %dynamic-slice_bitcast_fusion.11), channel_id=1, source_target_pairs={{0,2},{1,3},{2,0},{3,1},{4,6},{5,7},{6,4},{7,5},{8,10},{9,11},{10,... | collective-permute-start | bytes 393224 | tf_op jit(solution)/shard_map/ppermute | solution.py:29
  32.0 5.8 %collective-permute-start.5 = (bf16[2,2,64,256]{3,2,1,0:T(8,128)(2,1)S(1)}, bf16[2,2,64,256]{3,2,1,0:T(8,128)(2,1)S(1)}, u32[]{:S(2)}, u32[]{:S(2)}) collective-permute-start(bf16[2,2,64,256]{3,2,1,0:T(8,128)(2,1)S(1)} %dynamic-slice_bitcast_fusion.10), channel_id=1, source_target_pairs={{0,4},{1,5},{2,6},{3,7},{4,0},{5,1},{6,2},{7,3},{8,12},{9,13},{10,... | collective-permute-start | bytes 393224 | tf_op jit(solution)/shard_map/ppermute | solution.py:29
  37.2 4.8 %collective-permute-start.2 = (bf16[2,64,256]{2,1,0:T(8,128)(2,1)S(1)}, bf16[2,64,256]{2,1,0:T(8,128)(2,1)S(1)}, u32[]{:S(2)}, u32[]{:S(2)}) collective-permute-start(bf16[2,64,256]{2,1,0:T(8,128)(2,1)S(1)} %dynamic-slice_bitcast_fusion.15), channel_id=1, source_target_pairs={{0,4},{1,5},{2,6},{3,7},{4,0},{5,1},{6,2},{7,3},{8,12},{9,13},{10,... | collective-permute-start | bytes 196616 | tf_op jit(solution)/shard_map/ppermute | solution.py:29
  37.9 5.2 %collective-permute-start.6 = (bf16[2,64,256]{2,1,0:T(8,128)(2,1)S(1)}, bf16[2,64,256]{2,1,0:T(8,128)(2,1)S(1)}, u32[]{:S(2)}, u32[]{:S(2)}) collective-permute-start(bf16[2,64,256]{2,1,0:T(8,128)(2,1)S(1)} %dynamic-slice_bitcast_fusion.14), channel_id=1, source_target_pairs={{0,8},{1,9},{2,10},{3,11},{4,12},{5,13},{6,14},{7,15},{8,0},{9,1},... | collective-permute-start | bytes 196616 | tf_op jit(solution)/shard_map/ppermute | solution.py:29
  42.1 4.9 %collective-permute-start.3 = (bf16[64,256]{1,0:T(8,128)(2,1)S(1)}, bf16[64,256]{1,0:T(8,128)(2,1)S(1)}, u32[]{:S(2)}, u32[]{:S(2)}) collective-permute-start(bf16[64,256]{1,0:T(8,128)(2,1)S(1)} %dynamic-slice_bitcast_fusion.19), channel_id=1, source_target_pairs={{0,8},{1,9},{2,10},{3,11},{4,12},{5,13},{6,14},{7,15},{8,0},{9,1},... | collective-permute-start | bytes 98312 | tf_op jit(solution)/shard_map/ppermute | solution.py:29
  43.2 4.6 %collective-permute-start.7 = (bf16[64,256]{1,0:T(8,128)(2,1)S(1)}, bf16[64,256]{1,0:T(8,128)(2,1)S(1)}, u32[]{:S(2)}, u32[]{:S(2)}) collective-permute-start(bf16[64,256]{1,0:T(8,128)(2,1)S(1)} %dynamic-slice_bitcast_fusion.18), channel_id=1, source_target_pairs={{0,2},{1,3},{2,0},{3,1},{4,6},{5,7},{6,4},{7,5},{8,10},{9,11},{10,... | collective-permute-start | bytes 98312 | tf_op jit(solution)/shard_map/ppermute | solution.py:29
  47.9 1.2 collective-permute-start.8
  49.1 3.5 %collective-permute-start.9 = (f32[128]{0:T(128)S(1)}, f32[128]{0:T(128)S(1)}, u32[]{:S(2)}, u32[]{:S(2)}) collective-permute-start(f32[128]{0:T(128)S(1)} %add.229), channel_id=1, source_target_pairs={{0,2},{1,3},{2,0},{3,1},{4,6},{5,7},{6,4},{7,5},{8,10},{9,11},{10,... | collective-permute-start | bytes 1544 | tf_op jit(solution)/shard_map/ppermute | solution.py:39
  52.6 4.8 %collective-permute-start.10 = (f32[128]{0:T(128)S(1)}, f32[128]{0:T(128)S(1)}, u32[]{:S(2)}, u32[]{:S(2)}) collective-permute-start(f32[128]{0:T(128)S(1)} %add.230), channel_id=1, source_target_pairs={{0,4},{1,5},{2,6},{3,7},{4,0},{5,1},{6,2},{7,3},{8,12},{9,13},{10,... | collective-permute-start | bytes 1544 | tf_op jit(solution)/shard_map/ppermute | solution.py:39
  57.5 5.7 %collective-permute-start.11 = (f32[128]{0:T(128)S(1)}, f32[128]{0:T(128)S(1)}, u32[]{:S(2)}, u32[]{:S(2)}) collective-permute-start(f32[128]{0:T(128)S(1)} %add.231), channel_id=1, source_target_pairs={{0,8},{1,9},{2,10},{3,11},{4,12},{5,13},{6,14},{7,15},{8,0},{9,1},... | collective-permute-start | bytes 1544 | tf_op jit(solution)/shard_map/ppermute | solution.py:39
  64.4 3.8 %collective-permute-start.12 = (bf16[2,2,2,128,768]{4,3,2,1,0:T(8,128)(2,1)}, bf16[2,2,2,128,768]{4,3,2,1,0:T(8,128)(2,1)}, u32[]{:S(2)}, u32[]{:S(2)}) collective-permute-start(bf16[2,2,2,128,768]{4,3,2,1,0:T(8,128)(2,1)} %dynamic-slice_bitcast_fusion), channel_id=1, source_target_pairs={{0,1},{1,0},{2,3},{3,2},{4,5},{5,4},{6,7},{7,6},{8,9},{9,8},{10,11... | collective-permute-start | bytes 4718600 | tf_op jit(solution)/shard_map/ppermute | solution.py:29
  67.1 4.6 %collective-permute-start.16 = (bf16[2,2,2,128,768]{4,3,2,0,1:T(8,128)(2,1)}, bf16[2,2,2,128,768]{4,3,2,0,1:T(8,128)(2,1)}, u32[]{:S(2)}, u32[]{:S(2)}) collective-permute-start(bf16[2,2,2,128,768]{4,3,2,0,1:T(8,128)(2,1)} %bitcast.193), channel_id=1, source_target_pairs={{0,1},{1,0},{2,3},{3,2},{4,5},{5,4},{6,7},{7,6},{8,9},{9,8},{10,11... | collective-permute-start | bytes 4718600 | tf_op jit(solution)/shard_map/ppermute | solution.py:29
  67.6 4.0 %copy-start.1 = (bf16[2,2,2,1,128,768]{5,4,3,2,1,0:T(8,128)(2,1)S(1)}, bf16[2,2,2,1,128,768]{5,4,3,2,1,0:T(8,128)(2,1)}, u32[]{:S(2)}) copy-start(bf16[2,2,2,1,128,768]{5,4,3,2,1,0:T(8,128)(2,1)} %get-tuple-element.16) | copy-start | bytes 4718596
  70.0 3.5 %copy-start = (bf16[2,2,2,128,768]{4,3,2,1,0:T(8,128)(2,1)}, bf16[2,2,2,128,768]{4,3,2,1,0:T(8,128)(2,1)S(1)}, u32[]{:S(2)}) copy-start(bf16[2,2,2,128,768]{4,3,2,1,0:T(8,128)(2,1)S(1)} %fusion.9) | copy-start | bytes 4718596
  71.0 20.1 %collective-permute-start.13 = (bf16[2,2,128,768]{3,2,1,0:T(8,128)(2,1)}, bf16[2,2,128,768]{3,2,1,0:T(8,128)(2,1)S(1)}, u32[]{:S(2)}, u32[]{:S(2)}) collective-permute-start(bf16[2,2,128,768]{3,2,1,0:T(8,128)(2,1)} %dynamic-slice_bitcast_fusion.2), channel_id=1, source_target_pairs={{0,2},{1,3},{2,0},{3,1},{4,6},{5,7},{6,4},{7,5},{8,10},{9,11},{10,... | collective-permute-start | bytes 2359304 | tf_op jit(solution)/shard_map/ppermute | solution.py:29
  74.5 20.2 %collective-permute-start.17 = (bf16[2,2,128,768]{3,2,1,0:T(8,128)(2,1)}, bf16[2,2,128,768]{3,2,1,0:T(8,128)(2,1)S(1)}, u32[]{:S(2)}, u32[]{:S(2)}) collective-permute-start(bf16[2,2,128,768]{3,2,1,0:T(8,128)(2,1)} %dynamic-slice_bitcast_fusion.1), channel_id=1, source_target_pairs={{0,4},{1,5},{2,6},{3,7},{4,0},{5,1},{6,2},{7,3},{8,12},{9,13},{10,... | collective-permute-start | bytes 2359304 | tf_op jit(solution)/shard_map/ppermute | solution.py:29
  76.6 48.4 %all-to-all-start.1 = ((bf16[16,8,256]{2,1,0:T(8,128)(2,1)}), bf16[16,8,256]{2,1,0:T(8,128)(2,1)S(1)}, u32[]{:S(2)}, u32[]{:S(2)}) async-start(bf16[16,8,256]{2,1,0:T(8,128)(2,1)} %fusion.66), calls=%async_computation.1 | async-start | bytes 131072 | tf_op jit(solution)/shard_map/all_to_all | solution.py:143
  92.5 18.6 %collective-permute-start.14 = (bf16[2,128,768]{2,1,0:T(8,128)(2,1)S(1)}, bf16[2,128,768]{2,1,0:T(8,128)(2,1)S(1)}, u32[]{:S(2)}, u32[]{:S(2)}) collective-permute-start(bf16[2,128,768]{2,1,0:T(8,128)(2,1)S(1)} %dynamic-slice_bitcast_fusion.4), channel_id=1, source_target_pairs={{0,4},{1,5},{2,6},{3,7},{4,0},{5,1},{6,2},{7,3},{8,12},{9,13},{10,... | collective-permute-start | bytes 1179656 | tf_op jit(solution)/shard_map/ppermute | solution.py:29
  95.0 24.0 %collective-permute-start.18 = (bf16[2,128,768]{2,1,0:T(8,128)(2,1)S(1)}, bf16[2,128,768]{2,1,0:T(8,128)(2,1)S(1)}, u32[]{:S(2)}, u32[]{:S(2)}) collective-permute-start(bf16[2,128,768]{2,1,0:T(8,128)(2,1)S(1)} %dynamic-slice_bitcast_fusion.3), channel_id=1, source_target_pairs={{0,8},{1,9},{2,10},{3,11},{4,12},{5,13},{6,14},{7,15},{8,0},{9,1},... | collective-permute-start | bytes 1179656 | tf_op jit(solution)/shard_map/ppermute | solution.py:29
  111.2 11.2 %collective-permute-start.15 = (bf16[128,768]{1,0:T(8,128)(2,1)S(1)}, bf16[128,768]{1,0:T(8,128)(2,1)S(1)}, u32[]{:S(2)}, u32[]{:S(2)}) collective-permute-start(bf16[128,768]{1,0:T(8,128)(2,1)S(1)} %dynamic-slice_bitcast_fusion.7), channel_id=1, source_target_pairs={{0,8},{1,9},{2,10},{3,11},{4,12},{5,13},{6,14},{7,15},{8,0},{9,1},... | collective-permute-start | bytes 589832 | tf_op jit(solution)/shard_map/ppermute | solution.py:29
  119.1 5.8 %collective-permute-start.19 = (bf16[128,768]{1,0:T(8,128)(2,1)S(1)}, bf16[128,768]{1,0:T(8,128)(2,1)S(1)}, u32[]{:S(2)}, u32[]{:S(2)}) collective-permute-start(bf16[128,768]{1,0:T(8,128)(2,1)S(1)} %dynamic-slice_bitcast_fusion.6), channel_id=1, source_target_pairs={{0,2},{1,3},{2,0},{3,1},{4,6},{5,7},{6,4},{7,5},{8,10},{9,11},{10,... | collective-permute-start | bytes 589832 | tf_op jit(solution)/shard_map/ppermute | solution.py:29
  129.1 1.6 %collective-permute-start.20 = (bf16[2,2,2,8,2048]{4,3,0,1,2:T(8,128)(2,1)S(1)}, bf16[2,2,2,8,2048]{4,3,0,1,2:T(8,128)(2,1)S(1)}, u32[]{:S(2)}, u32[]{:S(2)}) collective-permute-start(bf16[2,2,2,8,2048]{4,3,0,1,2:T(8,128)(2,1)S(1)} %bitcast.214), channel_id=1, source_target_pairs={{0,1},{1,0},{2,3},{3,2},{4,5},{5,4},{6,7},{7,6},{8,9},{9,8},{10,11... | collective-permute-start | bytes 786440 | tf_op jit(solution)/shard_map/ppermute | solution.py:29
  129.9 3.0 %collective-permute-start.24 = (bf16[2,2,2,8,2048]{4,3,2,0,1:T(8,128)(2,1)S(1)}, bf16[2,2,2,8,2048]{4,3,2,0,1:T(8,128)(2,1)S(1)}, u32[]{:S(2)}, u32[]{:S(2)}) collective-permute-start(bf16[2,2,2,8,2048]{4,3,2,0,1:T(8,128)(2,1)S(1)} %bitcast.213), channel_id=1, source_target_pairs={{0,1},{1,0},{2,3},{3,2},{4,5},{5,4},{6,7},{7,6},{8,9},{9,8},{10,11... | collective-permute-start | bytes 786440 | tf_op jit(solution)/shard_map/ppermute | solution.py:29
  130.8 5.9 %collective-permute-start.21 = (bf16[2,2,8,2048]{3,2,0,1:T(8,128)(2,1)S(1)}, bf16[2,2,8,2048]{3,2,0,1:T(8,128)(2,1)S(1)}, u32[]{:S(2)}, u32[]{:S(2)}) collective-permute-start(bf16[2,2,8,2048]{3,2,0,1:T(8,128)(2,1)S(1)} %dynamic-slice_bitcast_fusion.9), channel_id=1, source_target_pairs={{0,2},{1,3},{2,0},{3,1},{4,6},{5,7},{6,4},{7,5},{8,10},{9,11},{10,... | collective-permute-start | bytes 393224 | tf_op jit(solution)/shard_map/ppermute | solution.py:29
  133.0 5.3 %collective-permute-start.25 = (bf16[2,2,8,2048]{3,2,1,0:T(8,128)(2,1)S(1)}, bf16[2,2,8,2048]{3,2,1,0:T(8,128)(2,1)S(1)}, u32[]{:S(2)}, u32[]{:S(2)}) collective-permute-start(bf16[2,2,8,2048]{3,2,1,0:T(8,128)(2,1)S(1)} %dynamic-slice_bitcast_fusion.8), channel_id=1, source_target_pairs={{0,4},{1,5},{2,6},{3,7},{4,0},{5,1},{6,2},{7,3},{8,12},{9,13},{10,... | collective-permute-start | bytes 393224 | tf_op jit(solution)/shard_map/ppermute | solution.py:29
  136.7 4.5 %collective-permute-start.22 = (bf16[2,8,2048]{2,1,0:T(8,128)(2,1)S(1)}, bf16[2,8,2048]{2,1,0:T(8,128)(2,1)S(1)}, u32[]{:S(2)}, u32[]{:S(2)}) collective-permute-start(bf16[2,8,2048]{2,1,0:T(8,128)(2,1)S(1)} %dynamic-slice_bitcast_fusion.13), channel_id=1, source_target_pairs={{0,4},{1,5},{2,6},{3,7},{4,0},{5,1},{6,2},{7,3},{8,12},{9,13},{10,... | collective-permute-start | bytes 196616 | tf_op jit(solution)/shard_map/ppermute | solution.py:29
  138.4 6.6 %collective-permute-start.26 = (bf16[2,8,2048]{2,1,0:T(8,128)(2,1)S(1)}, bf16[2,8,2048]{2,1,0:T(8,128)(2,1)S(1)}, u32[]{:S(2)}, u32[]{:S(2)}) collective-permute-start(bf16[2,8,2048]{2,1,0:T(8,128)(2,1)S(1)} %dynamic-slice_bitcast_fusion.12), channel_id=1, source_target_pairs={{0,8},{1,9},{2,10},{3,11},{4,12},{5,13},{6,14},{7,15},{8,0},{9,1},... | collective-permute-start | bytes 196616 | tf_op jit(solution)/shard_map/ppermute | solution.py:29
  141.3 4.9 %collective-permute-start.23 = (bf16[8,2048]{1,0:T(8,128)(2,1)S(1)}, bf16[8,2048]{1,0:T(8,128)(2,1)S(1)}, u32[]{:S(2)}, u32[]{:S(2)}) collective-permute-start(bf16[8,2048]{1,0:T(8,128)(2,1)S(1)} %dynamic-slice_bitcast_fusion.17), channel_id=1, source_target_pairs={{0,8},{1,9},{2,10},{3,11},{4,12},{5,13},{6,14},{7,15},{8,0},{9,1},... | collective-permute-start | bytes 98312 | tf_op jit(solution)/shard_map/ppermute | solution.py:29
  145.1 4.0 %collective-permute-start.27 = (bf16[8,2048]{1,0:T(8,128)(2,1)S(1)}, bf16[8,2048]{1,0:T(8,128)(2,1)S(1)}, u32[]{:S(2)}, u32[]{:S(2)}) collective-permute-start(bf16[8,2048]{1,0:T(8,128)(2,1)S(1)} %dynamic-slice_bitcast_fusion.16), channel_id=1, source_target_pairs={{0,2},{1,3},{2,0},{3,1},{4,6},{5,7},{6,4},{7,5},{8,10},{9,11},{10,... | collective-permute-start | bytes 98312 | tf_op jit(solution)/shard_map/ppermute | solution.py:29

commit v4 on v3

--- a/solution.py
+++ b/solution.py
@@ -124,7 +124,6 @@
     heads = out_proj.shape[0]
     coefs = spread[:, heads:].astype(F32)
     coefs = coefs[:, :experts] + coefs[:, experts : 2 * experts]
-    coefs = lax.dynamic_index_in_dim(coefs, me, 1, keepdims=False)
     if pair > 1:
         coefs = lax.all_gather(coefs, "dp", axis=0, tiled=True)
     spread = spread[:, :heads]
@@ -150,25 +149,47 @@
     scaled = (wide * gain[None, :]).astype(BF16)
     all_rows = scaled.shape[0]
 
+    cap = min(rows, max(2, 3 * rows * top // (2 * experts)))
+    present = (coefs > 0).astype(jnp.int32).reshape(-1, rows, experts)
+    rank = jnp.cumsum(present, axis=1) - present
+    blocks = present.shape[0]
+    slot = jnp.where(present > 0, jnp.arange(blocks)[:, None, None] * cap + rank, -1)
+    slot = slot.reshape(all_rows, experts).T
+    slots = blocks * cap
+    select = slot[:, None, :] == jnp.arange(slots)[None, :, None]
+    chosen = jnp.einsum("esr,rd->esd", select.astype(BF16), scaled, preferred_element_type=F32)
+    chosen = chosen.astype(BF16)
+
     def project(chosen, weight):
-        sums = jnp.einsum("rd,edf->erf", chosen, weight, preferred_element_type=F32).astype(BF16)
-        return sums.reshape(experts, chosen.shape[0], pair, units // pair).swapaxes(1, 2)
+        sums = jnp.einsum("esd,edf->esf", chosen, weight, preferred_element_type=F32).astype(BF16)
+        return sums.reshape(experts, chosen.shape[1], pair, units // pair).swapaxes(1, 2)
 
     def both(chosen, total):
         gate, up = project(chosen, gate_update), project(chosen, up_update)
         gate, up, total = lax.optimization_barrier((gate, up, total))
-        return scatter_both(gate, near_first), scatter_both(up, far_first), total
-
-    if all_rows <= 128:
-        gate, up, square = both(scaled, square)
+        cut = chosen.shape[1] // 2
+        gate = scatter_both(gate, near_first)
+        first = scatter_both(up[:, :, :cut], near_first)
+        second = scatter_both(up[:, :, cut:], far_first)
+        return gate, jnp.concatenate([first, second], axis=0), total
+
+    if slots <= 128:
+        gate, up, square = both(chosen, square)
     else:
-        gate, up = lax.map(lambda chosen: both(chosen, square)[:2], scaled.reshape(-1, 128, depth))
-    scale = lax.rsqrt(square / width + 1e-6)[:, None]
+        parts = chosen.reshape(experts, -1, 128, depth).swapaxes(0, 1)
+        gate, up = lax.map(lambda part: both(part, square)[:2], parts)
+    scale = lax.rsqrt(square / width + 1e-6)
     gate, up, back = lax.optimization_barrier((gate, up, back))
     stream = back.reshape(residual.shape)
-    gate = gate.reshape(all_rows, -1).astype(F32) * scale
-    up = up.reshape(all_rows, -1).astype(F32) * scale
-    hidden = (jax.nn.silu(gate) * up * coefs[:, None]).astype(BF16)
+    mine = lax.dynamic_index_in_dim(select, me, 0, keepdims=False)
+    weight = lax.dynamic_index_in_dim(coefs, me, 1, keepdims=False)
+    scale = jnp.sum(jnp.where(mine, scale[None, :], 0.0), axis=1, keepdims=True)
+    weight = jnp.sum(jnp.where(mine, weight[None, :], 0.0), axis=1, keepdims=True)
+    gate = gate.reshape(slots, -1).astype(F32) * scale
+    up = up.reshape(slots, -1).astype(F32) * scale
+    hidden = (jax.nn.silu(gate) * up * weight).astype(BF16)
+    hidden = jnp.einsum("sr,sf->rf", mine.astype(BF16), hidden, preferred_element_type=F32)
+    hidden = hidden.astype(BF16)
     out = jnp.dot(hidden, down_weight[0], preferred_element_type=F32).astype(BF16)
     out = out.reshape(pair, ring, own, width).swapaxes(0, 1)
     middle = width // 2

time: 150 us -> 136 us (0.907)
  waiting for transfers between devices: 67.7 us -> 57.8 us
  starting transfers between devices: 39.2 us -> 45.1 us
  local copies, waits for them, and re-layouts: 16.1 us -> 10.4 us
  other arithmetic: 9.22 us -> 4.73 us
    ppermute x24 -> x28, waiting for transfers between devices: 58.4 us -> 49.9 us  [scatter_sum(): lax.ppermute(send, axis_name, [(i, i ^ 1 << bit) for i in range(count)])]
    ppermute x24 -> x28, starting transfers between devices: 23.1 us -> 30.6 us  [scatter_sum(): lax.ppermute(send, axis_name, [(i, i ^ 1 << bit) for i in range(count)])]
    convert_element_type x24 -> x28, other arithmetic: 5.98 us -> 1.7 us  [scatter_sum(): x = (keep.astype(F32) + got.astype(F32)).astype(BF16)]
    squeeze x20 -> x23, local copies, waits for them, and re-layouts: 3.62 us -> 0.48 us  [scatter_sum(): send = lax.dynamic_index_in_dim(x, 1 - mine, at, keepdims=False)]
    ppermute x4, starting transfers between devices: 4.99 us -> 3.02 us  [add_up(): x = x + lax.ppermute(x, 'expert', [(i, i ^ 1 << bit) for i in range(count)])]
    slice x1, local copies, waits for them, and re-layouts: 0.08 us -> 1.79 us  [both(): first = scatter_both(up[:, :, :cut], near_first)]
    another operation x1, local copies, waits for them, and re-layouts: 1.82 us -> 0.18 us  [attend(): kc = key_rows[0].reshape(rows, slots, KEY_VALUE_HEADS, HEAD_SIZE)]
    another operation x1, local copies, waits for them, and re-layouts: 0.18 us -> 1.75 us  [attend(): vc = value_rows[0].reshape(rows, slots, KEY_VALUE_HEADS, HEAD_SIZE)]
  transfers between devices with their start and end apart: 30 -> 34, of which waited for: 23 -> 23; matrix products, arithmetic and copies ran while one was open for 15% -> 11% of each run, Pallas kernels for 0% -> 0%
where the time goes in v4:
time: 136 us; the launch traced here: 135 us
  waiting for transfers between devices  57.8 us (42%)
  starting transfers between devices  45.1 us (33%)
  matrix products  15.5 us (11%)
  local copies, waits for them, and re-layouts  10.4 us (8%)
  other arithmetic  4.73 us (3%)
  between operations  1.5 us (1%)
    ppermute x28, waiting for transfers between devices, scatter_sum(): lax.ppermute(send, axis_name, [(i, i ^ 1 << bit) for i in range(count)])  49.9 us
    ppermute x28, starting transfers between devices, scatter_sum(): lax.ppermute(send, axis_name, [(i, i ^ 1 << bit) for i in range(count)])  30.6 us
    all_to_all x1, starting transfers between devices, shards(): lax.all_to_all(packed.reshape(own, -1), 'expert', split_axis=1, concat_ax...  7.39 us
    all_to_all x1, waiting for transfers between devices, shards(): lax.all_to_all(packed.reshape(own, -1), 'expert', split_axis=1, concat_ax...  6.41 us
    dot_general x2, matrix products, project(): jnp.einsum('esd,edf->esf', chosen, weight, preferred_element_type=F32)  6.41 us
    all_to_all x1, starting transfers between devices, shards(): lax.all_to_all(columns, 'expert', split_axis=0, concat_axis=1, tiled=True)  4.13 us
    dot_general x1, matrix products, shards(): jnp.dot(hidden, down_weight[0], preferred_element_type=F32).astype(BF16)  4.03 us
    ppermute x4, starting transfers between devices, add_up(): x = x + lax.ppermute(x, 'expert', [(i, i ^ 1 << bit) for i in range(count)])  3.02 us
  transfers between devices with their start and end apart: 34, of which 23 were waited for; matrix products, arithmetic and copies ran while one was open for 11% of the time, Pallas kernels for 0%

profile of v4, /device:TPU:0, one launch (start us, length us, event | category | flops | bytes accessed | tf_op | source)
XLA Modules:
  0.0 135.1 jit_solution(2285202372975722019)
XLA Ops:
  0.7 0.9 select_reduce_fusion.2
  1.6 1.8 %reshape_squeeze.33 = bf16[4,192,4,128]{3,2,1,0:T(4,128)(2,1)S(1)} reshape(bf16[1,4,192,512]{3,2,1,0:T(8,128)(2,1)} %param.24) | data formatting | bytes 1572864 | tf_op jit(solution)/shard_map/reshape;squeeze | solution.py:65
  3.8 0.7 fusion.84
  4.5 0.4 fusion.85
  5.4 0.4 fusion.18
  6.3 0.7 copy.99
  7.0 7.4 %all-to-all-start = ((bf16[8,16,640]{2,0,1:T(8,128)(2,1)}), bf16[8,16,640]{2,0,1:T(8,128)(2,1)S(1)}, u32[]{:S(2)}, u32[]{:S(2)}) async-start(bf16[8,16,640]{2,0,1:T(8,128)(2,1)} %copy.99), calls=%async_computation | async-start | bytes 327680 | tf_op jit(solution)/shard_map/all_to_all | solution.py:121
  14.7 0.7 copy.131
  15.7 0.8 dynamic_slice.217
  16.5 6.4 %all-to-all-done = bf16[8,16,640]{2,0,1:T(8,128)(2,1)S(1)} async-done(((bf16[8,16,640]{2,0,1:T(8,128)(2,1)}), bf16[8,16,640]{2,0,1:T(8,128)(2,1)S(1)}, u32[]{:S(2)}, u32[]{:S(2)}) %all-to-all-start) | async-done | bytes 163872 | tf_op jit(solution)/shard_map/all_to_all | solution.py:121
  22.9 2.9 %fusion.48 = f32[128,4096]{1,0:T(8,128)S(1)} fusion(bf16[512,4096]{1,0:T(8,128)(2,1)} %param.17, bf16[128,640]{1,0:T(8,128)(2,1)S(1)} %bitcast.245), kind=kOutput, calls=%fused_computation.96 | convolution fusion | flops 536870912 | bytes 6422528 | tf_op jit(solution)/shard_map/dot_general | solution.py:130
  25.8 0.7 copy.130
  27.4 0.6 collective-permute-start
  29.2 0.4 collective-permute-start.1
  29.6 4.8 %collective-permute-done.5 = bf16[2,2,64,256]{3,2,1,0:T(8,128)(2,1)S(1)} collective-permute-done((bf16[2,2,64,256]{3,2,1,0:T(8,128)(2,1)S(1)}, bf16[2,2,64,256]{3,2,1,0:T(8,128)(2,1)S(1)}, u32[]{:S(2)}, u32[]{:S(2)}) %collective-permute-start.5) | collective-permute-done | bytes 131104 | tf_op jit(solution)/shard_map/ppermute | solution.py:29
  34.5 0.6 collective-permute-start.6
  35.1 1.3 collective-permute-start.2
  36.4 3.8 %collective-permute-done.6 = bf16[2,64,256]{2,1,0:T(8,128)(2,1)S(1)} collective-permute-done((bf16[2,64,256]{2,1,0:T(8,128)(2,1)S(1)}, bf16[2,64,256]{2,1,0:T(8,128)(2,1)S(1)}, u32[]{:S(2)}, u32[]{:S(2)}) %collective-permute-start.6) | collective-permute-done | bytes 65568 | tf_op jit(solution)/shard_map/ppermute | solution.py:29
  40.4 1.5 %collective-permute-start.3 = (bf16[64,256]{1,0:T(8,128)(2,1)S(1)}, bf16[64,256]{1,0:T(8,128)(2,1)S(1)}, u32[]{:S(2)}, u32[]{:S(2)}) collective-permute-start(bf16[64,256]{1,0:T(8,128)(2,1)S(1)} %dynamic-slice_bitcast_fusion.22), channel_id=1, source_target_pairs={{0,8},{1,9},{2,10},{3,11},{4,12},{5,13},{6,14},{7,15},{8,0},{9,1},... | collective-permute-start | bytes 98312 | tf_op jit(solution)/shard_map/ppermute | solution.py:29
  42.0 2.3 %collective-permute-done.7 = bf16[64,256]{1,0:T(8,128)(2,1)S(1)} collective-permute-done((bf16[64,256]{1,0:T(8,128)(2,1)S(1)}, bf16[64,256]{1,0:T(8,128)(2,1)S(1)}, u32[]{:S(2)}, u32[]{:S(2)}) %collective-permute-start.7) | collective-permute-done | bytes 32800 | tf_op jit(solution)/shard_map/ppermute | solution.py:29
  44.3 1.3 collective-permute-done.3
  45.8 0.4 convolution_convert_fusion
  46.1 0.7 collective-permute-done.8
  46.9 2.0 %collective-permute-start.9 = (f32[128]{0:T(128)S(1)}, f32[128]{0:T(128)S(1)}, u32[]{:S(2)}, u32[]{:S(2)}) collective-permute-start(f32[128]{0:T(128)S(1)} %add.273), channel_id=1, source_target_pairs={{0,2},{1,3},{2,0},{3,1},{4,6},{5,7},{6,4},{7,5},{8,10},{9,11},{10,... | collective-permute-start | bytes 1544 | tf_op jit(solution)/shard_map/ppermute | solution.py:39
  48.9 3.9 %convert_bitcast_fusion.1 = bf16[16,1,96,768]{3,2,0,1:T(8,128)(2,1)S(1)} fusion(bf16[16,96,256]{2,1,0:T(8,128)(2,1)S(1)} %convolution_convert_fusion, bf16[16,256,768]{2,1,0:T(8,128)(2,1)} %param.14), kind=kOutput, calls=%fused_computation.7 | convolution fusion | flops 605159424 | bytes 9437184 | tf_op jit(solution)/shard_map/esd,edf->esf/dot_general | solution.py:164
  53.1 2.5 %convert_bitcast_fusion = bf16[16,1,96,768]{3,2,0,1:T(8,128)(2,1)} fusion(bf16[16,96,256]{2,1,0:T(8,128)(2,1)S(1)} %convolution_convert_fusion, bf16[16,256,768]{2,1,0:T(8,128)(2,1)S(1)} %bitcast.233), kind=kOutput, calls=%fused_computation.6 | convolution fusion | flops 605159424 | bytes 9437184 | tf_op jit(solution)/shard_map/esd,edf->esf/dot_general | solution.py:164
  55.6 0.8 collective-permute-done.10
  56.4 0.6 collective-permute-start.11
  57.0 0.6 fusion.67
  57.7 4.1 %all-to-all-start.1 = ((bf16[16,8,256]{2,1,0:T(8,128)(2,1)}), bf16[16,8,256]{2,1,0:T(8,128)(2,1)S(1)}, u32[]{:S(2)}, u32[]{:S(2)}) async-start(bf16[16,8,256]{2,1,0:T(8,128)(2,1)} %fusion.67), calls=%async_computation.1 | async-start | bytes 131072 | tf_op jit(solution)/shard_map/all_to_all | solution.py:142
  61.8 1.8 %fusion.81 = (bf16[16,1,48,768]{3,2,0,1:T(8,128)(2,1)S(1)}, bf16[16,1,48,768]{3,2,0,1:T(8,128)(2,1)S(1)}) fusion(bf16[16,1,96,768]{3,2,0,1:T(8,128)(2,1)} %convert_bitcast_fusion), kind=kLoop, calls=%fused_computation.176 | loop fusion | bytes 4718592 | tf_op jit(solution)/shard_map/slice | solution.py:172
  63.8 0.5 collective-permute-start.20
  64.6 0.5 collective-permute-start.16
  65.2 0.7 collective-permute-done.20
  66.0 2.0 %collective-permute-start.21 = (bf16[2,2,48,768]{3,2,1,0:T(8,128)(2,1)S(1)}, bf16[2,2,48,768]{3,2,1,0:T(8,128)(2,1)S(1)}, u32[]{:S(2)}, u32[]{:S(2)}) collective-permute-start(bf16[2,2,48,768]{3,2,1,0:T(8,128)(2,1)S(1)} %dynamic-slice_bitcast_fusion.2), channel_id=1, source_target_pairs={{0,4},{1,5},{2,6},{3,7},{4,0},{5,1},{6,2},{7,3},{8,12},{9,13},{10,... | collective-permute-start | bytes 884744 | tf_op jit(solution)/shard_map/ppermute | solution.py:29
  68.0 0.4 collective-permute-done.16
  68.6 2.0 %collective-permute-start.17 = (bf16[2,2,48,768]{3,2,0,1:T(8,128)(2,1)S(1)}, bf16[2,2,48,768]{3,2,0,1:T(8,128)(2,1)S(1)}, u32[]{:S(2)}, u32[]{:S(2)}) collective-permute-start(bf16[2,2,48,768]{3,2,0,1:T(8,128)(2,1)S(1)} %dynamic-slice_bitcast_fusion.3), channel_id=1, source_target_pairs={{0,2},{1,3},{2,0},{3,1},{4,6},{5,7},{6,4},{7,5},{8,10},{9,11},{10,... | collective-permute-start | bytes 884744 | tf_op jit(solution)/shard_map/ppermute | solution.py:29
  70.5 4.9 %collective-permute-done.21 = bf16[2,2,48,768]{3,2,1,0:T(8,128)(2,1)S(1)} collective-permute-done((bf16[2,2,48,768]{3,2,1,0:T(8,128)(2,1)S(1)}, bf16[2,2,48,768]{3,2,1,0:T(8,128)(2,1)S(1)}, u32[]{:S(2)}, u32[]{:S(2)}) %collective-permute-start.21) | collective-permute-done | bytes 294944 | tf_op jit(solution)/shard_map/ppermute | solution.py:29
  75.5 2.6 %collective-permute-start.22 = (bf16[2,48,768]{2,1,0:T(8,128)(2,1)S(1)}, bf16[2,48,768]{2,1,0:T(8,128)(2,1)S(1)}, u32[]{:S(2)}, u32[]{:S(2)}) collective-permute-start(bf16[2,48,768]{2,1,0:T(8,128)(2,1)S(1)} %dynamic-slice_bitcast_fusion.6), channel_id=1, source_target_pairs={{0,8},{1,9},{2,10},{3,11},{4,12},{5,13},{6,14},{7,15},{8,0},{9,1},... | collective-permute-start | bytes 442376 | tf_op jit(solution)/shard_map/ppermute | solution.py:29
  78.6 1.5 %collective-permute-start.13 = (bf16[2,2,96,768]{3,2,1,0:T(8,128)(2,1)S(1)}, bf16[2,2,96,768]{3,2,1,0:T(8,128)(2,1)S(1)}, u32[]{:S(2)}, u32[]{:S(2)}) collective-permute-start(bf16[2,2,96,768]{3,2,1,0:T(8,128)(2,1)S(1)} %dynamic-slice_bitcast_fusion.1), channel_id=1, source_target_pairs={{0,2},{1,3},{2,0},{3,1},{4,6},{5,7},{6,4},{7,5},{8,10},{9,11},{10,... | collective-permute-start | bytes 1769480 | tf_op jit(solution)/shard_map/ppermute | solution.py:29
  80.2 1.5 %collective-permute-start.18 = (bf16[2,48,768]{2,1,0:T(8,128)(2,1)S(1)}, bf16[2,48,768]{2,1,0:T(8,128)(2,1)S(1)}, u32[]{:S(2)}, u32[]{:S(2)}) collective-permute-start(bf16[2,48,768]{2,1,0:T(8,128)(2,1)S(1)} %dynamic-slice_bitcast_fusion.7), channel_id=1, source_target_pairs={{0,4},{1,5},{2,6},{3,7},{4,0},{5,1},{6,2},{7,3},{8,12},{9,13},{10,... | collective-permute-start | bytes 442376 | tf_op jit(solution)/shard_map/ppermute | solution.py:29
  81.7 3.4 %collective-permute-done.22 = bf16[2,48,768]{2,1,0:T(8,128)(2,1)S(1)} collective-permute-done((bf16[2,48,768]{2,1,0:T(8,128)(2,1)S(1)}, bf16[2,48,768]{2,1,0:T(8,128)(2,1)S(1)}, u32[]{:S(2)}, u32[]{:S(2)}) %collective-permute-start.22) | collective-permute-done | bytes 147488 | tf_op jit(solution)/shard_map/ppermute | solution.py:29
  85.1 1.5 %collective-permute-start.23 = (bf16[48,768]{1,0:T(8,128)(2,1)S(1)}, bf16[48,768]{1,0:T(8,128)(2,1)S(1)}, u32[]{:S(2)}, u32[]{:S(2)}) collective-permute-start(bf16[48,768]{1,0:T(8,128)(2,1)S(1)} %dynamic-slice_bitcast_fusion.13), channel_id=1, source_target_pairs={{0,2},{1,3},{2,0},{3,1},{4,6},{5,7},{6,4},{7,5},{8,10},{9,11},{10,... | collective-permute-start | bytes 221192 | tf_op jit(solution)/shard_map/ppermute | solution.py:29
  86.6 0.6 collective-permute-done.18
  87.2 6.8 %collective-permute-done.13 = bf16[2,2,96,768]{3,2,1,0:T(8,128)(2,1)S(1)} collective-permute-done((bf16[2,2,96,768]{3,2,1,0:T(8,128)(2,1)S(1)}, bf16[2,2,96,768]{3,2,1,0:T(8,128)(2,1)S(1)}, u32[]{:S(2)}, u32[]{:S(2)}) %collective-permute-start.13) | collective-permute-done | bytes 589856 | tf_op jit(solution)/shard_map/ppermute | solution.py:29
  94.2 1.5 %collective-permute-start.14 = (bf16[2,96,768]{2,1,0:T(8,128)(2,1)S(1)}, bf16[2,96,768]{2,1,0:T(8,128)(2,1)S(1)}, u32[]{:S(2)}, u32[]{:S(2)}) collective-permute-start(bf16[2,96,768]{2,1,0:T(8,128)(2,1)S(1)} %dynamic-slice_bitcast_fusion.4), channel_id=1, source_target_pairs={{0,4},{1,5},{2,6},{3,7},{4,0},{5,1},{6,2},{7,3},{8,12},{9,13},{10,... | collective-permute-start | bytes 884744 | tf_op jit(solution)/shard_map/ppermute | solution.py:29
  95.7 2.4 %collective-permute-start.19 = (bf16[48,768]{1,0:T(8,128)(2,1)S(1)}, bf16[48,768]{1,0:T(8,128)(2,1)S(1)}, u32[]{:S(2)}, u32[]{:S(2)}) collective-permute-start(bf16[48,768]{1,0:T(8,128)(2,1)S(1)} %dynamic-slice_bitcast_fusion.14), channel_id=1, source_target_pairs={{0,8},{1,9},{2,10},{3,11},{4,12},{5,13},{6,14},{7,15},{8,0},{9,1},... | collective-permute-start | bytes 221192 | tf_op jit(solution)/shard_map/ppermute | solution.py:29
  98.1 4.3 %collective-permute-done.14 = bf16[2,96,768]{2,1,0:T(8,128)(2,1)S(1)} collective-permute-done((bf16[2,96,768]{2,1,0:T(8,128)(2,1)S(1)}, bf16[2,96,768]{2,1,0:T(8,128)(2,1)S(1)}, u32[]{:S(2)}, u32[]{:S(2)}) %collective-permute-start.14) | collective-permute-done | bytes 294944 | tf_op jit(solution)/shard_map/ppermute | solution.py:29
  102.5 1.6 %collective-permute-start.15 = (bf16[96,768]{1,0:T(8,128)(2,1)S(1)}, bf16[96,768]{1,0:T(8,128)(2,1)S(1)}, u32[]{:S(2)}, u32[]{:S(2)}) collective-permute-start(bf16[96,768]{1,0:T(8,128)(2,1)S(1)} %dynamic-slice_bitcast_fusion.8), channel_id=1, source_target_pairs={{0,8},{1,9},{2,10},{3,11},{4,12},{5,13},{6,14},{7,15},{8,0},{9,1},... | collective-permute-start | bytes 442376 | tf_op jit(solution)/shard_map/ppermute | solution.py:29
  104.2 6.0 %collective-permute-done.15 = bf16[96,768]{1,0:T(8,128)(2,1)S(1)} collective-permute-done((bf16[96,768]{1,0:T(8,128)(2,1)S(1)}, bf16[96,768]{1,0:T(8,128)(2,1)S(1)}, u32[]{:S(2)}, u32[]{:S(2)}) %collective-permute-start.15) | collective-permute-done | bytes 147488 | tf_op jit(solution)/shard_map/ppermute | solution.py:29
  110.3 4.0 %fusion.5 = bf16[16,1,8,4096]{3,2,0,1:T(8,128)(2,1)S(1)} fusion(bf16[1,768,4096]{2,1,0:T(8,128)(2,1)} %param.16, bf16[96,768]{1,0:T(8,128)(2,1)S(1)} %pad_maximum_fusion.1, bf16[96,768]{1,0:T(8,128)(2,1)S(1)} %fusion.31, f32[96]{0:T(128)S(1)} %get-tuple-element.15, f32[96]{0:T(128)S(1)} %get-tuple-element.14, ...), kind=kOutput, calls=%fused_computation.3 | convolution fusion | flops 825614336 | bytes 7648260 | tf_op jit(solution)/shard_map/dot_general | solution.py:193
  114.6 0.7 reshape.171
  115.3 0.6 collective-permute-start.24
  116.3 0.7 collective-permute-done.24
  117.1 1.5 %collective-permute-start.25 = (bf16[2,2,8,2048]{3,2,0,1:T(8,128)(2,1)S(1)}, bf16[2,2,8,2048]{3,2,0,1:T(8,128)(2,1)S(1)}, u32[]{:S(2)}, u32[]{:S(2)}) collective-permute-start(bf16[2,2,8,2048]{3,2,0,1:T(8,128)(2,1)S(1)} %dynamic-slice_bitcast_fusion.10), channel_id=1, source_target_pairs={{0,2},{1,3},{2,0},{3,1},{4,6},{5,7},{6,4},{7,5},{8,10},{9,11},{10,... | collective-permute-start | bytes 393224 | tf_op jit(solution)/shard_map/ppermute | solution.py:29
  118.6 3.2 %collective-permute-done.29 = bf16[2,2,8,2048]{3,2,1,0:T(8,128)(2,1)S(1)} collective-permute-done((bf16[2,2,8,2048]{3,2,1,0:T(8,128)(2,1)S(1)}, bf16[2,2,8,2048]{3,2,1,0:T(8,128)(2,1)S(1)}, u32[]{:S(2)}, u32[]{:S(2)}) %collective-permute-start.29) | collective-permute-done | bytes 131104 | tf_op jit(solution)/shard_map/ppermute | solution.py:29
  121.9 1.3 collective-permute-start.30
  123.3 1.8 %collective-permute-start.26 = (bf16[2,8,2048]{2,1,0:T(8,128)(2,1)S(1)}, bf16[2,8,2048]{2,1,0:T(8,128)(2,1)S(1)}, u32[]{:S(2)}, u32[]{:S(2)}) collective-permute-start(bf16[2,8,2048]{2,1,0:T(8,128)(2,1)S(1)} %dynamic-slice_bitcast_fusion.16), channel_id=1, source_target_pairs={{0,4},{1,5},{2,6},{3,7},{4,0},{5,1},{6,2},{7,3},{8,12},{9,13},{10,... | collective-permute-start | bytes 196616 | tf_op jit(solution)/shard_map/ppermute | solution.py:29
  125.1 2.6 %collective-permute-done.30 = bf16[2,8,2048]{2,1,0:T(8,128)(2,1)S(1)} collective-permute-done((bf16[2,8,2048]{2,1,0:T(8,128)(2,1)S(1)}, bf16[2,8,2048]{2,1,0:T(8,128)(2,1)S(1)}, u32[]{:S(2)}, u32[]{:S(2)}) %collective-permute-start.30) | collective-permute-done | bytes 65568 | tf_op jit(solution)/shard_map/ppermute | solution.py:29
  127.8 1.5 %collective-permute-start.31 = (bf16[8,2048]{1,0:T(8,128)(2,1)S(1)}, bf16[8,2048]{1,0:T(8,128)(2,1)S(1)}, u32[]{:S(2)}, u32[]{:S(2)}) collective-permute-start(bf16[8,2048]{1,0:T(8,128)(2,1)S(1)} %dynamic-slice_bitcast_fusion.19), channel_id=1, source_target_pairs={{0,2},{1,3},{2,0},{3,1},{4,6},{5,7},{6,4},{7,5},{8,10},{9,11},{10,... | collective-permute-start | bytes 98312 | tf_op jit(solution)/shard_map/ppermute | solution.py:29
  129.3 1.5 %collective-permute-start.27 = (bf16[8,2048]{1,0:T(8,128)(2,1)S(1)}, bf16[8,2048]{1,0:T(8,128)(2,1)S(1)}, u32[]{:S(2)}, u32[]{:S(2)}) collective-permute-start(bf16[8,2048]{1,0:T(8,128)(2,1)S(1)} %dynamic-slice_bitcast_fusion.20), channel_id=1, source_target_pairs={{0,8},{1,9},{2,10},{3,11},{4,12},{5,13},{6,14},{7,15},{8,0},{9,1},... | collective-permute-start | bytes 98312 | tf_op jit(solution)/shard_map/ppermute | solution.py:29
  130.8 0.9 collective-permute-done.31
  131.8 2.6 %collective-permute-done.27 = bf16[8,2048]{1,0:T(8,128)(2,1)S(1)} collective-permute-done((bf16[8,2048]{1,0:T(8,128)(2,1)S(1)}, bf16[8,2048]{1,0:T(8,128)(2,1)S(1)}, u32[]{:S(2)}, u32[]{:S(2)}) %collective-permute-start.27) | collective-permute-done | bytes 32800 | tf_op jit(solution)/shard_map/ppermute | solution.py:29
  134.4 0.7 reshape.172
  (145 shorter events, 7.8 us)
Async XLA Ops:
  0.6 2.7 %copy-start = (bf16[1,4,192,512]{3,2,1,0:T(8,128)(2,1)S(1)}, bf16[1,4,192,512]{3,2,1,0:T(8,128)(2,1)}, u32[]{:S(2)}) copy-start(bf16[1,4,192,512]{3,2,1,0:T(8,128)(2,1)} %param.23) | copy-start | bytes 2359300
  0.6 2.9 %copy-start.1 = (bf16[2,1,4,8192]{3,2,1,0:T(4,128)(2,1)S(1)}, bf16[2,1,4,8192]{3,2,1,0:T(4,128)(2,1)}, u32[]{:S(2)}) copy-start(bf16[2,1,4,8192]{3,2,1,0:T(4,128)(2,1)} %param.20) | copy-start | bytes 393220
  0.7 3.1 %copy-start.5 = (s32[1,4]{1,0:T(1,128)S(1)}, s32[1,4]{1,0:T(1,128)}, u32[]{:S(2)}) copy-start(s32[1,4]{1,0:T(1,128)} %param.25) | copy-start | bytes 52
  0.7 3.1 %copy-start.3 = (bf16[2,1,4,512]{3,2,1,0:T(4,128)(2,1)S(1)}, bf16[2,1,4,512]{3,2,1,0:T(4,128)(2,1)}, u32[]{:S(2)}) copy-start(bf16[2,1,4,512]{3,2,1,0:T(4,128)(2,1)} %param.21) | copy-start | bytes 24580
  3.3 2.0 %copy-start.4 = (bf16[2,1,4,512]{3,2,1,0:T(4,128)(2,1)S(1)}, bf16[2,1,4,512]{3,2,1,0:T(4,128)(2,1)}, u32[]{:S(2)}) copy-start(bf16[2,1,4,512]{3,2,1,0:T(4,128)(2,1)} %param.22) | copy-start | bytes 24580
  5.4 9.0 %copy-start.2 = (bf16[2,1,4,4096]{3,2,1,0:T(4,128)(2,1)S(1)}, bf16[2,1,4,4096]{3,2,1,0:T(4,128)(2,1)}, u32[]{:S(2)}) copy-start(bf16[2,1,4,4096]{3,2,1,0:T(4,128)(2,1)} %param.19) | copy-start | bytes 196612
  7.0 15.9 %all-to-all-start = ((bf16[8,16,640]{2,0,1:T(8,128)(2,1)}), bf16[8,16,640]{2,0,1:T(8,128)(2,1)S(1)}, u32[]{:S(2)}, u32[]{:S(2)}) async-start(bf16[8,16,640]{2,0,1:T(8,128)(2,1)} %copy.99), calls=%async_computation | async-start | bytes 327680 | tf_op jit(solution)/shard_map/all_to_all | solution.py:121
  27.1 1.6 %collective-permute-start.4 = (bf16[2,2,2,64,256]{4,3,2,0,1:T(8,128)(2,1)S(1)}, bf16[2,2,2,64,256]{4,3,2,0,1:T(8,128)(2,1)S(1)}, u32[]{:S(2)}, u32[]{:S(2)}) collective-permute-start(bf16[2,2,2,64,256]{4,3,2,0,1:T(8,128)(2,1)S(1)} %bitcast.249), channel_id=1, source_target_pairs={{0,1},{1,0},{2,3},{3,2},{4,5},{5,4},{6,7},{7,6},{8,9},{9,8},{10,11... | collective-permute-start | bytes 786440 | tf_op jit(solution)/shard_map/ppermute | solution.py:29
  27.4 1.7 %collective-permute-start = (bf16[2,2,2,64,256]{4,3,2,1,0:T(8,128)(2,1)S(1)}, bf16[2,2,2,64,256]{4,3,2,1,0:T(8,128)(2,1)S(1)}, u32[]{:S(2)}, u32[]{:S(2)}) collective-permute-start(bf16[2,2,2,64,256]{4,3,2,1,0:T(8,128)(2,1)S(1)} %dynamic-slice_bitcast_fusion.5), channel_id=1, source_target_pairs={{0,1},{1,0},{2,3},{3,2},{4,5},{5,4},{6,7},{7,6},{8,9},{9,8},{10,11... | collective-permute-start | bytes 786440 | tf_op jit(solution)/shard_map/ppermute | solution.py:29
  28.8 5.6 %collective-permute-start.5 = (bf16[2,2,64,256]{3,2,1,0:T(8,128)(2,1)S(1)}, bf16[2,2,64,256]{3,2,1,0:T(8,128)(2,1)S(1)}, u32[]{:S(2)}, u32[]{:S(2)}) collective-permute-start(bf16[2,2,64,256]{3,2,1,0:T(8,128)(2,1)S(1)} %dynamic-slice_bitcast_fusion.11), channel_id=1, source_target_pairs={{0,4},{1,5},{2,6},{3,7},{4,0},{5,1},{6,2},{7,3},{8,12},{9,13},{10,... | collective-permute-start | bytes 393224 | tf_op jit(solution)/shard_map/ppermute | solution.py:29
  29.2 5.9 %collective-permute-start.1 = (bf16[2,2,64,256]{3,2,1,0:T(8,128)(2,1)S(1)}, bf16[2,2,64,256]{3,2,1,0:T(8,128)(2,1)S(1)}, u32[]{:S(2)}, u32[]{:S(2)}) collective-permute-start(bf16[2,2,64,256]{3,2,1,0:T(8,128)(2,1)S(1)} %dynamic-slice_bitcast_fusion.12), channel_id=1, source_target_pairs={{0,2},{1,3},{2,0},{3,1},{4,6},{5,7},{6,4},{7,5},{8,10},{9,11},{10,... | collective-permute-start | bytes 393224 | tf_op jit(solution)/shard_map/ppermute | solution.py:29
  34.5 5.8 %collective-permute-start.6 = (bf16[2,64,256]{2,1,0:T(8,128)(2,1)S(1)}, bf16[2,64,256]{2,1,0:T(8,128)(2,1)S(1)}, u32[]{:S(2)}, u32[]{:S(2)}) collective-permute-start(bf16[2,64,256]{2,1,0:T(8,128)(2,1)S(1)} %dynamic-slice_bitcast_fusion.17), channel_id=1, source_target_pairs={{0,8},{1,9},{2,10},{3,11},{4,12},{5,13},{6,14},{7,15},{8,0},{9,1},... | collective-permute-start | bytes 196616 | tf_op jit(solution)/shard_map/ppermute | solution.py:29
  35.1 18.0 %slice-start = ((s8[6291456]{0:T(1024)(128)(4,1)}), s8[4194304]{0:T(1024)(128)(4,1)S(1)}, s32[]{:S(2)}) async-start(s8[6291456]{0:T(1024)(128)(4,1)} %bitcast.232), calls=%async_computation.2 | async-start | bytes 8388608
  35.1 5.2 %collective-permute-start.2 = (bf16[2,64,256]{2,1,0:T(8,128)(2,1)S(1)}, bf16[2,64,256]{2,1,0:T(8,128)(2,1)S(1)}, u32[]{:S(2)}, u32[]{:S(2)}) collective-permute-start(bf16[2,64,256]{2,1,0:T(8,128)(2,1)S(1)} %dynamic-slice_bitcast_fusion.18), channel_id=1, source_target_pairs={{0,4},{1,5},{2,6},{3,7},{4,0},{5,1},{6,2},{7,3},{8,12},{9,13},{10,... | collective-permute-start | bytes 196616 | tf_op jit(solution)/shard_map/ppermute | solution.py:29
  40.3 4.0 %collective-permute-start.7 = (bf16[64,256]{1,0:T(8,128)(2,1)S(1)}, bf16[64,256]{1,0:T(8,128)(2,1)S(1)}, u32[]{:S(2)}, u32[]{:S(2)}) collective-permute-start(bf16[64,256]{1,0:T(8,128)(2,1)S(1)} %dynamic-slice_bitcast_fusion.21), channel_id=1, source_target_pairs={{0,2},{1,3},{2,0},{3,1},{4,6},{5,7},{6,4},{7,5},{8,10},{9,11},{10,... | collective-permute-start | bytes 98312 | tf_op jit(solution)/shard_map/ppermute | solution.py:29
  40.4 5.1 %collective-permute-start.3 = (bf16[64,256]{1,0:T(8,128)(2,1)S(1)}, bf16[64,256]{1,0:T(8,128)(2,1)S(1)}, u32[]{:S(2)}, u32[]{:S(2)}) collective-permute-start(bf16[64,256]{1,0:T(8,128)(2,1)S(1)} %dynamic-slice_bitcast_fusion.22), channel_id=1, source_target_pairs={{0,8},{1,9},{2,10},{3,11},{4,12},{5,13},{6,14},{7,15},{8,0},{9,1},... | collective-permute-start | bytes 98312 | tf_op jit(solution)/shard_map/ppermute | solution.py:29
  45.7 1.2 collective-permute-start.8
  46.9 6.2 %slice-start.1 = ((s8[6291456]{0:T(1024)(128)(4,1)}), s8[2097152]{0:T(1024)(128)(4,1)S(1)}, s32[]{:S(2)}) async-start(s8[6291456]{0:T(1024)(128)(4,1)} %bitcast.232), calls=%async_computation.3 | async-start | bytes 4194304
  46.9 5.9 %collective-permute-start.9 = (f32[128]{0:T(128)S(1)}, f32[128]{0:T(128)S(1)}, u32[]{:S(2)}, u32[]{:S(2)}) collective-permute-start(f32[128]{0:T(128)S(1)} %add.273), channel_id=1, source_target_pairs={{0,2},{1,3},{2,0},{3,1},{4,6},{5,7},{6,4},{7,5},{8,10},{9,11},{10,... | collective-permute-start | bytes 1544 | tf_op jit(solution)/shard_map/ppermute | solution.py:39
  52.8 3.6 %collective-permute-start.10 = (f32[128]{0:T(128)S(1)}, f32[128]{0:T(128)S(1)}, u32[]{:S(2)}, u32[]{:S(2)}) collective-permute-start(f32[128]{0:T(128)S(1)} %add.274), channel_id=1, source_target_pairs={{0,4},{1,5},{2,6},{3,7},{4,0},{5,1},{6,2},{7,3},{8,12},{9,13},{10,... | collective-permute-start | bytes 1544 | tf_op jit(solution)/shard_map/ppermute | solution.py:39
  56.4 5.4 %collective-permute-start.11 = (f32[128]{0:T(128)S(1)}, f32[128]{0:T(128)S(1)}, u32[]{:S(2)}, u32[]{:S(2)}) collective-permute-start(f32[128]{0:T(128)S(1)} %add.275), channel_id=1, source_target_pairs={{0,8},{1,9},{2,10},{3,11},{4,12},{5,13},{6,14},{7,15},{8,0},{9,1},... | collective-permute-start | bytes 1544 | tf_op jit(solution)/shard_map/ppermute | solution.py:39
  57.7 52.6 %all-to-all-start.1 = ((bf16[16,8,256]{2,1,0:T(8,128)(2,1)}), bf16[16,8,256]{2,1,0:T(8,128)(2,1)S(1)}, u32[]{:S(2)}, u32[]{:S(2)}) async-start(bf16[16,8,256]{2,1,0:T(8,128)(2,1)} %fusion.67), calls=%async_computation.1 | async-start | bytes 131072 | tf_op jit(solution)/shard_map/all_to_all | solution.py:142
  63.8 2.1 %collective-permute-start.20 = (bf16[2,2,2,48,768]{4,3,2,0,1:T(8,128)(2,1)S(1)}, bf16[2,2,2,48,768]{4,3,2,0,1:T(8,128)(2,1)S(1)}, u32[]{:S(2)}, u32[]{:S(2)}) collective-permute-start(bf16[2,2,2,48,768]{4,3,2,0,1:T(8,128)(2,1)S(1)} %bitcast.246), channel_id=1, source_target_pairs={{0,1},{1,0},{2,3},{3,2},{4,5},{5,4},{6,7},{7,6},{8,9},{9,8},{10,11... | collective-permute-start | bytes 1769480 | tf_op jit(solution)/shard_map/ppermute | solution.py:29
  64.3 13.9 %collective-permute-start.12 = (bf16[2,2,2,96,768]{4,3,2,1,0:T(8,128)(2,1)S(1)}, bf16[2,2,2,96,768]{4,3,2,1,0:T(8,128)(2,1)S(1)}, u32[]{:S(2)}, u32[]{:S(2)}) collective-permute-start(bf16[2,2,2,96,768]{4,3,2,1,0:T(8,128)(2,1)S(1)} %dynamic-slice_bitcast_fusion), channel_id=1, source_target_pairs={{0,1},{1,0},{2,3},{3,2},{4,5},{5,4},{6,7},{7,6},{8,9},{9,8},{10,11... | collective-permute-start | bytes 3538952 | tf_op jit(solution)/shard_map/ppermute | solution.py:29
  64.6 3.8 %collective-permute-start.16 = (bf16[2,2,2,48,768]{4,3,0,1,2:T(8,128)(2,1)S(1)}, bf16[2,2,2,48,768]{4,3,0,1,2:T(8,128)(2,1)S(1)}, u32[]{:S(2)}, u32[]{:S(2)}) collective-permute-start(bf16[2,2,2,48,768]{4,3,0,1,2:T(8,128)(2,1)S(1)} %bitcast.247), channel_id=1, source_target_pairs={{0,1},{1,0},{2,3},{3,2},{4,5},{5,4},{6,7},{7,6},{8,9},{9,8},{10,11... | collective-permute-start | bytes 1769480 | tf_op jit(solution)/shard_map/ppermute | solution.py:29
  66.0 9.4 %collective-permute-start.21 = (bf16[2,2,48,768]{3,2,1,0:T(8,128)(2,1)S(1)}, bf16[2,2,48,768]{3,2,1,0:T(8,128)(2,1)S(1)}, u32[]{:S(2)}, u32[]{:S(2)}) collective-permute-start(bf16[2,2,48,768]{3,2,1,0:T(8,128)(2,1)S(1)} %dynamic-slice_bitcast_fusion.2), channel_id=1, source_target_pairs={{0,4},{1,5},{2,6},{3,7},{4,0},{5,1},{6,2},{7,3},{8,12},{9,13},{10,... | collective-permute-start | bytes 884744 | tf_op jit(solution)/shard_map/ppermute | solution.py:29
  68.6 9.6 %collective-permute-start.17 = (bf16[2,2,48,768]{3,2,0,1:T(8,128)(2,1)S(1)}, bf16[2,2,48,768]{3,2,0,1:T(8,128)(2,1)S(1)}, u32[]{:S(2)}, u32[]{:S(2)}) collective-permute-start(bf16[2,2,48,768]{3,2,0,1:T(8,128)(2,1)S(1)} %dynamic-slice_bitcast_fusion.3), channel_id=1, source_target_pairs={{0,2},{1,3},{2,0},{3,1},{4,6},{5,7},{6,4},{7,5},{8,10},{9,11},{10,... | collective-permute-start | bytes 884744 | tf_op jit(solution)/shard_map/ppermute | solution.py:29
  75.5 9.5 %collective-permute-start.22 = (bf16[2,48,768]{2,1,0:T(8,128)(2,1)S(1)}, bf16[2,48,768]{2,1,0:T(8,128)(2,1)S(1)}, u32[]{:S(2)}, u32[]{:S(2)}) collective-permute-start(bf16[2,48,768]{2,1,0:T(8,128)(2,1)S(1)} %dynamic-slice_bitcast_fusion.6), channel_id=1, source_target_pairs={{0,8},{1,9},{2,10},{3,11},{4,12},{5,13},{6,14},{7,15},{8,0},{9,1},... | collective-permute-start | bytes 442376 | tf_op jit(solution)/shard_map/ppermute | solution.py:29
  78.6 15.4 %collective-permute-start.13 = (bf16[2,2,96,768]{3,2,1,0:T(8,128)(2,1)S(1)}, bf16[2,2,96,768]{3,2,1,0:T(8,128)(2,1)S(1)}, u32[]{:S(2)}, u32[]{:S(2)}) collective-permute-start(bf16[2,2,96,768]{3,2,1,0:T(8,128)(2,1)S(1)} %dynamic-slice_bitcast_fusion.1), channel_id=1, source_target_pairs={{0,2},{1,3},{2,0},{3,1},{4,6},{5,7},{6,4},{7,5},{8,10},{9,11},{10,... | collective-permute-start | bytes 1769480 | tf_op jit(solution)/shard_map/ppermute | solution.py:29
  80.2 7.0 %collective-permute-start.18 = (bf16[2,48,768]{2,1,0:T(8,128)(2,1)S(1)}, bf16[2,48,768]{2,1,0:T(8,128)(2,1)S(1)}, u32[]{:S(2)}, u32[]{:S(2)}) collective-permute-start(bf16[2,48,768]{2,1,0:T(8,128)(2,1)S(1)} %dynamic-slice_bitcast_fusion.7), channel_id=1, source_target_pairs={{0,4},{1,5},{2,6},{3,7},{4,0},{5,1},{6,2},{7,3},{8,12},{9,13},{10,... | collective-permute-start | bytes 442376 | tf_op jit(solution)/shard_map/ppermute | solution.py:29
  85.1 13.0 %collective-permute-start.23 = (bf16[48,768]{1,0:T(8,128)(2,1)S(1)}, bf16[48,768]{1,0:T(8,128)(2,1)S(1)}, u32[]{:S(2)}, u32[]{:S(2)}) collective-permute-start(bf16[48,768]{1,0:T(8,128)(2,1)S(1)} %dynamic-slice_bitcast_fusion.13), channel_id=1, source_target_pairs={{0,2},{1,3},{2,0},{3,1},{4,6},{5,7},{6,4},{7,5},{8,10},{9,11},{10,... | collective-permute-start | bytes 221192 | tf_op jit(solution)/shard_map/ppermute | solution.py:29
  94.2 8.2 %collective-permute-start.14 = (bf16[2,96,768]{2,1,0:T(8,128)(2,1)S(1)}, bf16[2,96,768]{2,1,0:T(8,128)(2,1)S(1)}, u32[]{:S(2)}, u32[]{:S(2)}) collective-permute-start(bf16[2,96,768]{2,1,0:T(8,128)(2,1)S(1)} %dynamic-slice_bitcast_fusion.4), channel_id=1, source_target_pairs={{0,4},{1,5},{2,6},{3,7},{4,0},{5,1},{6,2},{7,3},{8,12},{9,13},{10,... | collective-permute-start | bytes 884744 | tf_op jit(solution)/shard_map/ppermute | solution.py:29
  95.7 8.4 %collective-permute-start.19 = (bf16[48,768]{1,0:T(8,128)(2,1)S(1)}, bf16[48,768]{1,0:T(8,128)(2,1)S(1)}, u32[]{:S(2)}, u32[]{:S(2)}) collective-permute-start(bf16[48,768]{1,0:T(8,128)(2,1)S(1)} %dynamic-slice_bitcast_fusion.14), channel_id=1, source_target_pairs={{0,8},{1,9},{2,10},{3,11},{4,12},{5,13},{6,14},{7,15},{8,0},{9,1},... | collective-permute-start | bytes 221192 | tf_op jit(solution)/shard_map/ppermute | solution.py:29
  102.5 7.7 %collective-permute-start.15 = (bf16[96,768]{1,0:T(8,128)(2,1)S(1)}, bf16[96,768]{1,0:T(8,128)(2,1)S(1)}, u32[]{:S(2)}, u32[]{:S(2)}) collective-permute-start(bf16[96,768]{1,0:T(8,128)(2,1)S(1)} %dynamic-slice_bitcast_fusion.8), channel_id=1, source_target_pairs={{0,8},{1,9},{2,10},{3,11},{4,12},{5,13},{6,14},{7,15},{8,0},{9,1},... | collective-permute-start | bytes 442376 | tf_op jit(solution)/shard_map/ppermute | solution.py:29
  114.5 1.6 %collective-permute-start.28 = (bf16[2,2,2,8,2048]{4,3,2,0,1:T(8,128)(2,1)S(1)}, bf16[2,2,2,8,2048]{4,3,2,0,1:T(8,128)(2,1)S(1)}, u32[]{:S(2)}, u32[]{:S(2)}) collective-permute-start(bf16[2,2,2,8,2048]{4,3,2,0,1:T(8,128)(2,1)S(1)} %bitcast.251), channel_id=1, source_target_pairs={{0,1},{1,0},{2,3},{3,2},{4,5},{5,4},{6,7},{7,6},{8,9},{9,8},{10,11... | collective-permute-start | bytes 786440 | tf_op jit(solution)/shard_map/ppermute | solution.py:29
  115.3 1.7 %collective-permute-start.24 = (bf16[2,2,2,8,2048]{4,3,0,1,2:T(8,128)(2,1)S(1)}, bf16[2,2,2,8,2048]{4,3,0,1,2:T(8,128)(2,1)S(1)}, u32[]{:S(2)}, u32[]{:S(2)}) collective-permute-start(bf16[2,2,2,8,2048]{4,3,0,1,2:T(8,128)(2,1)S(1)} %bitcast.250), channel_id=1, source_target_pairs={{0,1},{1,0},{2,3},{3,2},{4,5},{5,4},{6,7},{7,6},{8,9},{9,8},{10,11... | collective-permute-start | bytes 786440 | tf_op jit(solution)/shard_map/ppermute | solution.py:29
  116.2 5.6 %collective-permute-start.29 = (bf16[2,2,8,2048]{3,2,1,0:T(8,128)(2,1)S(1)}, bf16[2,2,8,2048]{3,2,1,0:T(8,128)(2,1)S(1)}, u32[]{:S(2)}, u32[]{:S(2)}) collective-permute-start(bf16[2,2,8,2048]{3,2,1,0:T(8,128)(2,1)S(1)} %dynamic-slice_bitcast_fusion.9), channel_id=1, source_target_pairs={{0,4},{1,5},{2,6},{3,7},{4,0},{5,1},{6,2},{7,3},{8,12},{9,13},{10,... | collective-permute-start | bytes 393224 | tf_op jit(solution)/shard_map/ppermute | solution.py:29
  117.1 6.1 %collective-permute-start.25 = (bf16[2,2,8,2048]{3,2,0,1:T(8,128)(2,1)S(1)}, bf16[2,2,8,2048]{3,2,0,1:T(8,128)(2,1)S(1)}, u32[]{:S(2)}, u32[]{:S(2)}) collective-permute-start(bf16[2,2,8,2048]{3,2,0,1:T(8,128)(2,1)S(1)} %dynamic-slice_bitcast_fusion.10), channel_id=1, source_target_pairs={{0,2},{1,3},{2,0},{3,1},{4,6},{5,7},{6,4},{7,5},{8,10},{9,11},{10,... | collective-permute-start | bytes 393224 | tf_op jit(solution)/shard_map/ppermute | solution.py:29
  121.9 5.8 %collective-permute-start.30 = (bf16[2,8,2048]{2,1,0:T(8,128)(2,1)S(1)}, bf16[2,8,2048]{2,1,0:T(8,128)(2,1)S(1)}, u32[]{:S(2)}, u32[]{:S(2)}) collective-permute-start(bf16[2,8,2048]{2,1,0:T(8,128)(2,1)S(1)} %dynamic-slice_bitcast_fusion.15), channel_id=1, source_target_pairs={{0,8},{1,9},{2,10},{3,11},{4,12},{5,13},{6,14},{7,15},{8,0},{9,1},... | collective-permute-start | bytes 196616 | tf_op jit(solution)/shard_map/ppermute | solution.py:29
  123.3 5.9 %collective-permute-start.26 = (bf16[2,8,2048]{2,1,0:T(8,128)(2,1)S(1)}, bf16[2,8,2048]{2,1,0:T(8,128)(2,1)S(1)}, u32[]{:S(2)}, u32[]{:S(2)}) collective-permute-start(bf16[2,8,2048]{2,1,0:T(8,128)(2,1)S(1)} %dynamic-slice_bitcast_fusion.16), channel_id=1, source_target_pairs={{0,4},{1,5},{2,6},{3,7},{4,0},{5,1},{6,2},{7,3},{8,12},{9,13},{10,... | collective-permute-start | bytes 196616 | tf_op jit(solution)/shard_map/ppermute | solution.py:29
  127.8 4.0 %collective-permute-start.31 = (bf16[8,2048]{1,0:T(8,128)(2,1)S(1)}, bf16[8,2048]{1,0:T(8,128)(2,1)S(1)}, u32[]{:S(2)}, u32[]{:S(2)}) collective-permute-start(bf16[8,2048]{1,0:T(8,128)(2,1)S(1)} %dynamic-slice_bitcast_fusion.19), channel_id=1, source_target_pairs={{0,2},{1,3},{2,0},{3,1},{4,6},{5,7},{6,4},{7,5},{8,10},{9,11},{10,... | collective-permute-start | bytes 98312 | tf_op jit(solution)/shard_map/ppermute | solution.py:29
  129.3 5.1 %collective-permute-start.27 = (bf16[8,2048]{1,0:T(8,128)(2,1)S(1)}, bf16[8,2048]{1,0:T(8,128)(2,1)S(1)}, u32[]{:S(2)}, u32[]{:S(2)}) collective-permute-start(bf16[8,2048]{1,0:T(8,128)(2,1)S(1)} %dynamic-slice_bitcast_fusion.20), channel_id=1, source_target_pairs={{0,8},{1,9},{2,10},{3,11},{4,12},{5,13},{6,14},{7,15},{8,0},{9,1},... | collective-permute-start | bytes 98312 | tf_op jit(solution)/shard_map/ppermute | solution.py:29

commit v5 on v4

--- a/solution.py
+++ b/solution.py
@@ -139,11 +139,11 @@
         ],
         axis=0,
     )
-    back = lax.all_to_all(columns, "expert", split_axis=0, concat_axis=1, tiled=True)
+    spans = columns
     if pair > 1:
-        columns = lax.all_to_all(columns, "dp", split_axis=1, concat_axis=0, tiled=True)
-
-    wide = columns.astype(F32)
+        spans = lax.all_to_all(columns, "dp", split_axis=1, concat_axis=0, tiled=True)
+
+    wide = spans.astype(F32)
     square = add_up(jnp.sum(wide * wide, axis=1))
     gain = lax.dynamic_slice_in_dim(norm_gain, (me * pair + half) * depth, depth)
     scaled = (wide * gain[None, :]).astype(BF16)
@@ -165,19 +165,22 @@
         return sums.reshape(experts, chosen.shape[1], pair, units // pair).swapaxes(1, 2)
 
     def both(chosen, total):
-        gate, up = project(chosen, gate_update), project(chosen, up_update)
-        gate, up, total = lax.optimization_barrier((gate, up, total))
         cut = chosen.shape[1] // 2
-        gate = scatter_both(gate, near_first)
-        first = scatter_both(up[:, :, :cut], near_first)
-        second = scatter_both(up[:, :, cut:], far_first)
-        return gate, jnp.concatenate([first, second], axis=0), total
+        gate = project(chosen, gate_update)
+        gate, chosen = lax.optimization_barrier((gate, chosen))
+        up, total = lax.optimization_barrier((project(chosen, up_update), total))
+        last = scatter_both(up[:, :, cut:], far_first)
+        gate = [scatter_both(part, near_first) for part in (gate[:, :, :cut], gate[:, :, cut:])]
+        up = [scatter_both(up[:, :, :cut], near_first), last]
+        return jnp.concatenate(gate, axis=0), jnp.concatenate(up, axis=0), total, last
 
     if slots <= 128:
-        gate, up, square = both(chosen, square)
+        gate, up, square, last = both(chosen, square)
+        columns, last = lax.optimization_barrier((columns, last))
     else:
         parts = chosen.reshape(experts, -1, 128, depth).swapaxes(0, 1)
         gate, up = lax.map(lambda part: both(part, square)[:2], parts)
+    back = lax.all_to_all(columns, "expert", split_axis=0, concat_axis=1, tiled=True)
     scale = lax.rsqrt(square / width + 1e-6)
     gate, up, back = lax.optimization_barrier((gate, up, back))
     stream = back.reshape(residual.shape)

time: 136 us -> 133 us (0.978)
  starting transfers between devices: 45.1 us -> 36.9 us
  waiting for transfers between devices: 57.8 us -> 66 us
  local copies, waits for them, and re-layouts: 10.4 us -> 9.01 us
    ppermute x28 -> x32, starting transfers between devices: 30.6 us -> 21.2 us  [scatter_sum(): lax.ppermute(send, axis_name, [(i, i ^ 1 << bit) for i in range(count)])]
    all_to_all x1, waiting for transfers between devices: 0.01 us -> 6.83 us  [shards(): lax.all_to_all(columns, 'expert', split_axis=0, concat_axis=1, tiled=True)]
    ppermute x4, waiting for transfers between devices: 1.5 us -> 7.16 us  [add_up(): x = x + lax.ppermute(x, 'expert', [(i, i ^ 1 << bit) for i in range(count)])]
    ppermute x28 -> x32, waiting for transfers between devices: 49.9 us -> 45.6 us  [scatter_sum(): lax.ppermute(send, axis_name, [(i, i ^ 1 << bit) for i in range(count)])]
    slice x1 -> x2, local copies, waits for them, and re-layouts: 1.79 us -> 0.31 us  [the longest x1 0.15 us: both(): up = [scatter_both(up[:, :, :cut], near_first), last]]
  transfers between devices with their start and end apart: 34 -> 38, of which waited for: 23 -> 25; matrix products, arithmetic and copies ran while one was open for 11% -> 6% of each run, Pallas kernels for 0% -> 0%
where the time goes in v5:
time: 133 us
  waiting for transfers between devices  66 us (50%)
  starting transfers between devices  36.9 us (28%)
  matrix products  14.2 us (11%)
  local copies, waits for them, and re-layouts  9.01 us (7%)
  other arithmetic  4.74 us (4%)
  between operations  1.63 us (1%)
    ppermute x32, waiting for transfers between devices, scatter_sum(): lax.ppermute(send, axis_name, [(i, i ^ 1 << bit) for i in range(count)])  45.6 us
    ppermute x32, starting transfers between devices, scatter_sum(): lax.ppermute(send, axis_name, [(i, i ^ 1 << bit) for i in range(count)])  21.2 us
    all_to_all x1, starting transfers between devices, shards(): lax.all_to_all(packed.reshape(own, -1), 'expert', split_axis=1, concat_ax...  7.39 us
    ppermute x4, waiting for transfers between devices, add_up(): x = x + lax.ppermute(x, 'expert', [(i, i ^ 1 << bit) for i in range(count)])  7.16 us
    all_to_all x1, waiting for transfers between devices, shards(): lax.all_to_all(columns, 'expert', split_axis=0, concat_axis=1, tiled=True)  6.83 us
    all_to_all x1, waiting for transfers between devices, shards(): lax.all_to_all(packed.reshape(own, -1), 'expert', split_axis=1, concat_ax...  6.4 us
    dot_general x2, matrix products, project(): jnp.einsum('esd,edf->esf', chosen, weight, preferred_element_type=F32)  5.13 us
    all_to_all x1, starting transfers between devices, shards(): lax.all_to_all(columns, 'expert', split_axis=0, concat_axis=1, tiled=True)  4.81 us
  transfers between devices with their start and end apart: 38, of which 25 were waited for; matrix products, arithmetic and copies ran while one was open for 6% of the time, Pallas kernels for 0%

profile of v5, /device:TPU:0, one launch (start us, length us, event | category | flops | bytes accessed | tf_op | source)
XLA Modules:
  0.0 132.5 jit_solution(9035768678977513417)
XLA Ops:
  0.7 0.9 select_reduce_fusion.2
  1.6 1.8 %reshape_squeeze.36 = bf16[4,192,4,128]{3,2,1,0:T(4,128)(2,1)S(1)} reshape(bf16[1,4,192,512]{3,2,1,0:T(8,128)(2,1)} %param.24) | data formatting | bytes 1572864 | tf_op jit(solution)/shard_map/reshape;squeeze | solution.py:65
  3.8 0.7 fusion.87
  4.5 0.4 fusion.88
  5.4 0.4 fusion.18
  6.3 0.7 copy.107
  7.0 7.4 %all-to-all-start = ((bf16[8,16,640]{2,0,1:T(8,128)(2,1)}), bf16[8,16,640]{2,0,1:T(8,128)(2,1)S(1)}, u32[]{:S(2)}, u32[]{:S(2)}) async-start(bf16[8,16,640]{2,0,1:T(8,128)(2,1)} %copy.107), calls=%async_computation | async-start | bytes 327680 | tf_op jit(solution)/shard_map/all_to_all | solution.py:121
  14.8 0.7 copy.142
  15.7 0.8 dynamic_slice.237
  16.5 6.4 %all-to-all-done = bf16[8,16,640]{2,0,1:T(8,128)(2,1)S(1)} async-done(((bf16[8,16,640]{2,0,1:T(8,128)(2,1)}), bf16[8,16,640]{2,0,1:T(8,128)(2,1)S(1)}, u32[]{:S(2)}, u32[]{:S(2)}) %all-to-all-start) | async-done | bytes 163872 | tf_op jit(solution)/shard_map/all_to_all | solution.py:121
  23.1 2.9 %fusion.52 = f32[128,4096]{1,0:T(8,128)S(1)} fusion(bf16[512,4096]{1,0:T(8,128)(2,1)} %param.17, bf16[128,640]{1,0:T(8,128)(2,1)S(1)} %bitcast.269), kind=kOutput, calls=%fused_computation.108 | convolution fusion | flops 536870912 | bytes 6422528 | tf_op jit(solution)/shard_map/dot_general | solution.py:130
  26.0 0.7 copy.141
  26.6 0.3 fusion.9
  27.7 0.5 collective-permute-start
  28.5 0.4 collective-permute-done.4
  29.1 0.3 collective-permute-done
  29.8 4.8 %collective-permute-done.5 = bf16[2,2,64,256]{3,2,1,0:T(8,128)(2,1)S(1)} collective-permute-done((bf16[2,2,64,256]{3,2,1,0:T(8,128)(2,1)S(1)}, bf16[2,2,64,256]{3,2,1,0:T(8,128)(2,1)S(1)}, u32[]{:S(2)}, u32[]{:S(2)}) %collective-permute-start.5) | collective-permute-done | bytes 131104 | tf_op jit(solution)/shard_map/ppermute | solution.py:29
  34.7 0.6 collective-permute-start.6
  35.4 1.2 collective-permute-start.2
  36.6 3.8 %collective-permute-done.6 = bf16[2,64,256]{2,1,0:T(8,128)(2,1)S(1)} collective-permute-done((bf16[2,64,256]{2,1,0:T(8,128)(2,1)S(1)}, bf16[2,64,256]{2,1,0:T(8,128)(2,1)S(1)}, u32[]{:S(2)}, u32[]{:S(2)}) %collective-permute-start.6) | collective-permute-done | bytes 65568 | tf_op jit(solution)/shard_map/ppermute | solution.py:29
  40.6 1.5 %collective-permute-start.3 = (bf16[64,256]{1,0:T(8,128)(2,1)S(1)}, bf16[64,256]{1,0:T(8,128)(2,1)S(1)}, u32[]{:S(2)}, u32[]{:S(2)}) collective-permute-start(bf16[64,256]{1,0:T(8,128)(2,1)S(1)} %dynamic-slice_bitcast_fusion.25), channel_id=1, source_target_pairs={{0,8},{1,9},{2,10},{3,11},{4,12},{5,13},{6,14},{7,15},{8,0},{9,1},... | collective-permute-start | bytes 98312 | tf_op jit(solution)/shard_map/ppermute | solution.py:29
  42.2 2.3 %collective-permute-done.7 = bf16[64,256]{1,0:T(8,128)(2,1)S(1)} collective-permute-done((bf16[64,256]{1,0:T(8,128)(2,1)S(1)}, bf16[64,256]{1,0:T(8,128)(2,1)S(1)}, u32[]{:S(2)}, u32[]{:S(2)}) %collective-permute-start.7) | collective-permute-done | bytes 32800 | tf_op jit(solution)/shard_map/ppermute | solution.py:29
  44.5 1.3 collective-permute-done.3
  45.9 0.4 convolution_convert_fusion
  46.3 4.0 %convert_bitcast_fusion.1 = bf16[16,1,96,768]{3,2,0,1:T(8,128)(2,1)S(1)} fusion(bf16[16,96,256]{2,1,0:T(8,128)(2,1)S(1)} %convolution_convert_fusion, bf16[16,256,768]{2,1,0:T(8,128)(2,1)} %param.14), kind=kOutput, calls=%fused_computation.5 | convolution fusion | flops 605159424 | bytes 9437184 | tf_op jit(solution)/shard_map/esd,edf->esf/dot_general | solution.py:164
  50.6 1.1 collective-permute-done.16
  51.7 2.0 %collective-permute-start.17 = (f32[128]{0:T(128)S(1)}, f32[128]{0:T(128)S(1)}, u32[]{:S(2)}, u32[]{:S(2)}) collective-permute-start(f32[128]{0:T(128)S(1)} %add.297), channel_id=1, source_target_pairs={{0,2},{1,3},{2,0},{3,1},{4,6},{5,7},{6,4},{7,5},{8,10},{9,11},{10,... | collective-permute-start | bytes 1544 | tf_op jit(solution)/shard_map/ppermute | solution.py:39
  53.7 0.6 pad_maximum_fusion.3
  54.3 0.9 collective-permute-done.17
  55.7 3.1 %collective-permute-done.18 = f32[128]{0:T(128)S(1)} collective-permute-done((f32[128]{0:T(128)S(1)}, f32[128]{0:T(128)S(1)}, u32[]{:S(2)}, u32[]{:S(2)}) %collective-permute-start.18) | collective-permute-done | bytes 544 | tf_op jit(solution)/shard_map/ppermute | solution.py:39
  58.8 1.2 collective-permute-start.19
  60.0 1.1 convert_bitcast_fusion
  61.1 2.1 %collective-permute-done.19 = f32[128]{0:T(128)S(1)} collective-permute-done((f32[128]{0:T(128)S(1)}, f32[128]{0:T(128)S(1)}, u32[]{:S(2)}, u32[]{:S(2)}) %collective-permute-start.19) | collective-permute-done | bytes 544 | tf_op jit(solution)/shard_map/ppermute | solution.py:39
  63.7 0.6 collective-permute-start.20
  64.6 2.1 %collective-permute-start.13 = (bf16[2,2,48,768]{3,2,1,0:T(8,128)(2,1)S(1)}, bf16[2,2,48,768]{3,2,1,0:T(8,128)(2,1)S(1)}, u32[]{:S(2)}, u32[]{:S(2)}) collective-permute-start(bf16[2,2,48,768]{3,2,1,0:T(8,128)(2,1)S(1)} %dynamic-slice_bitcast_fusion.3), channel_id=1, source_target_pairs={{0,2},{1,3},{2,0},{3,1},{4,6},{5,7},{6,4},{7,5},{8,10},{9,11},{10,... | collective-permute-start | bytes 884744 | tf_op jit(solution)/shard_map/ppermute | solution.py:29
  67.1 0.3 collective-permute-start.25
  67.6 2.1 %collective-permute-start.21 = (bf16[2,2,48,768]{3,2,0,1:T(8,128)(2,1)S(1)}, bf16[2,2,48,768]{3,2,0,1:T(8,128)(2,1)S(1)}, u32[]{:S(2)}, u32[]{:S(2)}) collective-permute-start(bf16[2,2,48,768]{3,2,0,1:T(8,128)(2,1)S(1)} %dynamic-slice_bitcast_fusion.2), channel_id=1, source_target_pairs={{0,2},{1,3},{2,0},{3,1},{4,6},{5,7},{6,4},{7,5},{8,10},{9,11},{10,... | collective-permute-start | bytes 884744 | tf_op jit(solution)/shard_map/ppermute | solution.py:29
  69.7 4.8 %collective-permute-done.13 = bf16[2,2,48,768]{3,2,1,0:T(8,128)(2,1)S(1)} collective-permute-done((bf16[2,2,48,768]{3,2,1,0:T(8,128)(2,1)S(1)}, bf16[2,2,48,768]{3,2,1,0:T(8,128)(2,1)S(1)}, u32[]{:S(2)}, u32[]{:S(2)}) %collective-permute-start.13) | collective-permute-done | bytes 294944 | tf_op jit(solution)/shard_map/ppermute | solution.py:29
  74.6 0.3 collective-permute-start.14
  74.9 5.9 %collective-permute-done.9 = bf16[2,2,48,768]{3,2,0,1:T(8,128)(2,1)S(1)} collective-permute-done((bf16[2,2,48,768]{3,2,0,1:T(8,128)(2,1)S(1)}, bf16[2,2,48,768]{3,2,0,1:T(8,128)(2,1)S(1)}, u32[]{:S(2)}, u32[]{:S(2)}) %collective-permute-start.9) | collective-permute-done | bytes 294944 | tf_op jit(solution)/shard_map/ppermute | solution.py:29
  80.9 0.3 collective-permute-start.10
  81.4 2.0 %collective-permute-start.26 = (bf16[2,48,768]{2,1,0:T(8,128)(2,1)S(1)}, bf16[2,48,768]{2,1,0:T(8,128)(2,1)S(1)}, u32[]{:S(2)}, u32[]{:S(2)}) collective-permute-start(bf16[2,48,768]{2,1,0:T(8,128)(2,1)S(1)} %dynamic-slice_bitcast_fusion.6), channel_id=1, source_target_pairs={{0,8},{1,9},{2,10},{3,11},{4,12},{5,13},{6,14},{7,15},{8,0},{9,1},... | collective-permute-start | bytes 442376 | tf_op jit(solution)/shard_map/ppermute | solution.py:29
  83.4 3.2 %collective-permute-done.21 = bf16[2,2,48,768]{3,2,0,1:T(8,128)(2,1)S(1)} collective-permute-done((bf16[2,2,48,768]{3,2,0,1:T(8,128)(2,1)S(1)}, bf16[2,2,48,768]{3,2,0,1:T(8,128)(2,1)S(1)}, u32[]{:S(2)}, u32[]{:S(2)}) %collective-permute-start.21) | collective-permute-done | bytes 294944 | tf_op jit(solution)/shard_map/ppermute | solution.py:29
  86.6 0.3 collective-permute-start.22
  87.0 1.7 %collective-permute-start.15 = (bf16[48,768]{1,0:T(8,128)(2,1)S(1)}, bf16[48,768]{1,0:T(8,128)(2,1)S(1)}, u32[]{:S(2)}, u32[]{:S(2)}) collective-permute-start(bf16[48,768]{1,0:T(8,128)(2,1)S(1)} %dynamic-slice_bitcast_fusion.16), channel_id=1, source_target_pairs={{0,8},{1,9},{2,10},{3,11},{4,12},{5,13},{6,14},{7,15},{8,0},{9,1},... | collective-permute-start | bytes 221192 | tf_op jit(solution)/shard_map/ppermute | solution.py:29
  88.8 1.4 %collective-permute-start.11 = (bf16[48,768]{1,0:T(8,128)(2,1)S(1)}, bf16[48,768]{1,0:T(8,128)(2,1)S(1)}, u32[]{:S(2)}, u32[]{:S(2)}) collective-permute-start(bf16[48,768]{1,0:T(8,128)(2,1)S(1)} %dynamic-slice_bitcast_fusion.17), channel_id=1, source_target_pairs={{0,8},{1,9},{2,10},{3,11},{4,12},{5,13},{6,14},{7,15},{8,0},{9,1},... | collective-permute-start | bytes 221192 | tf_op jit(solution)/shard_map/ppermute | solution.py:29
  90.2 1.8 %collective-permute-start.27 = (bf16[48,768]{1,0:T(8,128)(2,1)S(1)}, bf16[48,768]{1,0:T(8,128)(2,1)S(1)}, u32[]{:S(2)}, u32[]{:S(2)}) collective-permute-start(bf16[48,768]{1,0:T(8,128)(2,1)S(1)} %dynamic-slice_bitcast_fusion.14), channel_id=1, source_target_pairs={{0,2},{1,3},{2,0},{3,1},{4,6},{5,7},{6,4},{7,5},{8,10},{9,11},{10,... | collective-permute-start | bytes 221192 | tf_op jit(solution)/shard_map/ppermute | solution.py:29
  92.0 2.9 %collective-permute-done.22 = bf16[2,48,768]{2,1,0:T(8,128)(2,1)S(1)} collective-permute-done((bf16[2,48,768]{2,1,0:T(8,128)(2,1)S(1)}, bf16[2,48,768]{2,1,0:T(8,128)(2,1)S(1)}, u32[]{:S(2)}, u32[]{:S(2)}) %collective-permute-start.22) | collective-permute-done | bytes 147488 | tf_op jit(solution)/shard_map/ppermute | solution.py:29
  95.1 2.2 %collective-permute-done.11 = bf16[48,768]{1,0:T(8,128)(2,1)S(1)} collective-permute-done((bf16[48,768]{1,0:T(8,128)(2,1)S(1)}, bf16[48,768]{1,0:T(8,128)(2,1)S(1)}, u32[]{:S(2)}, u32[]{:S(2)}) %collective-permute-start.11) | collective-permute-done | bytes 73760 | tf_op jit(solution)/shard_map/ppermute | solution.py:29
  97.4 4.8 %all-to-all-start.1 = ((bf16[16,8,256]{2,1,0:T(8,128)(2,1)}), bf16[16,8,256]{2,1,0:T(8,128)(2,1)S(1)}, u32[]{:S(2)}, u32[]{:S(2)}) async-start(bf16[16,8,256]{2,1,0:T(8,128)(2,1)} %bitcast.72), calls=%async_computation.1 | async-start | bytes 131072 | tf_op jit(solution)/shard_map/all_to_all | solution.py:183
  102.3 6.8 %all-to-all-done.1 = bf16[16,8,256]{2,1,0:T(8,128)(2,1)S(1)} async-done(((bf16[16,8,256]{2,1,0:T(8,128)(2,1)}), bf16[16,8,256]{2,1,0:T(8,128)(2,1)S(1)}, u32[]{:S(2)}, u32[]{:S(2)}) %all-to-all-start.1) | async-done | bytes 65568 | tf_op jit(solution)/shard_map/all_to_all | solution.py:183
  109.1 4.0 %fusion.5 = bf16[16,1,8,4096]{3,2,0,1:T(8,128)(2,1)S(1)} fusion(bf16[1,768,4096]{2,1,0:T(8,128)(2,1)} %param.16, bf16[96,768]{1,0:T(8,128)(2,1)S(1)} %pad_maximum_fusion.2, bf16[96,768]{1,0:T(8,128)(2,1)S(1)} %pad_maximum_fusion.1, f32[96]{0:T(128)S(1)} %get-tuple-element.19, f32[96]{0:T(128)S(1)} %get-tuple-element.18, ...), kind=kOutput, calls=%fused_computation.3 | convolution fusion | flops 825614336 | bytes 7648260 | tf_op jit(solution)/shard_map/dot_general | solution.py:196
  113.4 0.7 reshape.179
  114.1 0.6 collective-permute-start.28
  115.2 0.6 collective-permute-done.28
  116.1 4.5 %collective-permute-done.33 = bf16[2,2,8,2048]{3,2,1,0:T(8,128)(2,1)S(1)} collective-permute-done((bf16[2,2,8,2048]{3,2,1,0:T(8,128)(2,1)S(1)}, bf16[2,2,8,2048]{3,2,1,0:T(8,128)(2,1)S(1)}, u32[]{:S(2)}, u32[]{:S(2)}) %collective-permute-start.33) | collective-permute-done | bytes 131104 | tf_op jit(solution)/shard_map/ppermute | solution.py:29
  121.0 0.8 collective-permute-done.29
  121.8 0.9 collective-permute-start.30
  122.7 3.8 %collective-permute-done.34 = bf16[2,8,2048]{2,1,0:T(8,128)(2,1)S(1)} collective-permute-done((bf16[2,8,2048]{2,1,0:T(8,128)(2,1)S(1)}, bf16[2,8,2048]{2,1,0:T(8,128)(2,1)S(1)}, u32[]{:S(2)}, u32[]{:S(2)}) %collective-permute-start.34) | collective-permute-done | bytes 65568 | tf_op jit(solution)/shard_map/ppermute | solution.py:29
  126.6 0.3 collective-permute-start.35
  127.0 1.2 collective-permute-start.31
  128.2 2.3 %collective-permute-done.35 = bf16[8,2048]{1,0:T(8,128)(2,1)S(1)} collective-permute-done((bf16[8,2048]{1,0:T(8,128)(2,1)S(1)}, bf16[8,2048]{1,0:T(8,128)(2,1)S(1)}, u32[]{:S(2)}, u32[]{:S(2)}) %collective-permute-start.35) | collective-permute-done | bytes 32800 | tf_op jit(solution)/shard_map/ppermute | solution.py:29
  130.6 1.3 collective-permute-done.31
  131.9 0.7 reshape.180
  (164 shorter events, 8.6 us)
Async XLA Ops:
  0.6 2.7 %copy-start = (bf16[1,4,192,512]{3,2,1,0:T(8,128)(2,1)S(1)}, bf16[1,4,192,512]{3,2,1,0:T(8,128)(2,1)}, u32[]{:S(2)}) copy-start(bf16[1,4,192,512]{3,2,1,0:T(8,128)(2,1)} %param.23) | copy-start | bytes 2359300
  0.6 2.9 %copy-start.1 = (bf16[2,1,4,8192]{3,2,1,0:T(4,128)(2,1)S(1)}, bf16[2,1,4,8192]{3,2,1,0:T(4,128)(2,1)}, u32[]{:S(2)}) copy-start(bf16[2,1,4,8192]{3,2,1,0:T(4,128)(2,1)} %param.20) | copy-start | bytes 393220
  0.7 3.1 %copy-start.5 = (s32[1,4]{1,0:T(1,128)S(1)}, s32[1,4]{1,0:T(1,128)}, u32[]{:S(2)}) copy-start(s32[1,4]{1,0:T(1,128)} %param.25) | copy-start | bytes 52
  0.7 3.1 %copy-start.3 = (bf16[2,1,4,512]{3,2,1,0:T(4,128)(2,1)S(1)}, bf16[2,1,4,512]{3,2,1,0:T(4,128)(2,1)}, u32[]{:S(2)}) copy-start(bf16[2,1,4,512]{3,2,1,0:T(4,128)(2,1)} %param.21) | copy-start | bytes 24580
  3.3 2.0 %copy-start.4 = (bf16[2,1,4,512]{3,2,1,0:T(4,128)(2,1)S(1)}, bf16[2,1,4,512]{3,2,1,0:T(4,128)(2,1)}, u32[]{:S(2)}) copy-start(bf16[2,1,4,512]{3,2,1,0:T(4,128)(2,1)} %param.22) | copy-start | bytes 24580
  5.4 9.2 %copy-start.2 = (bf16[2,1,4,4096]{3,2,1,0:T(4,128)(2,1)S(1)}, bf16[2,1,4,4096]{3,2,1,0:T(4,128)(2,1)}, u32[]{:S(2)}) copy-start(bf16[2,1,4,4096]{3,2,1,0:T(4,128)(2,1)} %param.19) | copy-start | bytes 196612
  7.0 15.9 %all-to-all-start = ((bf16[8,16,640]{2,0,1:T(8,128)(2,1)}), bf16[8,16,640]{2,0,1:T(8,128)(2,1)S(1)}, u32[]{:S(2)}, u32[]{:S(2)}) async-start(bf16[8,16,640]{2,0,1:T(8,128)(2,1)} %copy.107), calls=%async_computation | async-start | bytes 327680 | tf_op jit(solution)/shard_map/all_to_all | solution.py:121
  27.3 1.6 %collective-permute-start.4 = (bf16[2,2,2,64,256]{4,3,2,0,1:T(8,128)(2,1)S(1)}, bf16[2,2,2,64,256]{4,3,2,0,1:T(8,128)(2,1)S(1)}, u32[]{:S(2)}, u32[]{:S(2)}) collective-permute-start(bf16[2,2,2,64,256]{4,3,2,0,1:T(8,128)(2,1)S(1)} %bitcast.274), channel_id=1, source_target_pairs={{0,1},{1,0},{2,3},{3,2},{4,5},{5,4},{6,7},{7,6},{8,9},{9,8},{10,11... | collective-permute-start | bytes 786440 | tf_op jit(solution)/shard_map/ppermute | solution.py:29
  27.7 1.7 %collective-permute-start = (bf16[2,2,2,64,256]{4,3,2,1,0:T(8,128)(2,1)S(1)}, bf16[2,2,2,64,256]{4,3,2,1,0:T(8,128)(2,1)S(1)}, u32[]{:S(2)}, u32[]{:S(2)}) collective-permute-start(bf16[2,2,2,64,256]{4,3,2,1,0:T(8,128)(2,1)S(1)} %dynamic-slice_bitcast_fusion.5), channel_id=1, source_target_pairs={{0,1},{1,0},{2,3},{3,2},{4,5},{5,4},{6,7},{7,6},{8,9},{9,8},{10,11... | collective-permute-start | bytes 786440 | tf_op jit(solution)/shard_map/ppermute | solution.py:29
  29.0 5.6 %collective-permute-start.5 = (bf16[2,2,64,256]{3,2,1,0:T(8,128)(2,1)S(1)}, bf16[2,2,64,256]{3,2,1,0:T(8,128)(2,1)S(1)}, u32[]{:S(2)}, u32[]{:S(2)}) collective-permute-start(bf16[2,2,64,256]{3,2,1,0:T(8,128)(2,1)S(1)} %dynamic-slice_bitcast_fusion.12), channel_id=1, source_target_pairs={{0,4},{1,5},{2,6},{3,7},{4,0},{5,1},{6,2},{7,3},{8,12},{9,13},{10,... | collective-permute-start | bytes 393224 | tf_op jit(solution)/shard_map/ppermute | solution.py:29
  29.5 5.8 %collective-permute-start.1 = (bf16[2,2,64,256]{3,2,1,0:T(8,128)(2,1)S(1)}, bf16[2,2,64,256]{3,2,1,0:T(8,128)(2,1)S(1)}, u32[]{:S(2)}, u32[]{:S(2)}) collective-permute-start(bf16[2,2,64,256]{3,2,1,0:T(8,128)(2,1)S(1)} %dynamic-slice_bitcast_fusion.13), channel_id=1, source_target_pairs={{0,2},{1,3},{2,0},{3,1},{4,6},{5,7},{6,4},{7,5},{8,10},{9,11},{10,... | collective-permute-start | bytes 393224 | tf_op jit(solution)/shard_map/ppermute | solution.py:29
  34.7 5.8 %collective-permute-start.6 = (bf16[2,64,256]{2,1,0:T(8,128)(2,1)S(1)}, bf16[2,64,256]{2,1,0:T(8,128)(2,1)S(1)}, u32[]{:S(2)}, u32[]{:S(2)}) collective-permute-start(bf16[2,64,256]{2,1,0:T(8,128)(2,1)S(1)} %dynamic-slice_bitcast_fusion.20), channel_id=1, source_target_pairs={{0,8},{1,9},{2,10},{3,11},{4,12},{5,13},{6,14},{7,15},{8,0},{9,1},... | collective-permute-start | bytes 196616 | tf_op jit(solution)/shard_map/ppermute | solution.py:29
  35.4 5.2 %collective-permute-start.2 = (bf16[2,64,256]{2,1,0:T(8,128)(2,1)S(1)}, bf16[2,64,256]{2,1,0:T(8,128)(2,1)S(1)}, u32[]{:S(2)}, u32[]{:S(2)}) collective-permute-start(bf16[2,64,256]{2,1,0:T(8,128)(2,1)S(1)} %dynamic-slice_bitcast_fusion.21), channel_id=1, source_target_pairs={{0,4},{1,5},{2,6},{3,7},{4,0},{5,1},{6,2},{7,3},{8,12},{9,13},{10,... | collective-permute-start | bytes 196616 | tf_op jit(solution)/shard_map/ppermute | solution.py:29
  40.5 4.0 %collective-permute-start.7 = (bf16[64,256]{1,0:T(8,128)(2,1)S(1)}, bf16[64,256]{1,0:T(8,128)(2,1)S(1)}, u32[]{:S(2)}, u32[]{:S(2)}) collective-permute-start(bf16[64,256]{1,0:T(8,128)(2,1)S(1)} %dynamic-slice_bitcast_fusion.24), channel_id=1, source_target_pairs={{0,2},{1,3},{2,0},{3,1},{4,6},{5,7},{6,4},{7,5},{8,10},{9,11},{10,... | collective-permute-start | bytes 98312 | tf_op jit(solution)/shard_map/ppermute | solution.py:29
  40.6 5.1 %collective-permute-start.3 = (bf16[64,256]{1,0:T(8,128)(2,1)S(1)}, bf16[64,256]{1,0:T(8,128)(2,1)S(1)}, u32[]{:S(2)}, u32[]{:S(2)}) collective-permute-start(bf16[64,256]{1,0:T(8,128)(2,1)S(1)} %dynamic-slice_bitcast_fusion.25), channel_id=1, source_target_pairs={{0,8},{1,9},{2,10},{3,11},{4,12},{5,13},{6,14},{7,15},{8,0},{9,1},... | collective-permute-start | bytes 98312 | tf_op jit(solution)/shard_map/ppermute | solution.py:29
  46.3 13.7 %slice-start = ((s8[6291456]{0:T(1024)(128)(4,1)}), s8[4194304]{0:T(1024)(128)(4,1)S(1)}, s32[]{:S(2)}) async-start(s8[6291456]{0:T(1024)(128)(4,1)} %bitcast.253), calls=%async_computation.2 | async-start | bytes 8388608
  50.3 9.7 %slice-start.1 = ((s8[6291456]{0:T(1024)(128)(4,1)}), s8[2097152]{0:T(1024)(128)(4,1)S(1)}, s32[]{:S(2)}) async-start(s8[6291456]{0:T(1024)(128)(4,1)} %bitcast.253), calls=%async_computation.3 | async-start | bytes 4194304
  50.5 1.2 collective-permute-start.16
  51.7 3.5 %collective-permute-start.17 = (f32[128]{0:T(128)S(1)}, f32[128]{0:T(128)S(1)}, u32[]{:S(2)}, u32[]{:S(2)}) collective-permute-start(f32[128]{0:T(128)S(1)} %add.297), channel_id=1, source_target_pairs={{0,2},{1,3},{2,0},{3,1},{4,6},{5,7},{6,4},{7,5},{8,10},{9,11},{10,... | collective-permute-start | bytes 1544 | tf_op jit(solution)/shard_map/ppermute | solution.py:39
  54.3 10.1 %collective-permute-start.12 = (bf16[2,2,2,48,768]{4,3,2,1,0:T(8,128)(2,1)S(1)}, bf16[2,2,2,48,768]{4,3,2,1,0:T(8,128)(2,1)S(1)}, u32[]{:S(2)}, u32[]{:S(2)}) collective-permute-start(bf16[2,2,2,48,768]{4,3,2,1,0:T(8,128)(2,1)S(1)} %dynamic-slice_bitcast_fusion), channel_id=1, source_target_pairs={{0,1},{1,0},{2,3},{3,2},{4,5},{5,4},{6,7},{7,6},{8,9},{9,8},{10,11... | collective-permute-start | bytes 1769480 | tf_op jit(solution)/shard_map/ppermute | solution.py:29
  55.2 3.5 %collective-permute-start.18 = (f32[128]{0:T(128)S(1)}, f32[128]{0:T(128)S(1)}, u32[]{:S(2)}, u32[]{:S(2)}) collective-permute-start(f32[128]{0:T(128)S(1)} %add.298), channel_id=1, source_target_pairs={{0,4},{1,5},{2,6},{3,7},{4,0},{5,1},{6,2},{7,3},{8,12},{9,13},{10,... | collective-permute-start | bytes 1544 | tf_op jit(solution)/shard_map/ppermute | solution.py:39
  55.6 11.1 %collective-permute-start.8 = (bf16[2,2,2,48,768]{4,3,0,1,2:T(8,128)(2,1)S(1)}, bf16[2,2,2,48,768]{4,3,0,1,2:T(8,128)(2,1)S(1)}, u32[]{:S(2)}, u32[]{:S(2)}) collective-permute-start(bf16[2,2,2,48,768]{4,3,0,1,2:T(8,128)(2,1)S(1)} %bitcast.270), channel_id=1, source_target_pairs={{0,1},{1,0},{2,3},{3,2},{4,5},{5,4},{6,7},{7,6},{8,9},{9,8},{10,11... | collective-permute-start | bytes 1769480 | tf_op jit(solution)/shard_map/ppermute | solution.py:29
  58.8 4.4 %collective-permute-start.19 = (f32[128]{0:T(128)S(1)}, f32[128]{0:T(128)S(1)}, u32[]{:S(2)}, u32[]{:S(2)}) collective-permute-start(f32[128]{0:T(128)S(1)} %add.299), channel_id=1, source_target_pairs={{0,8},{1,9},{2,10},{3,11},{4,12},{5,13},{6,14},{7,15},{8,0},{9,1},... | collective-permute-start | bytes 1544 | tf_op jit(solution)/shard_map/ppermute | solution.py:39
  63.5 3.4 %collective-permute-start.24 = (bf16[2,2,2,48,768]{4,3,2,0,1:T(8,128)(2,1)S(1)}, bf16[2,2,2,48,768]{4,3,2,0,1:T(8,128)(2,1)S(1)}, u32[]{:S(2)}, u32[]{:S(2)}) collective-permute-start(bf16[2,2,2,48,768]{4,3,2,0,1:T(8,128)(2,1)S(1)} %bitcast.272), channel_id=1, source_target_pairs={{0,1},{1,0},{2,3},{3,2},{4,5},{5,4},{6,7},{7,6},{8,9},{9,8},{10,11... | collective-permute-start | bytes 1769480 | tf_op jit(solution)/shard_map/ppermute | solution.py:29
  63.7 3.7 %collective-permute-start.20 = (bf16[2,2,2,48,768]{4,3,0,1,2:T(8,128)(2,1)S(1)}, bf16[2,2,2,48,768]{4,3,0,1,2:T(8,128)(2,1)S(1)}, u32[]{:S(2)}, u32[]{:S(2)}) collective-permute-start(bf16[2,2,2,48,768]{4,3,0,1,2:T(8,128)(2,1)S(1)} %bitcast.271), channel_id=1, source_target_pairs={{0,1},{1,0},{2,3},{3,2},{4,5},{5,4},{6,7},{7,6},{8,9},{9,8},{10,11... | collective-permute-start | bytes 1769480 | tf_op jit(solution)/shard_map/ppermute | solution.py:29
  64.6 9.9 %collective-permute-start.13 = (bf16[2,2,48,768]{3,2,1,0:T(8,128)(2,1)S(1)}, bf16[2,2,48,768]{3,2,1,0:T(8,128)(2,1)S(1)}, u32[]{:S(2)}, u32[]{:S(2)}) collective-permute-start(bf16[2,2,48,768]{3,2,1,0:T(8,128)(2,1)S(1)} %dynamic-slice_bitcast_fusion.3), channel_id=1, source_target_pairs={{0,2},{1,3},{2,0},{3,1},{4,6},{5,7},{6,4},{7,5},{8,10},{9,11},{10,... | collective-permute-start | bytes 884744 | tf_op jit(solution)/shard_map/ppermute | solution.py:29
  66.9 14.0 %collective-permute-start.9 = (bf16[2,2,48,768]{3,2,0,1:T(8,128)(2,1)S(1)}, bf16[2,2,48,768]{3,2,0,1:T(8,128)(2,1)S(1)}, u32[]{:S(2)}, u32[]{:S(2)}) collective-permute-start(bf16[2,2,48,768]{3,2,0,1:T(8,128)(2,1)S(1)} %dynamic-slice_bitcast_fusion.4), channel_id=1, source_target_pairs={{0,2},{1,3},{2,0},{3,1},{4,6},{5,7},{6,4},{7,5},{8,10},{9,11},{10,... | collective-permute-start | bytes 884744 | tf_op jit(solution)/shard_map/ppermute | solution.py:29
  67.1 14.1 %collective-permute-start.25 = (bf16[2,2,48,768]{3,2,1,0:T(8,128)(2,1)S(1)}, bf16[2,2,48,768]{3,2,1,0:T(8,128)(2,1)S(1)}, u32[]{:S(2)}, u32[]{:S(2)}) collective-permute-start(bf16[2,2,48,768]{3,2,1,0:T(8,128)(2,1)S(1)} %dynamic-slice_bitcast_fusion.1), channel_id=1, source_target_pairs={{0,4},{1,5},{2,6},{3,7},{4,0},{5,1},{6,2},{7,3},{8,12},{9,13},{10,... | collective-permute-start | bytes 884744 | tf_op jit(solution)/shard_map/ppermute | solution.py:29
  67.6 18.9 %collective-permute-start.21 = (bf16[2,2,48,768]{3,2,0,1:T(8,128)(2,1)S(1)}, bf16[2,2,48,768]{3,2,0,1:T(8,128)(2,1)S(1)}, u32[]{:S(2)}, u32[]{:S(2)}) collective-permute-start(bf16[2,2,48,768]{3,2,0,1:T(8,128)(2,1)S(1)} %dynamic-slice_bitcast_fusion.2), channel_id=1, source_target_pairs={{0,2},{1,3},{2,0},{3,1},{4,6},{5,7},{6,4},{7,5},{8,10},{9,11},{10,... | collective-permute-start | bytes 884744 | tf_op jit(solution)/shard_map/ppermute | solution.py:29
  74.6 12.3 %collective-permute-start.14 = (bf16[2,48,768]{2,1,0:T(8,128)(2,1)S(1)}, bf16[2,48,768]{2,1,0:T(8,128)(2,1)S(1)}, u32[]{:S(2)}, u32[]{:S(2)}) collective-permute-start(bf16[2,48,768]{2,1,0:T(8,128)(2,1)S(1)} %dynamic-slice_bitcast_fusion.8), channel_id=1, source_target_pairs={{0,4},{1,5},{2,6},{3,7},{4,0},{5,1},{6,2},{7,3},{8,12},{9,13},{10,... | collective-permute-start | bytes 442376 | tf_op jit(solution)/shard_map/ppermute | solution.py:29
  80.9 7.8 %collective-permute-start.10 = (bf16[2,48,768]{2,1,0:T(8,128)(2,1)S(1)}, bf16[2,48,768]{2,1,0:T(8,128)(2,1)S(1)}, u32[]{:S(2)}, u32[]{:S(2)}) collective-permute-start(bf16[2,48,768]{2,1,0:T(8,128)(2,1)S(1)} %dynamic-slice_bitcast_fusion.9), channel_id=1, source_target_pairs={{0,4},{1,5},{2,6},{3,7},{4,0},{5,1},{6,2},{7,3},{8,12},{9,13},{10,... | collective-permute-start | bytes 442376 | tf_op jit(solution)/shard_map/ppermute | solution.py:29
  81.4 8.8 %collective-permute-start.26 = (bf16[2,48,768]{2,1,0:T(8,128)(2,1)S(1)}, bf16[2,48,768]{2,1,0:T(8,128)(2,1)S(1)}, u32[]{:S(2)}, u32[]{:S(2)}) collective-permute-start(bf16[2,48,768]{2,1,0:T(8,128)(2,1)S(1)} %dynamic-slice_bitcast_fusion.6), channel_id=1, source_target_pairs={{0,8},{1,9},{2,10},{3,11},{4,12},{5,13},{6,14},{7,15},{8,0},{9,1},... | collective-permute-start | bytes 442376 | tf_op jit(solution)/shard_map/ppermute | solution.py:29
  86.6 8.3 %collective-permute-start.22 = (bf16[2,48,768]{2,1,0:T(8,128)(2,1)S(1)}, bf16[2,48,768]{2,1,0:T(8,128)(2,1)S(1)}, u32[]{:S(2)}, u32[]{:S(2)}) collective-permute-start(bf16[2,48,768]{2,1,0:T(8,128)(2,1)S(1)} %dynamic-slice_bitcast_fusion.7), channel_id=1, source_target_pairs={{0,4},{1,5},{2,6},{3,7},{4,0},{5,1},{6,2},{7,3},{8,12},{9,13},{10,... | collective-permute-start | bytes 442376 | tf_op jit(solution)/shard_map/ppermute | solution.py:29
  87.0 8.1 %collective-permute-start.15 = (bf16[48,768]{1,0:T(8,128)(2,1)S(1)}, bf16[48,768]{1,0:T(8,128)(2,1)S(1)}, u32[]{:S(2)}, u32[]{:S(2)}) collective-permute-start(bf16[48,768]{1,0:T(8,128)(2,1)S(1)} %dynamic-slice_bitcast_fusion.16), channel_id=1, source_target_pairs={{0,8},{1,9},{2,10},{3,11},{4,12},{5,13},{6,14},{7,15},{8,0},{9,1},... | collective-permute-start | bytes 221192 | tf_op jit(solution)/shard_map/ppermute | solution.py:29
  88.8 8.5 %collective-permute-start.11 = (bf16[48,768]{1,0:T(8,128)(2,1)S(1)}, bf16[48,768]{1,0:T(8,128)(2,1)S(1)}, u32[]{:S(2)}, u32[]{:S(2)}) collective-permute-start(bf16[48,768]{1,0:T(8,128)(2,1)S(1)} %dynamic-slice_bitcast_fusion.17), channel_id=1, source_target_pairs={{0,8},{1,9},{2,10},{3,11},{4,12},{5,13},{6,14},{7,15},{8,0},{9,1},... | collective-permute-start | bytes 221192 | tf_op jit(solution)/shard_map/ppermute | solution.py:29
  90.2 7.1 %collective-permute-start.27 = (bf16[48,768]{1,0:T(8,128)(2,1)S(1)}, bf16[48,768]{1,0:T(8,128)(2,1)S(1)}, u32[]{:S(2)}, u32[]{:S(2)}) collective-permute-start(bf16[48,768]{1,0:T(8,128)(2,1)S(1)} %dynamic-slice_bitcast_fusion.14), channel_id=1, source_target_pairs={{0,2},{1,3},{2,0},{3,1},{4,6},{5,7},{6,4},{7,5},{8,10},{9,11},{10,... | collective-permute-start | bytes 221192 | tf_op jit(solution)/shard_map/ppermute | solution.py:29
  95.0 7.2 %collective-permute-start.23 = (bf16[48,768]{1,0:T(8,128)(2,1)S(1)}, bf16[48,768]{1,0:T(8,128)(2,1)S(1)}, u32[]{:S(2)}, u32[]{:S(2)}) collective-permute-start(bf16[48,768]{1,0:T(8,128)(2,1)S(1)} %dynamic-slice_bitcast_fusion.15), channel_id=1, source_target_pairs={{0,8},{1,9},{2,10},{3,11},{4,12},{5,13},{6,14},{7,15},{8,0},{9,1},... | collective-permute-start | bytes 221192 | tf_op jit(solution)/shard_map/ppermute | solution.py:29
  97.4 11.7 %all-to-all-start.1 = ((bf16[16,8,256]{2,1,0:T(8,128)(2,1)}), bf16[16,8,256]{2,1,0:T(8,128)(2,1)S(1)}, u32[]{:S(2)}, u32[]{:S(2)}) async-start(bf16[16,8,256]{2,1,0:T(8,128)(2,1)} %bitcast.72), calls=%async_computation.1 | async-start | bytes 131072 | tf_op jit(solution)/shard_map/all_to_all | solution.py:183
  113.4 1.6 %collective-permute-start.32 = (bf16[2,2,2,8,2048]{4,3,2,0,1:T(8,128)(2,1)S(1)}, bf16[2,2,2,8,2048]{4,3,2,0,1:T(8,128)(2,1)S(1)}, u32[]{:S(2)}, u32[]{:S(2)}) collective-permute-start(bf16[2,2,2,8,2048]{4,3,2,0,1:T(8,128)(2,1)S(1)} %bitcast.276), channel_id=1, source_target_pairs={{0,1},{1,0},{2,3},{3,2},{4,5},{5,4},{6,7},{7,6},{8,9},{9,8},{10,11... | collective-permute-start | bytes 786440 | tf_op jit(solution)/shard_map/ppermute | solution.py:29
  114.1 1.7 %collective-permute-start.28 = (bf16[2,2,2,8,2048]{4,3,0,1,2:T(8,128)(2,1)S(1)}, bf16[2,2,2,8,2048]{4,3,0,1,2:T(8,128)(2,1)S(1)}, u32[]{:S(2)}, u32[]{:S(2)}) collective-permute-start(bf16[2,2,2,8,2048]{4,3,0,1,2:T(8,128)(2,1)S(1)} %bitcast.275), channel_id=1, source_target_pairs={{0,1},{1,0},{2,3},{3,2},{4,5},{5,4},{6,7},{7,6},{8,9},{9,8},{10,11... | collective-permute-start | bytes 786440 | tf_op jit(solution)/shard_map/ppermute | solution.py:29
  115.0 5.6 %collective-permute-start.33 = (bf16[2,2,8,2048]{3,2,1,0:T(8,128)(2,1)S(1)}, bf16[2,2,8,2048]{3,2,1,0:T(8,128)(2,1)S(1)}, u32[]{:S(2)}, u32[]{:S(2)}) collective-permute-start(bf16[2,2,8,2048]{3,2,1,0:T(8,128)(2,1)S(1)} %dynamic-slice_bitcast_fusion.10), channel_id=1, source_target_pairs={{0,4},{1,5},{2,6},{3,7},{4,0},{5,1},{6,2},{7,3},{8,12},{9,13},{10,... | collective-permute-start | bytes 393224 | tf_op jit(solution)/shard_map/ppermute | solution.py:29
  115.9 5.8 %collective-permute-start.29 = (bf16[2,2,8,2048]{3,2,0,1:T(8,128)(2,1)S(1)}, bf16[2,2,8,2048]{3,2,0,1:T(8,128)(2,1)S(1)}, u32[]{:S(2)}, u32[]{:S(2)}) collective-permute-start(bf16[2,2,8,2048]{3,2,0,1:T(8,128)(2,1)S(1)} %dynamic-slice_bitcast_fusion.11), channel_id=1, source_target_pairs={{0,2},{1,3},{2,0},{3,1},{4,6},{5,7},{6,4},{7,5},{8,10},{9,11},{10,... | collective-permute-start | bytes 393224 | tf_op jit(solution)/shard_map/ppermute | solution.py:29
  120.7 5.8 %collective-permute-start.34 = (bf16[2,8,2048]{2,1,0:T(8,128)(2,1)S(1)}, bf16[2,8,2048]{2,1,0:T(8,128)(2,1)S(1)}, u32[]{:S(2)}, u32[]{:S(2)}) collective-permute-start(bf16[2,8,2048]{2,1,0:T(8,128)(2,1)S(1)} %dynamic-slice_bitcast_fusion.18), channel_id=1, source_target_pairs={{0,8},{1,9},{2,10},{3,11},{4,12},{5,13},{6,14},{7,15},{8,0},{9,1},... | collective-permute-start | bytes 196616 | tf_op jit(solution)/shard_map/ppermute | solution.py:29
  121.8 5.1 %collective-permute-start.30 = (bf16[2,8,2048]{2,1,0:T(8,128)(2,1)S(1)}, bf16[2,8,2048]{2,1,0:T(8,128)(2,1)S(1)}, u32[]{:S(2)}, u32[]{:S(2)}) collective-permute-start(bf16[2,8,2048]{2,1,0:T(8,128)(2,1)S(1)} %dynamic-slice_bitcast_fusion.19), channel_id=1, source_target_pairs={{0,4},{1,5},{2,6},{3,7},{4,0},{5,1},{6,2},{7,3},{8,12},{9,13},{10,... | collective-permute-start | bytes 196616 | tf_op jit(solution)/shard_map/ppermute | solution.py:29
  126.6 4.0 %collective-permute-start.35 = (bf16[8,2048]{1,0:T(8,128)(2,1)S(1)}, bf16[8,2048]{1,0:T(8,128)(2,1)S(1)}, u32[]{:S(2)}, u32[]{:S(2)}) collective-permute-start(bf16[8,2048]{1,0:T(8,128)(2,1)S(1)} %dynamic-slice_bitcast_fusion.22), channel_id=1, source_target_pairs={{0,2},{1,3},{2,0},{3,1},{4,6},{5,7},{6,4},{7,5},{8,10},{9,11},{10,... | collective-permute-start | bytes 98312 | tf_op jit(solution)/shard_map/ppermute | solution.py:29
  127.0 4.9 %collective-permute-start.31 = (bf16[8,2048]{1,0:T(8,128)(2,1)S(1)}, bf16[8,2048]{1,0:T(8,128)(2,1)S(1)}, u32[]{:S(2)}, u32[]{:S(2)}) collective-permute-start(bf16[8,2048]{1,0:T(8,128)(2,1)S(1)} %dynamic-slice_bitcast_fusion.23), channel_id=1, source_target_pairs={{0,8},{1,9},{2,10},{3,11},{4,12},{5,13},{6,14},{7,15},{8,0},{9,1},... | collective-permute-start | bytes 98312 | tf_op jit(solution)/shard_map/ppermute | solution.py:29

commit v6 on v5

--- a/solution.py
+++ b/solution.py
@@ -12,7 +12,7 @@
 BF16 = jnp.bfloat16
 
 
-def scatter_sum(x, axis_name, order):
+def scatter_sum(x, axis_name, order, trail=None):
     count = x.shape[0]
     bits = count.bit_length() - 1
     if bits == 0:
@@ -28,6 +28,8 @@
         send = lax.dynamic_index_in_dim(x, 1 - mine, at, keepdims=False)
         got = lax.ppermute(send, axis_name, [(i, i ^ (1 << bit)) for i in range(count)])
         x = (keep.astype(F32) + got.astype(F32)).astype(BF16)
+        if trail is not None:
+            trail.append(x)
     return x
 
 
@@ -48,12 +50,12 @@
     return [0] + list(range(2, bits)) + [1] if bits > 2 else list(range(bits))
 
 
-def scatter_both(x, order):
+def scatter_both(x, order, trail=None):
     if x.shape[1] > 1:
         x = scatter_sum(jnp.moveaxis(x, 1, 0), "dp", near_first)
     else:
         x = x[:, 0]
-    return scatter_sum(x, "expert", order)
+    return scatter_sum(x, "expert", order, trail)
 
 
 def attend(queries, token_keys, token_values, key_rows, value_rows, lengths):
@@ -170,13 +172,17 @@
         gate, chosen = lax.optimization_barrier((gate, chosen))
         up, total = lax.optimization_barrier((project(chosen, up_update), total))
         last = scatter_both(up[:, :, cut:], far_first)
-        gate = [scatter_both(part, near_first) for part in (gate[:, :, :cut], gate[:, :, cut:])]
+        trail = []
+        gate = [
+            scatter_both(gate[:, :, :cut], near_first, trail),
+            scatter_both(gate[:, :, cut:], near_first),
+        ]
         up = [scatter_both(up[:, :, :cut], near_first), last]
-        return jnp.concatenate(gate, axis=0), jnp.concatenate(up, axis=0), total, last
+        return jnp.concatenate(gate, axis=0), jnp.concatenate(up, axis=0), total, trail[0]
 
     if slots <= 128:
-        gate, up, square, last = both(chosen, square)
-        columns, last = lax.optimization_barrier((columns, last))
+        gate, up, square, early = both(chosen, square)
+        columns, early = lax.optimization_barrier((columns, early))
     else:
         parts = chosen.reshape(experts, -1, 128, depth).swapaxes(0, 1)
         gate, up = lax.map(lambda part: both(part, square)[:2], parts)

time: 133 us -> 132 us (level)
  waiting for transfers between devices: 66 us -> 52.6 us
  starting transfers between devices: 36.9 us -> 43.3 us
  local copies, waits for them, and re-layouts: 9.01 us -> 12.9 us
  other arithmetic: 4.74 us -> 6.61 us
    ppermute x32, starting transfers between devices: 21.2 us -> 28.1 us  [scatter_sum(): lax.ppermute(send, axis_name, [(i, i ^ 1 << bit) for i in range(count)])]
    all_to_all x1, waiting for transfers between devices: 6.83 us -> 0.01 us  [shards(): lax.all_to_all(columns, 'expert', split_axis=0, concat_axis=1, tiled=True)]
    ppermute x32, waiting for transfers between devices: 45.6 us -> 39.1 us  [scatter_sum(): lax.ppermute(send, axis_name, [(i, i ^ 1 << bit) for i in range(count)])]
    convert_element_type x32, other arithmetic: 1.69 us -> 3.57 us  [scatter_sum(): x = (keep.astype(F32) + got.astype(F32)).astype(BF16)]
    dynamic_slice x6, local copies, waits for them, and re-layouts: 0.18 us -> 1.83 us  [scatter_sum(): send = lax.dynamic_index_in_dim(x, 1 - mine, at, keepdims=False)]
    squeeze x26, local copies, waits for them, and re-layouts: 0.5 us -> 1.94 us  [scatter_sum(): send = lax.dynamic_index_in_dim(x, 1 - mine, at, keepdims=False)]
  transfers between devices with their start and end apart: 38 -> 38, of which waited for: 25 -> 23; matrix products, arithmetic and copies ran while one was open for 6% -> 10% of each run, Pallas kernels for 0% -> 0%
where the time goes in v6:
time: 132 us; the launch traced here: 131 us
  waiting for transfers between devices  52.6 us (40%)
  starting transfers between devices  43.3 us (33%)
  matrix products  14.3 us (11%)
  local copies, waits for them, and re-layouts  12.9 us (10%)
  other arithmetic  6.61 us (5%)
  between operations  1.58 us (1%)
    ppermute x32, waiting for transfers between devices, scatter_sum(): lax.ppermute(send, axis_name, [(i, i ^ 1 << bit) for i in range(count)])  39.1 us
    ppermute x32, starting transfers between devices, scatter_sum(): lax.ppermute(send, axis_name, [(i, i ^ 1 << bit) for i in range(count)])  28.1 us
    all_to_all x1, starting transfers between devices, shards(): lax.all_to_all(packed.reshape(own, -1), 'expert', split_axis=1, concat_ax...  7.39 us
    ppermute x4, waiting for transfers between devices, add_up(): x = x + lax.ppermute(x, 'expert', [(i, i ^ 1 << bit) for i in range(count)])  7.17 us
    all_to_all x1, waiting for transfers between devices, shards(): lax.all_to_all(packed.reshape(own, -1), 'expert', split_axis=1, concat_ax...  6.41 us
    dot_general x2, matrix products, project(): jnp.einsum('esd,edf->esf', chosen, weight, preferred_element_type=F32)  5.13 us
    all_to_all x1, starting transfers between devices, shards(): lax.all_to_all(columns, 'expert', split_axis=0, concat_axis=1, tiled=True)  4.34 us
    dot_general x1, matrix products, shards(): jnp.dot(hidden, down_weight[0], preferred_element_type=F32).astype(BF16)  4.04 us
  transfers between devices with their start and end apart: 38, of which 23 were waited for; matrix products, arithmetic and copies ran while one was open for 10% of the time, Pallas kernels for 0%

profile of v6, /device:TPU:0, one launch (start us, length us, event | category | flops | bytes accessed | tf_op | source)
XLA Modules:
  0.0 131.4 jit_solution(1013251842264943582)
XLA Ops:
  0.7 0.9 select_reduce_fusion.2
  1.6 1.8 %reshape_squeeze.36 = bf16[4,192,4,128]{3,2,1,0:T(4,128)(2,1)S(1)} reshape(bf16[1,4,192,512]{3,2,1,0:T(8,128)(2,1)} %param.24) | data formatting | bytes 1572864 | tf_op jit(solution)/shard_map/reshape;squeeze | solution.py:67
  3.8 0.7 fusion.87
  6.3 0.7 copy.107
  7.0 7.4 %all-to-all-start = ((bf16[8,16,640]{2,0,1:T(8,128)(2,1)}), bf16[8,16,640]{2,0,1:T(8,128)(2,1)S(1)}, u32[]{:S(2)}, u32[]{:S(2)}) async-start(bf16[8,16,640]{2,0,1:T(8,128)(2,1)} %copy.107), calls=%async_computation | async-start | bytes 327680 | tf_op jit(solution)/shard_map/all_to_all | solution.py:123
  14.8 0.7 copy.142
  15.7 0.8 dynamic_slice.237
  16.4 6.4 %all-to-all-done = bf16[8,16,640]{2,0,1:T(8,128)(2,1)S(1)} async-done(((bf16[8,16,640]{2,0,1:T(8,128)(2,1)}), bf16[8,16,640]{2,0,1:T(8,128)(2,1)S(1)}, u32[]{:S(2)}, u32[]{:S(2)}) %all-to-all-start) | async-done | bytes 163872 | tf_op jit(solution)/shard_map/all_to_all | solution.py:123
  23.1 2.9 %fusion.52 = f32[128,4096]{1,0:T(8,128)S(1)} fusion(bf16[512,4096]{1,0:T(8,128)(2,1)} %param.17, bf16[128,640]{1,0:T(8,128)(2,1)S(1)} %bitcast.269), kind=kOutput, calls=%fused_computation.108 | convolution fusion | flops 536870912 | bytes 6422528 | tf_op jit(solution)/shard_map/dot_general | solution.py:132
  26.0 0.7 copy.141
  27.7 0.5 collective-permute-start
  29.8 4.8 %collective-permute-done.5 = bf16[2,2,64,256]{3,2,1,0:T(8,128)(2,1)S(1)} collective-permute-done((bf16[2,2,64,256]{3,2,1,0:T(8,128)(2,1)S(1)}, bf16[2,2,64,256]{3,2,1,0:T(8,128)(2,1)S(1)}, u32[]{:S(2)}, u32[]{:S(2)}) %collective-permute-start.5) | collective-permute-done | bytes 131104 | tf_op jit(solution)/shard_map/ppermute | solution.py:29
  34.7 0.6 collective-permute-start.6
  35.4 1.2 collective-permute-start.2
  36.6 3.8 %collective-permute-done.6 = bf16[2,64,256]{2,1,0:T(8,128)(2,1)S(1)} collective-permute-done((bf16[2,64,256]{2,1,0:T(8,128)(2,1)S(1)}, bf16[2,64,256]{2,1,0:T(8,128)(2,1)S(1)}, u32[]{:S(2)}, u32[]{:S(2)}) %collective-permute-start.6) | collective-permute-done | bytes 65568 | tf_op jit(solution)/shard_map/ppermute | solution.py:29
  40.6 1.5 %collective-permute-start.3 = (bf16[64,256]{1,0:T(8,128)(2,1)S(1)}, bf16[64,256]{1,0:T(8,128)(2,1)S(1)}, u32[]{:S(2)}, u32[]{:S(2)}) collective-permute-start(bf16[64,256]{1,0:T(8,128)(2,1)S(1)} %dynamic-slice_bitcast_fusion.25), channel_id=1, source_target_pairs={{0,8},{1,9},{2,10},{3,11},{4,12},{5,13},{6,14},{7,15},{8,0},{9,1},... | collective-permute-start | bytes 98312 | tf_op jit(solution)/shard_map/ppermute | solution.py:29
  42.2 2.3 %collective-permute-done.7 = bf16[64,256]{1,0:T(8,128)(2,1)S(1)} collective-permute-done((bf16[64,256]{1,0:T(8,128)(2,1)S(1)}, bf16[64,256]{1,0:T(8,128)(2,1)S(1)}, u32[]{:S(2)}, u32[]{:S(2)}) %collective-permute-start.7) | collective-permute-done | bytes 32800 | tf_op jit(solution)/shard_map/ppermute | solution.py:29
  44.5 1.3 collective-permute-done.3
  46.3 4.0 %convert_bitcast_fusion.1 = bf16[16,1,96,768]{3,2,0,1:T(8,128)(2,1)S(1)} fusion(bf16[16,96,256]{2,1,0:T(8,128)(2,1)S(1)} %convolution_convert_fusion, bf16[16,256,768]{2,1,0:T(8,128)(2,1)} %param.14), kind=kOutput, calls=%fused_computation.5 | convolution fusion | flops 605159424 | bytes 9437184 | tf_op jit(solution)/shard_map/esd,edf->esf/dot_general | solution.py:166
  50.6 1.1 collective-permute-done.16
  51.7 2.0 %collective-permute-start.17 = (f32[128]{0:T(128)S(1)}, f32[128]{0:T(128)S(1)}, u32[]{:S(2)}, u32[]{:S(2)}) collective-permute-start(f32[128]{0:T(128)S(1)} %add.297), channel_id=1, source_target_pairs={{0,2},{1,3},{2,0},{3,1},{4,6},{5,7},{6,4},{7,5},{8,10},{9,11},{10,... | collective-permute-start | bytes 1544 | tf_op jit(solution)/shard_map/ppermute | solution.py:41
  53.7 0.6 pad_maximum_fusion.3
  54.3 0.9 collective-permute-done.17
  55.7 3.1 %collective-permute-done.18 = f32[128]{0:T(128)S(1)} collective-permute-done((f32[128]{0:T(128)S(1)}, f32[128]{0:T(128)S(1)}, u32[]{:S(2)}, u32[]{:S(2)}) %collective-permute-start.18) | collective-permute-done | bytes 544 | tf_op jit(solution)/shard_map/ppermute | solution.py:41
  58.8 1.2 collective-permute-start.19
  60.0 1.1 convert_bitcast_fusion
  61.1 2.1 %collective-permute-done.19 = f32[128]{0:T(128)S(1)} collective-permute-done((f32[128]{0:T(128)S(1)}, f32[128]{0:T(128)S(1)}, u32[]{:S(2)}, u32[]{:S(2)}) %collective-permute-start.19) | collective-permute-done | bytes 544 | tf_op jit(solution)/shard_map/ppermute | solution.py:41
  63.5 0.8 copy.187
  64.4 0.9 copy.188
  65.3 0.5 collective-permute-start.20
  66.1 0.7 dynamic-slice_bitcast_fusion.3
  66.8 2.0 %collective-permute-start.13 = (bf16[2,2,48,768]{3,2,1,0:T(8,128)(2,1)}, bf16[2,2,48,768]{3,2,1,0:T(8,128)(2,1)}, u32[]{:S(2)}, u32[]{:S(2)}) collective-permute-start(bf16[2,2,48,768]{3,2,1,0:T(8,128)(2,1)} %dynamic-slice_bitcast_fusion.3), channel_id=1, source_target_pairs={{0,2},{1,3},{2,0},{3,1},{4,6},{5,7},{6,4},{7,5},{8,10},{9,11},{10,... | collective-permute-start | bytes 884744 | tf_op jit(solution)/shard_map/ppermute | solution.py:29
  69.0 0.7 dynamic-slice_bitcast_fusion.4
  69.8 4.3 %all-to-all-start.1 = ((bf16[16,8,256]{2,1,0:T(8,128)(2,1)}), bf16[16,8,256]{2,1,0:T(8,128)(2,1)}, u32[]{:S(2)}, u32[]{:S(2)}) async-start(bf16[16,8,256]{2,1,0:T(8,128)(2,1)} %bitcast.275), calls=%async_computation.1 | async-start | bytes 131072 | tf_op jit(solution)/shard_map/all_to_all | solution.py:189
  74.3 1.8 %collective-permute-start.25 = (bf16[2,2,48,768]{3,2,1,0:T(8,128)(2,1)S(1)}, bf16[2,2,48,768]{3,2,1,0:T(8,128)(2,1)S(1)}, u32[]{:S(2)}, u32[]{:S(2)}) collective-permute-start(bf16[2,2,48,768]{3,2,1,0:T(8,128)(2,1)S(1)} %dynamic-slice_bitcast_fusion.1), channel_id=1, source_target_pairs={{0,4},{1,5},{2,6},{3,7},{4,0},{5,1},{6,2},{7,3},{8,12},{9,13},{10,... | collective-permute-start | bytes 884744 | tf_op jit(solution)/shard_map/ppermute | solution.py:29
  76.3 1.5 %collective-permute-start.21 = (bf16[2,2,48,768]{3,2,0,1:T(8,128)(2,1)S(1)}, bf16[2,2,48,768]{3,2,0,1:T(8,128)(2,1)S(1)}, u32[]{:S(2)}, u32[]{:S(2)}) collective-permute-start(bf16[2,2,48,768]{3,2,0,1:T(8,128)(2,1)S(1)} %dynamic-slice_bitcast_fusion.2), channel_id=1, source_target_pairs={{0,2},{1,3},{2,0},{3,1},{4,6},{5,7},{6,4},{7,5},{8,10},{9,11},{10,... | collective-permute-start | bytes 884744 | tf_op jit(solution)/shard_map/ppermute | solution.py:29
  77.9 1.0 fusion.23
  78.9 0.7 collective-permute-start.14
  79.7 4.2 %collective-permute-done.9 = bf16[2,2,48,768]{3,2,0,1:T(8,128)(2,1)} collective-permute-done((bf16[2,2,48,768]{3,2,0,1:T(8,128)(2,1)}, bf16[2,2,48,768]{3,2,0,1:T(8,128)(2,1)}, u32[]{:S(2)}, u32[]{:S(2)}) %collective-permute-start.9) | collective-permute-done | bytes 294944 | tf_op jit(solution)/shard_map/ppermute | solution.py:29
  83.8 1.0 fusion.24
  85.3 2.2 %collective-permute-start.26 = (bf16[2,48,768]{2,1,0:T(8,128)(2,1)S(1)}, bf16[2,48,768]{2,1,0:T(8,128)(2,1)S(1)}, u32[]{:S(2)}, u32[]{:S(2)}) collective-permute-start(bf16[2,48,768]{2,1,0:T(8,128)(2,1)S(1)} %dynamic-slice_bitcast_fusion.6), channel_id=1, source_target_pairs={{0,8},{1,9},{2,10},{3,11},{4,12},{5,13},{6,14},{7,15},{8,0},{9,1},... | collective-permute-start | bytes 442376 | tf_op jit(solution)/shard_map/ppermute | solution.py:29
  87.5 2.1 %collective-permute-done.21 = bf16[2,2,48,768]{3,2,0,1:T(8,128)(2,1)S(1)} collective-permute-done((bf16[2,2,48,768]{3,2,0,1:T(8,128)(2,1)S(1)}, bf16[2,2,48,768]{3,2,0,1:T(8,128)(2,1)S(1)}, u32[]{:S(2)}, u32[]{:S(2)}) %collective-permute-start.21) | collective-permute-done | bytes 294944 | tf_op jit(solution)/shard_map/ppermute | solution.py:29
  90.1 1.7 %collective-permute-start.15 = (bf16[48,768]{1,0:T(8,128)(2,1)S(1)}, bf16[48,768]{1,0:T(8,128)(2,1)S(1)}, u32[]{:S(2)}, u32[]{:S(2)}) collective-permute-start(bf16[48,768]{1,0:T(8,128)(2,1)S(1)} %dynamic-slice_bitcast_fusion.16), channel_id=1, source_target_pairs={{0,8},{1,9},{2,10},{3,11},{4,12},{5,13},{6,14},{7,15},{8,0},{9,1},... | collective-permute-start | bytes 221192 | tf_op jit(solution)/shard_map/ppermute | solution.py:29
  91.8 2.8 %collective-permute-done.10 = bf16[2,48,768]{2,1,0:T(8,128)(2,1)S(1)} collective-permute-done((bf16[2,48,768]{2,1,0:T(8,128)(2,1)S(1)}, bf16[2,48,768]{2,1,0:T(8,128)(2,1)S(1)}, u32[]{:S(2)}, u32[]{:S(2)}) %collective-permute-start.10) | collective-permute-done | bytes 147488 | tf_op jit(solution)/shard_map/ppermute | solution.py:29
  94.7 0.5 collective-permute-start.11
  95.3 2.0 %collective-permute-start.27 = (bf16[48,768]{1,0:T(8,128)(2,1)S(1)}, bf16[48,768]{1,0:T(8,128)(2,1)S(1)}, u32[]{:S(2)}, u32[]{:S(2)}) collective-permute-start(bf16[48,768]{1,0:T(8,128)(2,1)S(1)} %dynamic-slice_bitcast_fusion.14), channel_id=1, source_target_pairs={{0,2},{1,3},{2,0},{3,1},{4,6},{5,7},{6,4},{7,5},{8,10},{9,11},{10,... | collective-permute-start | bytes 221192 | tf_op jit(solution)/shard_map/ppermute | solution.py:29
  97.3 2.4 %collective-permute-done.22 = bf16[2,48,768]{2,1,0:T(8,128)(2,1)S(1)} collective-permute-done((bf16[2,48,768]{2,1,0:T(8,128)(2,1)S(1)}, bf16[2,48,768]{2,1,0:T(8,128)(2,1)S(1)}, u32[]{:S(2)}, u32[]{:S(2)}) %collective-permute-start.22) | collective-permute-done | bytes 147488 | tf_op jit(solution)/shard_map/ppermute | solution.py:29
  99.8 0.5 collective-permute-start.23
  100.3 3.8 %collective-permute-done.11 = bf16[48,768]{1,0:T(8,128)(2,1)S(1)} collective-permute-done((bf16[48,768]{1,0:T(8,128)(2,1)S(1)}, bf16[48,768]{1,0:T(8,128)(2,1)S(1)}, u32[]{:S(2)}, u32[]{:S(2)}) %collective-permute-start.11) | collective-permute-done | bytes 73760 | tf_op jit(solution)/shard_map/ppermute | solution.py:29
  104.1 1.0 collective-permute-done.23
  105.2 4.0 %fusion.5 = bf16[16,1,8,4096]{3,2,0,1:T(8,128)(2,1)S(1)} fusion(bf16[1,768,4096]{2,1,0:T(8,128)(2,1)} %param.16, bf16[96,768]{1,0:T(8,128)(2,1)S(1)} %pad_maximum_fusion.2, bf16[96,768]{1,0:T(8,128)(2,1)S(1)} %pad_maximum_fusion.1, f32[96]{0:T(128)S(1)} %get-tuple-element.19, f32[96]{0:T(128)S(1)} %get-tuple-element.18, pred[16,96,128]{2,1,0:T(32,128)(4,1)} %copy-done.1, ...), kind=kOutput, calls=%fused_computation.3 | convolution fusion | flops 825614336 | bytes 7648004 | tf_op jit(solution)/shard_map/dot_general | solution.py:202
  109.6 1.5 %reshape.179 = bf16[2,1,4,4096]{3,2,1,0:T(4,128)(2,1)} reshape(bf16[8,4096]{1,0:T(8,128)(2,1)} %bitcast.74) | data formatting | bytes 131072 | tf_op jit(solution)/shard_map/reshape | solution.py:192
  111.1 0.6 collective-permute-start.28
  111.8 1.5 %collective-permute-start.33 = (bf16[2,2,8,2048]{3,2,1,0:T(8,128)(2,1)S(1)}, bf16[2,2,8,2048]{3,2,1,0:T(8,128)(2,1)S(1)}, u32[]{:S(2)}, u32[]{:S(2)}) collective-permute-start(bf16[2,2,8,2048]{3,2,1,0:T(8,128)(2,1)S(1)} %dynamic-slice_bitcast_fusion.10), channel_id=1, source_target_pairs={{0,4},{1,5},{2,6},{3,7},{4,0},{5,1},{6,2},{7,3},{8,12},{9,13},{10,... | collective-permute-start | bytes 393224 | tf_op jit(solution)/shard_map/ppermute | solution.py:29
  113.4 2.1 %collective-permute-start.29 = (bf16[2,2,8,2048]{3,2,0,1:T(8,128)(2,1)S(1)}, bf16[2,2,8,2048]{3,2,0,1:T(8,128)(2,1)S(1)}, u32[]{:S(2)}, u32[]{:S(2)}) collective-permute-start(bf16[2,2,8,2048]{3,2,0,1:T(8,128)(2,1)S(1)} %dynamic-slice_bitcast_fusion.11), channel_id=1, source_target_pairs={{0,2},{1,3},{2,0},{3,1},{4,6},{5,7},{6,4},{7,5},{8,10},{9,11},{10,... | collective-permute-start | bytes 393224 | tf_op jit(solution)/shard_map/ppermute | solution.py:29
  115.4 1.9 %collective-permute-done.33 = bf16[2,2,8,2048]{3,2,1,0:T(8,128)(2,1)S(1)} collective-permute-done((bf16[2,2,8,2048]{3,2,1,0:T(8,128)(2,1)S(1)}, bf16[2,2,8,2048]{3,2,1,0:T(8,128)(2,1)S(1)}, u32[]{:S(2)}, u32[]{:S(2)}) %collective-permute-start.33) | collective-permute-done | bytes 131104 | tf_op jit(solution)/shard_map/ppermute | solution.py:29
  117.3 1.1 collective-permute-start.34
  118.5 1.0 collective-permute-done.29
  119.5 0.8 collective-permute-start.30
  120.4 2.3 %collective-permute-done.34 = bf16[2,8,2048]{2,1,0:T(8,128)(2,1)S(1)} collective-permute-done((bf16[2,8,2048]{2,1,0:T(8,128)(2,1)S(1)}, bf16[2,8,2048]{2,1,0:T(8,128)(2,1)S(1)}, u32[]{:S(2)}, u32[]{:S(2)}) %collective-permute-start.34) | collective-permute-done | bytes 65568 | tf_op jit(solution)/shard_map/ppermute | solution.py:29
  122.7 3.0 %collective-permute-start.35 = (bf16[8,2048]{1,0:T(8,128)(2,1)S(1)}, bf16[8,2048]{1,0:T(8,128)(2,1)S(1)}, u32[]{:S(2)}, u32[]{:S(2)}) collective-permute-start(bf16[8,2048]{1,0:T(8,128)(2,1)S(1)} %dynamic-slice_bitcast_fusion.22), channel_id=1, source_target_pairs={{0,2},{1,3},{2,0},{3,1},{4,6},{5,7},{6,4},{7,5},{8,10},{9,11},{10,... | collective-permute-start | bytes 98312 | tf_op jit(solution)/shard_map/ppermute | solution.py:29
  126.0 1.6 %collective-permute-done.35 = bf16[8,2048]{1,0:T(8,128)(2,1)S(1)} collective-permute-done((bf16[8,2048]{1,0:T(8,128)(2,1)S(1)}, bf16[8,2048]{1,0:T(8,128)(2,1)S(1)}, u32[]{:S(2)}, u32[]{:S(2)}) %collective-permute-start.35) | collective-permute-done | bytes 32800 | tf_op jit(solution)/shard_map/ppermute | solution.py:29
  127.6 3.1 %collective-permute-done.31 = bf16[8,2048]{1,0:T(8,128)(2,1)S(1)} collective-permute-done((bf16[8,2048]{1,0:T(8,128)(2,1)S(1)}, bf16[8,2048]{1,0:T(8,128)(2,1)S(1)}, u32[]{:S(2)}, u32[]{:S(2)}) %collective-permute-start.31) | collective-permute-done | bytes 32800 | tf_op jit(solution)/shard_map/ppermute | solution.py:29
  130.7 0.7 reshape.180
  (166 shorter events, 10.2 us)
Async XLA Ops:
  0.6 2.7 %copy-start = (bf16[1,4,192,512]{3,2,1,0:T(8,128)(2,1)S(1)}, bf16[1,4,192,512]{3,2,1,0:T(8,128)(2,1)}, u32[]{:S(2)}) copy-start(bf16[1,4,192,512]{3,2,1,0:T(8,128)(2,1)} %param.23) | copy-start | bytes 2359300
  0.6 2.9 %copy-start.2 = (bf16[2,1,4,8192]{3,2,1,0:T(4,128)(2,1)S(1)}, bf16[2,1,4,8192]{3,2,1,0:T(4,128)(2,1)}, u32[]{:S(2)}) copy-start(bf16[2,1,4,8192]{3,2,1,0:T(4,128)(2,1)} %param.20) | copy-start | bytes 393220
  0.7 3.1 %copy-start.6 = (s32[1,4]{1,0:T(1,128)S(1)}, s32[1,4]{1,0:T(1,128)}, u32[]{:S(2)}) copy-start(s32[1,4]{1,0:T(1,128)} %param.25) | copy-start | bytes 52
  0.7 3.1 %copy-start.4 = (bf16[2,1,4,512]{3,2,1,0:T(4,128)(2,1)S(1)}, bf16[2,1,4,512]{3,2,1,0:T(4,128)(2,1)}, u32[]{:S(2)}) copy-start(bf16[2,1,4,512]{3,2,1,0:T(4,128)(2,1)} %param.21) | copy-start | bytes 24580
  3.3 2.0 %copy-start.5 = (bf16[2,1,4,512]{3,2,1,0:T(4,128)(2,1)S(1)}, bf16[2,1,4,512]{3,2,1,0:T(4,128)(2,1)}, u32[]{:S(2)}) copy-start(bf16[2,1,4,512]{3,2,1,0:T(4,128)(2,1)} %param.22) | copy-start | bytes 24580
  5.4 9.2 %copy-start.3 = (bf16[2,1,4,4096]{3,2,1,0:T(4,128)(2,1)S(1)}, bf16[2,1,4,4096]{3,2,1,0:T(4,128)(2,1)}, u32[]{:S(2)}) copy-start(bf16[2,1,4,4096]{3,2,1,0:T(4,128)(2,1)} %param.19) | copy-start | bytes 196612
  7.0 15.9 %all-to-all-start = ((bf16[8,16,640]{2,0,1:T(8,128)(2,1)}), bf16[8,16,640]{2,0,1:T(8,128)(2,1)S(1)}, u32[]{:S(2)}, u32[]{:S(2)}) async-start(bf16[8,16,640]{2,0,1:T(8,128)(2,1)} %copy.107), calls=%async_computation | async-start | bytes 327680 | tf_op jit(solution)/shard_map/all_to_all | solution.py:123
  27.3 1.6 %collective-permute-start.4 = (bf16[2,2,2,64,256]{4,3,2,0,1:T(8,128)(2,1)S(1)}, bf16[2,2,2,64,256]{4,3,2,0,1:T(8,128)(2,1)S(1)}, u32[]{:S(2)}, u32[]{:S(2)}) collective-permute-start(bf16[2,2,2,64,256]{4,3,2,0,1:T(8,128)(2,1)S(1)} %bitcast.272), channel_id=1, source_target_pairs={{0,1},{1,0},{2,3},{3,2},{4,5},{5,4},{6,7},{7,6},{8,9},{9,8},{10,11... | collective-permute-start | bytes 786440 | tf_op jit(solution)/shard_map/ppermute | solution.py:29
  27.7 1.7 %collective-permute-start = (bf16[2,2,2,64,256]{4,3,2,1,0:T(8,128)(2,1)S(1)}, bf16[2,2,2,64,256]{4,3,2,1,0:T(8,128)(2,1)S(1)}, u32[]{:S(2)}, u32[]{:S(2)}) collective-permute-start(bf16[2,2,2,64,256]{4,3,2,1,0:T(8,128)(2,1)S(1)} %dynamic-slice_bitcast_fusion.5), channel_id=1, source_target_pairs={{0,1},{1,0},{2,3},{3,2},{4,5},{5,4},{6,7},{7,6},{8,9},{9,8},{10,11... | collective-permute-start | bytes 786440 | tf_op jit(solution)/shard_map/ppermute | solution.py:29
  28.5 37.3 %copy-start.1 = (pred[16,96,128]{2,1,0:T(32,128)(4,1)}, pred[16,96,128]{2,1,0:T(32,128)(4,1)S(1)}, u32[]{:S(2)}) copy-start(pred[16,96,128]{2,1,0:T(32,128)(4,1)S(1)} %iota_compare_fusion) | copy-start | bytes 589828
  29.0 5.6 %collective-permute-start.5 = (bf16[2,2,64,256]{3,2,1,0:T(8,128)(2,1)S(1)}, bf16[2,2,64,256]{3,2,1,0:T(8,128)(2,1)S(1)}, u32[]{:S(2)}, u32[]{:S(2)}) collective-permute-start(bf16[2,2,64,256]{3,2,1,0:T(8,128)(2,1)S(1)} %dynamic-slice_bitcast_fusion.12), channel_id=1, source_target_pairs={{0,4},{1,5},{2,6},{3,7},{4,0},{5,1},{6,2},{7,3},{8,12},{9,13},{10,... | collective-permute-start | bytes 393224 | tf_op jit(solution)/shard_map/ppermute | solution.py:29
  29.5 5.8 %collective-permute-start.1 = (bf16[2,2,64,256]{3,2,1,0:T(8,128)(2,1)S(1)}, bf16[2,2,64,256]{3,2,1,0:T(8,128)(2,1)S(1)}, u32[]{:S(2)}, u32[]{:S(2)}) collective-permute-start(bf16[2,2,64,256]{3,2,1,0:T(8,128)(2,1)S(1)} %dynamic-slice_bitcast_fusion.13), channel_id=1, source_target_pairs={{0,2},{1,3},{2,0},{3,1},{4,6},{5,7},{6,4},{7,5},{8,10},{9,11},{10,... | collective-permute-start | bytes 393224 | tf_op jit(solution)/shard_map/ppermute | solution.py:29
  34.7 5.8 %collective-permute-start.6 = (bf16[2,64,256]{2,1,0:T(8,128)(2,1)S(1)}, bf16[2,64,256]{2,1,0:T(8,128)(2,1)S(1)}, u32[]{:S(2)}, u32[]{:S(2)}) collective-permute-start(bf16[2,64,256]{2,1,0:T(8,128)(2,1)S(1)} %dynamic-slice_bitcast_fusion.20), channel_id=1, source_target_pairs={{0,8},{1,9},{2,10},{3,11},{4,12},{5,13},{6,14},{7,15},{8,0},{9,1},... | collective-permute-start | bytes 196616 | tf_op jit(solution)/shard_map/ppermute | solution.py:29
  35.4 5.2 %collective-permute-start.2 = (bf16[2,64,256]{2,1,0:T(8,128)(2,1)S(1)}, bf16[2,64,256]{2,1,0:T(8,128)(2,1)S(1)}, u32[]{:S(2)}, u32[]{:S(2)}) collective-permute-start(bf16[2,64,256]{2,1,0:T(8,128)(2,1)S(1)} %dynamic-slice_bitcast_fusion.21), channel_id=1, source_target_pairs={{0,4},{1,5},{2,6},{3,7},{4,0},{5,1},{6,2},{7,3},{8,12},{9,13},{10,... | collective-permute-start | bytes 196616 | tf_op jit(solution)/shard_map/ppermute | solution.py:29
  40.5 4.0 %collective-permute-start.7 = (bf16[64,256]{1,0:T(8,128)(2,1)S(1)}, bf16[64,256]{1,0:T(8,128)(2,1)S(1)}, u32[]{:S(2)}, u32[]{:S(2)}) collective-permute-start(bf16[64,256]{1,0:T(8,128)(2,1)S(1)} %dynamic-slice_bitcast_fusion.24), channel_id=1, source_target_pairs={{0,2},{1,3},{2,0},{3,1},{4,6},{5,7},{6,4},{7,5},{8,10},{9,11},{10,... | collective-permute-start | bytes 98312 | tf_op jit(solution)/shard_map/ppermute | solution.py:29
  40.6 5.1 %collective-permute-start.3 = (bf16[64,256]{1,0:T(8,128)(2,1)S(1)}, bf16[64,256]{1,0:T(8,128)(2,1)S(1)}, u32[]{:S(2)}, u32[]{:S(2)}) collective-permute-start(bf16[64,256]{1,0:T(8,128)(2,1)S(1)} %dynamic-slice_bitcast_fusion.25), channel_id=1, source_target_pairs={{0,8},{1,9},{2,10},{3,11},{4,12},{5,13},{6,14},{7,15},{8,0},{9,1},... | collective-permute-start | bytes 98312 | tf_op jit(solution)/shard_map/ppermute | solution.py:29
  46.3 13.7 %slice-start = ((s8[6291456]{0:T(1024)(128)(4,1)}), s8[4194304]{0:T(1024)(128)(4,1)S(1)}, s32[]{:S(2)}) async-start(s8[6291456]{0:T(1024)(128)(4,1)} %bitcast.253), calls=%async_computation.2 | async-start | bytes 8388608
  50.3 9.7 %slice-start.1 = ((s8[6291456]{0:T(1024)(128)(4,1)}), s8[2097152]{0:T(1024)(128)(4,1)S(1)}, s32[]{:S(2)}) async-start(s8[6291456]{0:T(1024)(128)(4,1)} %bitcast.253), calls=%async_computation.3 | async-start | bytes 4194304
  50.5 1.2 collective-permute-start.16
  51.7 3.5 %collective-permute-start.17 = (f32[128]{0:T(128)S(1)}, f32[128]{0:T(128)S(1)}, u32[]{:S(2)}, u32[]{:S(2)}) collective-permute-start(f32[128]{0:T(128)S(1)} %add.297), channel_id=1, source_target_pairs={{0,2},{1,3},{2,0},{3,1},{4,6},{5,7},{6,4},{7,5},{8,10},{9,11},{10,... | collective-permute-start | bytes 1544 | tf_op jit(solution)/shard_map/ppermute | solution.py:41
  54.3 11.6 %collective-permute-start.12 = (bf16[2,2,2,48,768]{4,3,2,1,0:T(8,128)(2,1)S(1)}, bf16[2,2,2,48,768]{4,3,2,1,0:T(8,128)(2,1)S(1)}, u32[]{:S(2)}, u32[]{:S(2)}) collective-permute-start(bf16[2,2,2,48,768]{4,3,2,1,0:T(8,128)(2,1)S(1)} %dynamic-slice_bitcast_fusion), channel_id=1, source_target_pairs={{0,1},{1,0},{2,3},{3,2},{4,5},{5,4},{6,7},{7,6},{8,9},{9,8},{10,11... | collective-permute-start | bytes 1769480 | tf_op jit(solution)/shard_map/ppermute | solution.py:29
  55.2 3.5 %collective-permute-start.18 = (f32[128]{0:T(128)S(1)}, f32[128]{0:T(128)S(1)}, u32[]{:S(2)}, u32[]{:S(2)}) collective-permute-start(f32[128]{0:T(128)S(1)} %add.298), channel_id=1, source_target_pairs={{0,4},{1,5},{2,6},{3,7},{4,0},{5,1},{6,2},{7,3},{8,12},{9,13},{10,... | collective-permute-start | bytes 1544 | tf_op jit(solution)/shard_map/ppermute | solution.py:41
  55.6 13.2 %collective-permute-start.8 = (bf16[2,2,2,48,768]{4,3,0,1,2:T(8,128)(2,1)S(1)}, bf16[2,2,2,48,768]{4,3,0,1,2:T(8,128)(2,1)S(1)}, u32[]{:S(2)}, u32[]{:S(2)}) collective-permute-start(bf16[2,2,2,48,768]{4,3,0,1,2:T(8,128)(2,1)S(1)} %bitcast.270), channel_id=1, source_target_pairs={{0,1},{1,0},{2,3},{3,2},{4,5},{5,4},{6,7},{7,6},{8,9},{9,8},{10,11... | collective-permute-start | bytes 1769480 | tf_op jit(solution)/shard_map/ppermute | solution.py:29
  58.8 4.4 %collective-permute-start.19 = (f32[128]{0:T(128)S(1)}, f32[128]{0:T(128)S(1)}, u32[]{:S(2)}, u32[]{:S(2)}) collective-permute-start(f32[128]{0:T(128)S(1)} %add.299), channel_id=1, source_target_pairs={{0,8},{1,9},{2,10},{3,11},{4,12},{5,13},{6,14},{7,15},{8,0},{9,1},... | collective-permute-start | bytes 1544 | tf_op jit(solution)/shard_map/ppermute | solution.py:41
  64.3 9.8 %collective-permute-start.24 = (bf16[2,2,2,48,768]{4,3,2,0,1:T(8,128)(2,1)}, bf16[2,2,2,48,768]{4,3,2,0,1:T(8,128)(2,1)S(1)}, u32[]{:S(2)}, u32[]{:S(2)}) collective-permute-start(bf16[2,2,2,48,768]{4,3,2,0,1:T(8,128)(2,1)} %bitcast.245), channel_id=1, source_target_pairs={{0,1},{1,0},{2,3},{3,2},{4,5},{5,4},{6,7},{7,6},{8,9},{9,8},{10,11... | collective-permute-start | bytes 1769480 | tf_op jit(solution)/shard_map/ppermute | solution.py:29
  65.3 10.8 %collective-permute-start.20 = (bf16[2,2,2,48,768]{4,3,0,1,2:T(8,128)(2,1)}, bf16[2,2,2,48,768]{4,3,0,1,2:T(8,128)(2,1)S(1)}, u32[]{:S(2)}, u32[]{:S(2)}) collective-permute-start(bf16[2,2,2,48,768]{4,3,0,1,2:T(8,128)(2,1)} %bitcast.246), channel_id=1, source_target_pairs={{0,1},{1,0},{2,3},{3,2},{4,5},{5,4},{6,7},{7,6},{8,9},{9,8},{10,11... | collective-permute-start | bytes 1769480 | tf_op jit(solution)/shard_map/ppermute | solution.py:29
  66.8 11.0 %collective-permute-start.13 = (bf16[2,2,48,768]{3,2,1,0:T(8,128)(2,1)}, bf16[2,2,48,768]{3,2,1,0:T(8,128)(2,1)}, u32[]{:S(2)}, u32[]{:S(2)}) collective-permute-start(bf16[2,2,48,768]{3,2,1,0:T(8,128)(2,1)} %dynamic-slice_bitcast_fusion.3), channel_id=1, source_target_pairs={{0,2},{1,3},{2,0},{3,1},{4,6},{5,7},{6,4},{7,5},{8,10},{9,11},{10,... | collective-permute-start | bytes 884744 | tf_op jit(solution)/shard_map/ppermute | solution.py:29
  69.7 14.1 %collective-permute-start.9 = (bf16[2,2,48,768]{3,2,0,1:T(8,128)(2,1)}, bf16[2,2,48,768]{3,2,0,1:T(8,128)(2,1)}, u32[]{:S(2)}, u32[]{:S(2)}) collective-permute-start(bf16[2,2,48,768]{3,2,0,1:T(8,128)(2,1)} %dynamic-slice_bitcast_fusion.4), channel_id=1, source_target_pairs={{0,2},{1,3},{2,0},{3,1},{4,6},{5,7},{6,4},{7,5},{8,10},{9,11},{10,... | collective-permute-start | bytes 884744 | tf_op jit(solution)/shard_map/ppermute | solution.py:29
  69.8 35.5 %all-to-all-start.1 = ((bf16[16,8,256]{2,1,0:T(8,128)(2,1)}), bf16[16,8,256]{2,1,0:T(8,128)(2,1)}, u32[]{:S(2)}, u32[]{:S(2)}) async-start(bf16[16,8,256]{2,1,0:T(8,128)(2,1)} %bitcast.275), calls=%async_computation.1 | async-start | bytes 131072 | tf_op jit(solution)/shard_map/all_to_all | solution.py:189
  74.3 10.9 %collective-permute-start.25 = (bf16[2,2,48,768]{3,2,1,0:T(8,128)(2,1)S(1)}, bf16[2,2,48,768]{3,2,1,0:T(8,128)(2,1)S(1)}, u32[]{:S(2)}, u32[]{:S(2)}) collective-permute-start(bf16[2,2,48,768]{3,2,1,0:T(8,128)(2,1)S(1)} %dynamic-slice_bitcast_fusion.1), channel_id=1, source_target_pairs={{0,4},{1,5},{2,6},{3,7},{4,0},{5,1},{6,2},{7,3},{8,12},{9,13},{10,... | collective-permute-start | bytes 884744 | tf_op jit(solution)/shard_map/ppermute | solution.py:29
  76.3 13.3 %collective-permute-start.21 = (bf16[2,2,48,768]{3,2,0,1:T(8,128)(2,1)S(1)}, bf16[2,2,48,768]{3,2,0,1:T(8,128)(2,1)S(1)}, u32[]{:S(2)}, u32[]{:S(2)}) collective-permute-start(bf16[2,2,48,768]{3,2,0,1:T(8,128)(2,1)S(1)} %dynamic-slice_bitcast_fusion.2), channel_id=1, source_target_pairs={{0,2},{1,3},{2,0},{3,1},{4,6},{5,7},{6,4},{7,5},{8,10},{9,11},{10,... | collective-permute-start | bytes 884744 | tf_op jit(solution)/shard_map/ppermute | solution.py:29
  78.9 11.1 %collective-permute-start.14 = (bf16[2,48,768]{2,1,0:T(8,128)(2,1)S(1)}, bf16[2,48,768]{2,1,0:T(8,128)(2,1)S(1)}, u32[]{:S(2)}, u32[]{:S(2)}) collective-permute-start(bf16[2,48,768]{2,1,0:T(8,128)(2,1)S(1)} %dynamic-slice_bitcast_fusion.8), channel_id=1, source_target_pairs={{0,4},{1,5},{2,6},{3,7},{4,0},{5,1},{6,2},{7,3},{8,12},{9,13},{10,... | collective-permute-start | bytes 442376 | tf_op jit(solution)/shard_map/ppermute | solution.py:29
  84.9 9.7 %collective-permute-start.10 = (bf16[2,48,768]{2,1,0:T(8,128)(2,1)S(1)}, bf16[2,48,768]{2,1,0:T(8,128)(2,1)S(1)}, u32[]{:S(2)}, u32[]{:S(2)}) collective-permute-start(bf16[2,48,768]{2,1,0:T(8,128)(2,1)S(1)} %dynamic-slice_bitcast_fusion.9), channel_id=1, source_target_pairs={{0,4},{1,5},{2,6},{3,7},{4,0},{5,1},{6,2},{7,3},{8,12},{9,13},{10,... | collective-permute-start | bytes 442376 | tf_op jit(solution)/shard_map/ppermute | solution.py:29
  85.3 9.9 %collective-permute-start.26 = (bf16[2,48,768]{2,1,0:T(8,128)(2,1)S(1)}, bf16[2,48,768]{2,1,0:T(8,128)(2,1)S(1)}, u32[]{:S(2)}, u32[]{:S(2)}) collective-permute-start(bf16[2,48,768]{2,1,0:T(8,128)(2,1)S(1)} %dynamic-slice_bitcast_fusion.6), channel_id=1, source_target_pairs={{0,8},{1,9},{2,10},{3,11},{4,12},{5,13},{6,14},{7,15},{8,0},{9,1},... | collective-permute-start | bytes 442376 | tf_op jit(solution)/shard_map/ppermute | solution.py:29
  89.7 10.0 %collective-permute-start.22 = (bf16[2,48,768]{2,1,0:T(8,128)(2,1)S(1)}, bf16[2,48,768]{2,1,0:T(8,128)(2,1)S(1)}, u32[]{:S(2)}, u32[]{:S(2)}) collective-permute-start(bf16[2,48,768]{2,1,0:T(8,128)(2,1)S(1)} %dynamic-slice_bitcast_fusion.7), channel_id=1, source_target_pairs={{0,4},{1,5},{2,6},{3,7},{4,0},{5,1},{6,2},{7,3},{8,12},{9,13},{10,... | collective-permute-start | bytes 442376 | tf_op jit(solution)/shard_map/ppermute | solution.py:29
  90.1 10.2 %collective-permute-start.15 = (bf16[48,768]{1,0:T(8,128)(2,1)S(1)}, bf16[48,768]{1,0:T(8,128)(2,1)S(1)}, u32[]{:S(2)}, u32[]{:S(2)}) collective-permute-start(bf16[48,768]{1,0:T(8,128)(2,1)S(1)} %dynamic-slice_bitcast_fusion.16), channel_id=1, source_target_pairs={{0,8},{1,9},{2,10},{3,11},{4,12},{5,13},{6,14},{7,15},{8,0},{9,1},... | collective-permute-start | bytes 221192 | tf_op jit(solution)/shard_map/ppermute | solution.py:29
  94.7 9.4 %collective-permute-start.11 = (bf16[48,768]{1,0:T(8,128)(2,1)S(1)}, bf16[48,768]{1,0:T(8,128)(2,1)S(1)}, u32[]{:S(2)}, u32[]{:S(2)}) collective-permute-start(bf16[48,768]{1,0:T(8,128)(2,1)S(1)} %dynamic-slice_bitcast_fusion.17), channel_id=1, source_target_pairs={{0,8},{1,9},{2,10},{3,11},{4,12},{5,13},{6,14},{7,15},{8,0},{9,1},... | collective-permute-start | bytes 221192 | tf_op jit(solution)/shard_map/ppermute | solution.py:29
  95.3 8.8 %collective-permute-start.27 = (bf16[48,768]{1,0:T(8,128)(2,1)S(1)}, bf16[48,768]{1,0:T(8,128)(2,1)S(1)}, u32[]{:S(2)}, u32[]{:S(2)}) collective-permute-start(bf16[48,768]{1,0:T(8,128)(2,1)S(1)} %dynamic-slice_bitcast_fusion.14), channel_id=1, source_target_pairs={{0,2},{1,3},{2,0},{3,1},{4,6},{5,7},{6,4},{7,5},{8,10},{9,11},{10,... | collective-permute-start | bytes 221192 | tf_op jit(solution)/shard_map/ppermute | solution.py:29
  99.8 5.4 %collective-permute-start.23 = (bf16[48,768]{1,0:T(8,128)(2,1)S(1)}, bf16[48,768]{1,0:T(8,128)(2,1)S(1)}, u32[]{:S(2)}, u32[]{:S(2)}) collective-permute-start(bf16[48,768]{1,0:T(8,128)(2,1)S(1)} %dynamic-slice_bitcast_fusion.15), channel_id=1, source_target_pairs={{0,8},{1,9},{2,10},{3,11},{4,12},{5,13},{6,14},{7,15},{8,0},{9,1},... | collective-permute-start | bytes 221192 | tf_op jit(solution)/shard_map/ppermute | solution.py:29
  109.5 2.2 %collective-permute-start.32 = (bf16[2,2,2,8,2048]{4,3,2,0,1:T(8,128)(2,1)S(1)}, bf16[2,2,2,8,2048]{4,3,2,0,1:T(8,128)(2,1)S(1)}, u32[]{:S(2)}, u32[]{:S(2)}) collective-permute-start(bf16[2,2,2,8,2048]{4,3,2,0,1:T(8,128)(2,1)S(1)} %bitcast.274), channel_id=1, source_target_pairs={{0,1},{1,0},{2,3},{3,2},{4,5},{5,4},{6,7},{7,6},{8,9},{9,8},{10,11... | collective-permute-start | bytes 786440 | tf_op jit(solution)/shard_map/ppermute | solution.py:29
  111.1 2.1 %collective-permute-start.28 = (bf16[2,2,2,8,2048]{4,3,0,1,2:T(8,128)(2,1)S(1)}, bf16[2,2,2,8,2048]{4,3,0,1,2:T(8,128)(2,1)S(1)}, u32[]{:S(2)}, u32[]{:S(2)}) collective-permute-start(bf16[2,2,2,8,2048]{4,3,0,1,2:T(8,128)(2,1)S(1)} %bitcast.273), channel_id=1, source_target_pairs={{0,1},{1,0},{2,3},{3,2},{4,5},{5,4},{6,7},{7,6},{8,9},{9,8},{10,11... | collective-permute-start | bytes 786440 | tf_op jit(solution)/shard_map/ppermute | solution.py:29
  111.8 5.5 %collective-permute-start.33 = (bf16[2,2,8,2048]{3,2,1,0:T(8,128)(2,1)S(1)}, bf16[2,2,8,2048]{3,2,1,0:T(8,128)(2,1)S(1)}, u32[]{:S(2)}, u32[]{:S(2)}) collective-permute-start(bf16[2,2,8,2048]{3,2,1,0:T(8,128)(2,1)S(1)} %dynamic-slice_bitcast_fusion.10), channel_id=1, source_target_pairs={{0,4},{1,5},{2,6},{3,7},{4,0},{5,1},{6,2},{7,3},{8,12},{9,13},{10,... | collective-permute-start | bytes 393224 | tf_op jit(solution)/shard_map/ppermute | solution.py:29
  113.4 6.1 %collective-permute-start.29 = (bf16[2,2,8,2048]{3,2,0,1:T(8,128)(2,1)S(1)}, bf16[2,2,8,2048]{3,2,0,1:T(8,128)(2,1)S(1)}, u32[]{:S(2)}, u32[]{:S(2)}) collective-permute-start(bf16[2,2,8,2048]{3,2,0,1:T(8,128)(2,1)S(1)} %dynamic-slice_bitcast_fusion.11), channel_id=1, source_target_pairs={{0,2},{1,3},{2,0},{3,1},{4,6},{5,7},{6,4},{7,5},{8,10},{9,11},{10,... | collective-permute-start | bytes 393224 | tf_op jit(solution)/shard_map/ppermute | solution.py:29
  117.3 5.3 %collective-permute-start.34 = (bf16[2,8,2048]{2,1,0:T(8,128)(2,1)S(1)}, bf16[2,8,2048]{2,1,0:T(8,128)(2,1)S(1)}, u32[]{:S(2)}, u32[]{:S(2)}) collective-permute-start(bf16[2,8,2048]{2,1,0:T(8,128)(2,1)S(1)} %dynamic-slice_bitcast_fusion.18), channel_id=1, source_target_pairs={{0,8},{1,9},{2,10},{3,11},{4,12},{5,13},{6,14},{7,15},{8,0},{9,1},... | collective-permute-start | bytes 196616 | tf_op jit(solution)/shard_map/ppermute | solution.py:29
  119.5 6.2 %collective-permute-start.30 = (bf16[2,8,2048]{2,1,0:T(8,128)(2,1)S(1)}, bf16[2,8,2048]{2,1,0:T(8,128)(2,1)S(1)}, u32[]{:S(2)}, u32[]{:S(2)}) collective-permute-start(bf16[2,8,2048]{2,1,0:T(8,128)(2,1)S(1)} %dynamic-slice_bitcast_fusion.19), channel_id=1, source_target_pairs={{0,4},{1,5},{2,6},{3,7},{4,0},{5,1},{6,2},{7,3},{8,12},{9,13},{10,... | collective-permute-start | bytes 196616 | tf_op jit(solution)/shard_map/ppermute | solution.py:29
  122.7 4.9 %collective-permute-start.35 = (bf16[8,2048]{1,0:T(8,128)(2,1)S(1)}, bf16[8,2048]{1,0:T(8,128)(2,1)S(1)}, u32[]{:S(2)}, u32[]{:S(2)}) collective-permute-start(bf16[8,2048]{1,0:T(8,128)(2,1)S(1)} %dynamic-slice_bitcast_fusion.22), channel_id=1, source_target_pairs={{0,2},{1,3},{2,0},{3,1},{4,6},{5,7},{6,4},{7,5},{8,10},{9,11},{10,... | collective-permute-start | bytes 98312 | tf_op jit(solution)/shard_map/ppermute | solution.py:29
  125.7 5.0 %collective-permute-start.31 = (bf16[8,2048]{1,0:T(8,128)(2,1)S(1)}, bf16[8,2048]{1,0:T(8,128)(2,1)S(1)}, u32[]{:S(2)}, u32[]{:S(2)}) collective-permute-start(bf16[8,2048]{1,0:T(8,128)(2,1)S(1)} %dynamic-slice_bitcast_fusion.23), channel_id=1, source_target_pairs={{0,8},{1,9},{2,10},{3,11},{4,12},{5,13},{6,14},{7,15},{8,0},{9,1},... | collective-permute-start | bytes 98312 | tf_op jit(solution)/shard_map/ppermute | solution.py:29
